TPU v7x, 128 devices: a whole 4x4x4 slice. The times are simulated.
128 devices in a mesh: frow: 8 (over y, core), fcol: 16 (over x, z).
Axes of the slice: x: 4, y: 4, z: 4, core: 2. Of those that a mesh axis runs over, the one named last changes fastest.
Arguments:
- front_matrix: bfloat16 [28672, 28672], P('frow', 'fcol'), may hold values from -0.046875 to 0.046875
- test_matrix: bfloat16 [28672, 512], P('fcol'), may hold values from -6 to 6
- child_samples: bfloat16 [131072, 512], P(('frow', 'fcol')), may hold values from -6 to 6
- child_group: int32 [1024, 1], P(('frow', 'fcol')), may hold values from 0 to 7; in each aligned block of 8 rows (0 to 7, 8 to 15, ...) at most 4 rows name the same one
- child_block: int32 [1024], P(('frow', 'fcol')), may hold values from 0 to 27
- inv_leaf: bfloat16 [65536, 96], P(('frow', 'fcol')), may hold values from -0.25 to 0.25
- inv_parent: bfloat16 [32768, 64], P(('frow', 'fcol')), may hold values from -0.25 to 0.25
- pivot_leaf: int32 [128, 96], P(('frow', 'fcol')), may hold values from 0 to 223, as said below
- pivot_parent: int32 [128, 32], P(('frow', 'fcol')), may hold values from 0 to 191, as said below
Outputs:
- samples: bfloat16 [28672, 512], P(('frow', 'fcol'))
- interp_leaf: float32 [28672, 96], P(('frow', 'fcol'))
- interp_parent: float32 [12288, 64], P(('frow', 'fcol'))
- skeleton_parent: bfloat16 [4096, 512], P(('frow', 'fcol'))
Inputs may be any that keep to these rules, and one draw needn't show every extreme that they name: `pivot_leaf`: within each leaf's row, 96 distinct values. `pivot_parent`: the two rows of leaves 2p and 2p+1 together hold 64 distinct values. `child_group`: among the 8 rows of one device, no group is named more than 4 times.
All inputs are finite; a program needn't handle non-finite values.
Results may differ from a plain program's by a relative error of at most 0.003.
Values may be sent and summed in bfloat16 or wider, within the bound.
No kernel may reach another device: no remote copies, remote signals or barrier semaphores. Data moves between devices by JAX's collectives and lax.ppermute only.
A program may use at most 128 MiB of HBM per device.

v0:
```python
import jax
import jax.numpy as jnp
from jax import lax
from jax.sharding import PartitionSpec as P

BLK = 128
CBD = 8


def from_partner(x, axis, apart):
    return lax.ppermute(x, axis, [(i, i ^ 1 << apart) for i in range(lax.axis_size(axis))])


def on_device(
    front_matrix,
    test_matrix,
    child_samples,
    child_group,
    child_block,
    inv_leaf,
    inv_parent,
    pivot_leaf,
    pivot_parent,
):
    group_rows = front_matrix.shape[0]
    sample_cols = test_matrix.shape[1]
    groups = lax.axis_size("frow")
    capacity = CBD // 2
    children = child_block.shape[0]
    slot_count = groups * capacity
    dest_group = child_group[:, 0]
    group_hits = (dest_group[:, None] == jnp.arange(groups, dtype=jnp.int32)[None, :]).astype(
        jnp.int32
    )
    earlier = jnp.cumsum(group_hits, axis=0) - group_hits
    position = jnp.sum(earlier * group_hits, axis=1)
    slot_index = dest_group * capacity + position
    assign = jnp.arange(slot_count, dtype=jnp.int32)[:, None] == slot_index[None, :]
    payload = jnp.dot(
        assign.astype(jnp.bfloat16),
        child_samples.reshape(children, BLK * sample_cols),
        preferred_element_type=jnp.float32,
    ).astype(jnp.bfloat16)
    slot_ids = jnp.sum(assign.astype(jnp.int32) * (child_block + 1)[None, :], axis=1)
    arrived = lax.all_to_all(payload, "frow", split_axis=0, concat_axis=0, tiled=True)
    arrived_ids = lax.all_to_all(slot_ids, "frow", split_axis=0, concat_axis=0, tiled=True)
    group_blocks = group_rows // BLK
    placer = (
        arrived_ids[None, :] - 1 == jnp.arange(group_blocks, dtype=jnp.int32)[:, None]
    ).astype(jnp.bfloat16)
    child_part = jnp.dot(placer, arrived, preferred_element_type=jnp.float32).reshape(
        group_rows, sample_cols
    )
    leaf_count = group_rows // lax.axis_size("fcol")
    partial_value = (
        jnp.dot(front_matrix, test_matrix, preferred_element_type=jnp.float32) + child_part
    )
    summed = lax.psum(partial_value, "fcol")
    leaf_rows = lax.dynamic_slice_in_dim(summed, lax.axis_index("fcol") * leaf_count, leaf_count, 0)
    samples = leaf_rows.astype(jnp.bfloat16)
    interp_leaf = jnp.dot(samples, inv_leaf, preferred_element_type=jnp.float32)
    skeleton = samples[pivot_leaf[0]]
    other_skeleton, other_inverse = from_partner((skeleton, inv_parent), "fcol", 0)
    is_even = lax.axis_index("fcol") % 2 == 0
    upper_half = jnp.where(is_even, skeleton, other_skeleton)
    lower_half = jnp.where(is_even, other_skeleton, skeleton)
    stacked = jnp.concatenate([upper_half, lower_half], axis=0)
    inverse_top = jnp.where(is_even, inv_parent, other_inverse)
    inverse_bottom = jnp.where(is_even, other_inverse, inv_parent)
    inverse_full = jnp.concatenate([inverse_top, inverse_bottom], axis=0)
    interp_parent = jnp.dot(skeleton, inverse_full, preferred_element_type=jnp.float32)
    skeleton_parent = stacked[pivot_parent[0]]
    return (samples, interp_leaf, interp_parent, skeleton_parent)


def solution(mesh):
    placed = (
        P("frow", "fcol"),
        P("fcol", None),
        P(("frow", "fcol"), None),
        P(("frow", "fcol"), None),
        P(("frow", "fcol")),
        P(("frow", "fcol"), None),
        P(("frow", "fcol"), None),
        P(("frow", "fcol"), None),
        P(("frow", "fcol"), None),
    )
    return jax.shard_map(
        on_device,
        mesh=mesh,
        in_specs=placed,
        out_specs=(
            P(("frow", "fcol"), None),
            P(("frow", "fcol"), None),
            P(("frow", "fcol"), None),
            P(("frow", "fcol"), None),
        ),
        check_vma=False,
    )
```

profile of v0, /device:TPU:0, one launch (start us, length us, event | category | flops | bytes accessed | tf_op | source)
XLA Modules:
  0.0 284.3 jit_solution(11188651860606131753)
XLA Ops:
  0.6 0.0 copy-start
  0.6 0.9 fusion.6
  1.5 0.8 select_reduce_fusion.1
  2.4 0.7 multiply_add_fusion
  3.0 0.1 select_reduce_fusion
  3.1 0.7 all_to_all.14
  3.8 4.6 %all-to-all-start = ((s32[8,4,1]{1,2,0:T(1,128)}), s32[8,4,1]{1,2,0:T(1,128)S(1)}, u32[]{:S(2)}, u32[]{:S(2)}) async-start(s32[8,4,1]{1,2,0:T(1,128)} %bitcast.1), calls=%async_computation | async-start | bytes 8192 | tf_op jit(solution)/shard_map/all_to_all | solution.py:46
  8.4 1.7 reshape.91
  10.1 3.3 %convolution_convert_fusion = bf16[32,65536]{1,0:T(8,128)(2,1)} fusion(bf16[8,65536]{1,0:T(8,128)(2,1)S(1)} %reshape.91, s32[8]{0:T(128)S(1)} %get-tuple-element.8), kind=kOutput, calls=%fused_computation.2 | convolution fusion | flops 35651840 | bytes 5242912 | tf_op jit(solution)/shard_map/dot_general | solution.py:39
  13.4 5.3 %all_to_all.16 = bf16[8,4,65536]{2,1,0:T(4,128)(2,1)} reshape(bf16[32,65536]{1,0:T(8,128)(2,1)} %convolution_convert_fusion) | data formatting | bytes 8388608 | tf_op jit(solution)/shard_map/all_to_all | solution.py:45
  18.7 0.0 copy-start.3
  18.7 0.0 copy-start.4
  18.7 0.0 copy-start.5
  18.7 0.0 all-to-all-done
  18.7 4.9 %all-to-all-start.1 = ((bf16[8,4,65536]{2,1,0:T(4,128)(2,1)}), bf16[8,4,65536]{2,1,0:T(4,128)(2,1)}, u32[]{:S(2)}, u32[]{:S(2)}) async-start(bf16[8,4,65536]{2,1,0:T(4,128)(2,1)} %all_to_all.16), calls=%async_computation.1 | async-start | bytes 8388608 | tf_op jit(solution)/shard_map/all_to_all | solution.py:45
  23.7 0.0 copy-done.3
  23.7 2.0 collective-permute-start
  25.7 0.0 copy-done.4
  25.7 0.0 copy-done.5
  25.7 0.1 sub.11
  25.8 1.8 collective-permute-done
  27.7 45.8 %all-to-all-done.1 = bf16[8,4,65536]{2,1,0:T(4,128)(2,1)} async-done(((bf16[8,4,65536]{2,1,0:T(4,128)(2,1)}), bf16[8,4,65536]{2,1,0:T(4,128)(2,1)}, u32[]{:S(2)}, u32[]{:S(2)}) %all-to-all-start.1) | async-done | bytes 4194336 | tf_op jit(solution)/shard_map/all_to_all | solution.py:45
  73.4 5.1 %all_to_all.18 = bf16[32,65536]{1,0:T(8,128)(2,1)} reshape(bf16[8,4,65536]{2,1,0:T(4,128)(2,1)} %all-to-all-done.1) | data formatting | bytes 8388608 | tf_op jit(solution)/shard_map/all_to_all | solution.py:45
  78.6 6.6 %fusion.4 = f32[28,65536]{1,0:T(8,128)} fusion(bf16[32,65536]{1,0:T(8,128)(2,1)} %all_to_all.18, s32[32]{0:T(128)S(1)} %sub.11), kind=kOutput, calls=%fused_computation.15 | convolution fusion | flops 117441408 | bytes 11534464 | tf_op jit(solution)/shard_map/dot_general | solution.py:51
  85.2 7.2 %reshape.92 = f32[3584,512]{1,0:T(8,128)} reshape(f32[28,65536]{1,0:T(8,128)} %fusion.4) | data formatting | bytes 14680064 | tf_op jit(solution)/shard_map/reshape | solution.py:51
  92.4 0.0 copy-done
  92.5 14.7 %convolution_add_fusion = f32[3584,512]{1,0:T(8,128)} fusion(f32[3584,512]{1,0:T(8,128)} %reshape.92, bf16[3584,1792]{1,0:T(8,128)(2,1)} %param.9, bf16[1792,512]{1,0:T(8,128)(2,1)S(1)} %copy-done), kind=kOutput, calls=%fused_computation.3 | convolution fusion | flops 6578503680 | bytes 29360128 | tf_op jit(solution)/shard_map/dot_general | solution.py:56
  107.1 0.0 copy-start.2
  107.1 168.6 %all-reduce.1 = bf16[3584,512]{1,0:T(8,128)(2,1)} all-reduce(f32[3584,512]{1,0:T(8,128)} %convolution_add_fusion), channel_id=1, replica_groups=mesh['frow'=8,'fcol'=16] {'fcol'}, use_global_device_ids=true, to_apply=%region_3.4 | all-reduce | flops 1835008 | bytes 11010048 | tf_op jit(solution)/shard_map/psum | solution.py:58
  275.8 1.0 dynamic-slice_convert_fusion
  276.7 0.0 copy-done.2
  276.7 0.0 copy-start.1
  276.7 0.8 fusion.11
  277.6 0.8 gather_fusion
  278.4 0.1 collective-permute-start.1
  278.4 0.8 fusion
  279.2 3.8 %collective-permute-done.1 = bf16[96,512]{1,0:T(8,128)(2,1)S(1)} collective-permute-done((bf16[96,512]{1,0:T(8,128)(2,1)S(1)}, bf16[96,512]{1,0:T(8,128)(2,1)S(1)}, u32[]{:S(2)}, u32[]{:S(2)}) %collective-permute-start.1) | collective-permute-done | bytes 98336 | tf_op jit(solution)/shard_map/ppermute | solution.py:11
  283.1 1.2 gather_fusion.1
  284.3 0.0 copy-done.1
  (9 shorter events, 0.1 us)
Async XLA Ops:
  0.6 91.8 %copy-start = (bf16[1792,512]{1,0:T(8,128)(2,1)S(1)}, bf16[1792,512]{1,0:T(8,128)(2,1)}, u32[]{:S(2)}) copy-start(bf16[1792,512]{1,0:T(8,128)(2,1)} %param.10) | copy-start | bytes 5505028
  3.8 14.9 %all-to-all-start = ((s32[8,4,1]{1,2,0:T(1,128)}), s32[8,4,1]{1,2,0:T(1,128)S(1)}, u32[]{:S(2)}, u32[]{:S(2)}) async-start(s32[8,4,1]{1,2,0:T(1,128)} %bitcast.1), calls=%async_computation | async-start | bytes 8192 | tf_op jit(solution)/shard_map/all_to_all | solution.py:46
  18.7 5.0 %copy-start.3 = (bf16[256,64]{0,1:T(8,128)(2,1)S(1)}, bf16[256,64]{0,1:T(8,128)(2,1)}, u32[]{:S(2)}) copy-start(bf16[256,64]{0,1:T(8,128)(2,1)} %param.15) | copy-start | bytes 98308
  18.7 7.0 %copy-start.4 = (s32[1,96]{1,0:T(1,128)S(1)}, s32[1,96]{1,0:T(1,128)}, u32[]{:S(2)}) copy-start(s32[1,96]{1,0:T(1,128)} %param.16) | copy-start | bytes 1156
  18.7 7.0 %copy-start.5 = (s32[1,32]{1,0:T(1,128)S(1)}, s32[1,32]{1,0:T(1,128)}, u32[]{:S(2)}) copy-start(s32[1,32]{1,0:T(1,128)} %param.17) | copy-start | bytes 388
  18.7 54.7 %all-to-all-start.1 = ((bf16[8,4,65536]{2,1,0:T(4,128)(2,1)}), bf16[8,4,65536]{2,1,0:T(4,128)(2,1)}, u32[]{:S(2)}, u32[]{:S(2)}) async-start(bf16[8,4,65536]{2,1,0:T(4,128)(2,1)} %all_to_all.16), calls=%async_computation.1 | async-start | bytes 8388608 | tf_op jit(solution)/shard_map/all_to_all | solution.py:45
  23.7 4.0 %collective-permute-start = (bf16[256,64]{0,1:T(8,128)(2,1)S(1)}, bf16[256,64]{0,1:T(8,128)(2,1)S(1)}, u32[]{:S(2)}, u32[]{:S(2)}) collective-permute-start(bf16[256,64]{0,1:T(8,128)(2,1)S(1)} %copy-done.3), channel_id=1, source_target_pairs={{0,1},{1,0},{2,3},{3,2},{4,5},{5,4},{6,7},{7,6},{8,9},{9,8},{10,11... | collective-permute-start | bytes 98312 | tf_op jit(solution)/shard_map/ppermute | solution.py:11
  107.1 169.6 %copy-start.2 = (bf16[512,96]{0,1:T(8,128)(2,1)S(1)}, bf16[512,96]{0,1:T(8,128)(2,1)}, u32[]{:S(2)}) copy-start(bf16[512,96]{0,1:T(8,128)(2,1)} %param.14) | copy-start | bytes 294916
  276.7 7.6 %copy-start.1 = (bf16[224,512]{1,0:T(8,128)(2,1)}, bf16[224,512]{1,0:T(8,128)(2,1)S(1)}, u32[]{:S(2)}) copy-start(bf16[224,512]{1,0:T(8,128)(2,1)S(1)} %dynamic-slice_convert_fusion) | copy-start | bytes 688132
  278.4 4.7 %collective-permute-start.1 = (bf16[96,512]{1,0:T(8,128)(2,1)S(1)}, bf16[96,512]{1,0:T(8,128)(2,1)S(1)}, u32[]{:S(2)}, u32[]{:S(2)}) collective-permute-start(bf16[96,512]{1,0:T(8,128)(2,1)S(1)} %gather_fusion), channel_id=1, source_target_pairs={{0,1},{1,0},{2,3},{3,2},{4,5},{5,4},{6,7},{7,6},{8,9},{9,8},{10,11... | collective-permute-start | bytes 294920 | tf_op jit(solution)/shard_map/ppermute | solution.py:11
where the time goes:
time: 285 us; the launch traced here: 284 us
  blocking collectives  169 us (59%)
  waiting for transfers between devices  51.4 us (18%)
  matrix products  26.2 us (9%)
  local copies, waits for them, and re-layouts  23.2 us (8%)
  starting transfers between devices  11.6 us (4%)
    psum x1, blocking collectives, on_device(): summed = lax.psum(partial_value, 'fcol')  169 us
    all_to_all x1, waiting for transfers between devices, on_device(): lax.all_to_all(payload, 'frow', split_axis=0, concat_axis=0, tiled=True)  45.8 us
    dot_general x1, matrix products, on_device(): jnp.dot(front_matrix, test_matrix, preferred_element_type=jnp.float32)  14.7 us
    all_to_all x2, local copies, waits for them, and re-layouts, on_device(): lax.all_to_all(payload, 'frow', split_axis=0, concat_axis=0, tiled=True)  10.5 us
    reshape x1, local copies, waits for them, and re-layouts, on_device(): jnp.dot(placer, arrived, preferred_element_type=jnp.float32)  7.25 us
    dot_general x1, matrix products, on_device(): jnp.dot(placer, arrived, preferred_element_type=jnp.float32)  6.63 us
  transfers between devices with their start and end apart: 4, of which 3 were waited for; matrix products, arithmetic and copies ran while one was open for 2% of the time, Pallas kernels for 0%

commit v1 on v0

v1 whole, which is shorter than its diff:
```python
import functools

import jax
import jax.numpy as jnp
from jax import lax
from jax.experimental import pallas as pl
from jax.experimental.pallas import tpu as pltpu
from jax.sharding import PartitionSpec as P

BF16 = jnp.bfloat16
F32 = jnp.float32
BLK = 128
CBD = 8
NX = 4
NZ = 4
NY = 4
UNIT = 32
COLS = 128
LOCAL = pl.BlockSpec(memory_space=pltpu.VMEM)
SCALAR = pl.BlockSpec(memory_space=pltpu.SMEM)
REMAIN = pl.BlockSpec(memory_space=pltpu.HBM)


def params(mebibytes):
    return pltpu.CompilerParams(vmem_limit_bytes=mebibytes * 1024 * 1024)


def cost(flops, moved_bytes):
    return pl.CostEstimate(flops=flops, bytes_accessed=moved_bytes, transcendentals=0)


def fetch(pairs, sems):
    copies = [pltpu.make_async_copy(src, dst, sems.at[i]) for i, (src, dst) in enumerate(pairs)]
    for copy in copies:
        copy.start()
    return copies


def front_kernel(pos, a_hbm, b_hbm, x1, x2, x3, x0, z1, z2, z3, z0, a, b, value, sems):
    half = a.shape[1]
    rows = half * UNIT
    pieces = [(b_hbm, b)]
    for i, shift in enumerate((1, 3, 2, 0)):
        pieces.append((a_hbm.at[:half, (pos[0] + shift) % NX], a.at[i]))
    for jr in range(NX):
        pieces.append((a_hbm.at[half:, jr], a.at[NX + jr]))
    copies = fetch(pieces, sems)
    copies[0].wait()

    def product(pair):
        for q in (2 * pair, 2 * pair + 1):
            copies[1 + q].wait()
        both = a[2 * pair : 2 * pair + 2].reshape(2 * rows, a.shape[-1])
        return jnp.dot(both, b[...], preferred_element_type=F32)

    for pair, outs in ((0, (x1, x3)), (1, (x2, x0))):
        value[...] = product(pair)
        for t, out in enumerate(outs):
            out[...] = value[t * rows : (t + 1) * rows].astype(out.dtype)
    for pair in (2, 3):
        value[...] = product(pair)
        for shift, out in ((1, z1), (2, z2), (3, z3), (0, z0)):
            at = pl.multiple_of((pos[1] + shift) % NZ * COLS, COLS)
            piece = value[:, pl.ds(at, COLS)].astype(out.dtype)
            out[2 * (pair - 2) : 2 * (pair - 1)] = piece.reshape(2, rows, COLS)


def front_products(pos, front, test):
    blocks, depth, cols = front.shape[0] // BLK, front.shape[1], test.shape[1]
    half = blocks // 2
    rows = half * UNIT
    shapes = [((rows, cols), t) for t in (BF16, BF16, BF16, F32)]
    shapes += [((NX, rows, COLS), t) for t in (BF16, BF16, BF16, F32)]
    return pl.pallas_call(
        front_kernel,
        out_shape=[jax.ShapeDtypeStruct(*s) for s in shapes],
        in_specs=[SCALAR, REMAIN, REMAIN],
        out_specs=[LOCAL] * 8,
        scratch_shapes=[
            pltpu.VMEM((2 * NX, half, UNIT, depth), BF16),
            pltpu.VMEM(test.shape, BF16),
            pltpu.VMEM((2 * rows, cols), F32),
            pltpu.SemaphoreType.DMA((2 * NX + 1,)),
        ],
        compiler_params=params(28),
        cost_estimate=cost(
            2 * front.size * cols, 2 * (front.size + test.size) + 5 * blocks * BLK * cols
        ),
        name="front",
    )(pos, front.reshape(blocks, NX, UNIT, depth), test)


def sum_kernel(pos, own, r1, r2, r3, to1, to2, to3, keep, *, axis):
    for shift, out in ((1, to1), (2, to2), (3, to3), (0, keep)):
        if axis == 0:
            at = (pos[0] + shift) % NX
        else:
            at = (slice(None), pl.ds(pl.multiple_of((pos[1] + shift) % NZ * COLS, COLS), COLS))
        out[...] = own[at] + r1[at].astype(F32) + r2[at].astype(F32) + r3[at].astype(F32)


def partial_sum(pos, own, arrived, axis):
    piece = (own.shape[-2], COLS)
    return pl.pallas_call(
        functools.partial(sum_kernel, axis=axis),
        out_shape=[jax.ShapeDtypeStruct(piece, F32)] * 4,
        in_specs=[SCALAR] + [LOCAL] * 4,
        out_specs=[LOCAL] * 4,
        compiler_params=params(8),
        cost_estimate=cost(3 * own.size, 14 * own.size),
        name="sum_z" if axis == 0 else "sum_x",
    )(pos, own, *arrived)


def pack_kernel(child, group, block, pivots, out, facts, sems, *, blocks):
    copies = fetch(
        [
            (child.at[:, x * UNIT : (x + 1) * UNIT, z * COLS : (z + 1) * COLS], out.at[x * NZ + z, :CBD])
            for x in range(NX)
            for z in range(NZ)
        ],
        sems,
    )
    facts[...] = jnp.zeros_like(facts)
    facts[0:1, : group.shape[1]] = (group[...] * blocks + block[...]).astype(F32)
    facts[1:2, : pivots.shape[1]] = pivots[...].astype(F32)
    told = facts[...].astype(BF16)
    for i in range(out.shape[0]):
        out[i, CBD] = told
    for copy in copies:
        copy.wait()


def pack(child, group, block, pivots, blocks):
    return pl.pallas_call(
        functools.partial(pack_kernel, blocks=blocks),
        out_shape=jax.ShapeDtypeStruct((NX * NZ, CBD + 1, UNIT, COLS), BF16),
        in_specs=[REMAIN] + [LOCAL] * 3,
        out_specs=LOCAL,
        scratch_shapes=[pltpu.VMEM((UNIT, COLS), F32), pltpu.SemaphoreType.DMA((NX * NZ,))],
        compiler_params=params(4),
        cost_estimate=cost(0, 4 * child.size),
        name="pack",
    )(child.reshape(CBD, BLK, child.shape[1]), group, block, pivots)


def place_kernel(pos, mine, other, to1, to2, to3, own, pivots, total, facts, told, slots, sems):
    blocks = own.shape[0]
    sources = mine.shape[0]
    for t, ref in ((0, mine), (1, other)):
        told[t * sources : (t + 1) * sources] = ref[:, CBD].astype(F32)
    dest = told[:, 0].astype(jnp.int32)
    group = dest // blocks
    facts[...] = jnp.where(
        group % 2 == pos[4], (group // 2 + NY - pos[3]) % NY * blocks + dest % blocks, NY * blocks
    )
    copy = pltpu.make_async_copy(facts, slots, sems.at[0])
    copy.start()
    pivots[...] = told[pl.ds(pos[2] // 2 * 2, 2), 1].astype(jnp.int32)
    total[...] = jnp.zeros_like(total)
    copy.wait()
    for t, ref in ((0, mine), (1, other)):
        def body(i, _, t=t, ref=ref):
            for j in range(CBD):
                at = slots[t * sources + i, j]
                total[at] += ref[i, j].astype(F32)
            return _

        lax.fori_loop(0, sources, body, 0)
    own[...] = total[:blocks]
    for shift, ref in ((1, to1), (2, to2), (3, to3)):
        ref[...] = total[shift * blocks : (shift + 1) * blocks].astype(BF16)


def place(pos, mine, other, blocks):
    piece = (blocks, UNIT, COLS)
    sources = mine.shape[0]
    return pl.pallas_call(
        place_kernel,
        out_shape=[jax.ShapeDtypeStruct(piece, BF16)] * 3
        + [jax.ShapeDtypeStruct(piece, F32), jax.ShapeDtypeStruct((2, COLS), jnp.int32)],
        in_specs=[SCALAR] + [LOCAL] * 2,
        out_specs=[LOCAL] * 5,
        scratch_shapes=[
            pltpu.VMEM((NY * blocks + 1, UNIT, COLS), F32),
            pltpu.VMEM((2 * sources, COLS), jnp.int32),
            pltpu.VMEM((2 * sources, UNIT, COLS), F32),
            pltpu.SMEM((2 * sources, COLS), jnp.int32),
            pltpu.SemaphoreType.DMA((1,)),
        ],
        compiler_params=params(8),
        cost_estimate=cost(16 * mine.size, 8 * mine.size),
        name="place",
    )(pos, mine, other)


def finish_kernel(pos, *refs):
    fx, fz, child, out, total = refs[:4], refs[4:8], refs[8:12], refs[12], refs[13]
    half = fx[0].shape[0]
    blocks = 2 * half
    for first, part in ((0, fx), (half, fz)):
        value = part[0][...] + part[1][...] + part[2][...] + part[3][...]
        span = slice(first, first + half)
        value = value + child[0][span] + child[1][span].astype(F32)
        value = value + child[2][span].astype(F32) + child[3][span].astype(F32)
        total[span] = value.astype(BF16)
    units = blocks * NX // out.shape[0]
    for leaf in range(out.shape[0]):
        offset = (pos[0] - units * leaf) % NX
        for slot in range(2):
            unit = units * leaf + offset + NX * slot
            value = total[jnp.minimum(unit // NX, blocks - 1)]
            for dest in (leaf // 2 * 2, leaf // 2 * 2 + 1):
                out[dest, leaf % 2, slot] = value


def finish(pos, fx, fz, child, leaves):
    blocks = child[0].shape[0]
    piece = (blocks // 2, UNIT, COLS)
    return pl.pallas_call(
        finish_kernel,
        out_shape=jax.ShapeDtypeStruct((leaves, 2, 2, UNIT, COLS), BF16),
        in_specs=[SCALAR] + [LOCAL] * 12,
        out_specs=LOCAL,
        scratch_shapes=[pltpu.VMEM(child[0].shape, BF16)],
        compiler_params=params(8),
        cost_estimate=cost(8 * child[0].size, 30 * child[0].size),
        name="finish",
    )(pos, *[f.reshape(piece) for f in fx], *[f.reshape(piece) for f in fz], *child)


def across(a, b):
    return lax.dot_general(a, b, (((1,), (1,)), ((), ())), preferred_element_type=F32)


def tail_kernel(pos, arrived, inv_leaf, inv_own, inv_other, piv_leaf, piv_parent,
                samples, interp_leaf, interp_parent, skeleton_parent, rows, stacked):
    leaf = pos[2]
    units = samples.shape[0] // UNIT
    parity = leaf % 2
    for x in range(NX):
        for z in range(NZ):
            for t in range(2):
                offset = (x - units * (leaf - parity + t)) % NX
                for slot in range(2):
                    rows[t, offset + NX * slot, :, z * COLS : (z + 1) * COLS] = arrived[x * NZ + z, t, slot]
    padded = rows.shape[1] * UNIT
    count = samples.shape[0]
    rank = interp_parent.shape[1]
    leaf_rows = rows[parity].reshape(padded, rows.shape[-1])
    samples[...] = leaf_rows[:count]
    interp_leaf[...] = across(inv_leaf[...], leaf_rows)[:, :count]

    def pick(pivots, source):
        hit = lax.broadcasted_iota(jnp.int32, (source.shape[0], pivots.shape[1]), 0) == pivots
        return lax.dot_general(
            hit.astype(F32).astype(BF16), source, (((0,), (0,)), ((), ())), preferred_element_type=F32
        ).astype(BF16)

    for t in range(2):
        stacked[t] = pick(piv_leaf[t : t + 1], rows[t].reshape(padded, rows.shape[-1]))
    both = stacked[...].reshape(2 * rank, stacked.shape[-1])
    skeleton_parent[...] = pick(piv_parent[...], both)
    depth = inv_own.shape[1]
    skeleton = stacked[parity]
    even = lax.select(parity == 0, inv_own[...], inv_other[...])
    odd = lax.select(parity == 0, inv_other[...], inv_own[...])
    interp_parent[...] = across(even, skeleton[:, :depth]) + across(odd, skeleton[:, depth:])


def tail(pos, arrived, inv_leaf, inv_own, inv_other, piv_leaf, piv_parent, count):
    rank, cols = inv_leaf.shape
    padded = 2 * NX * UNIT
    args = (arrived, inv_leaf, inv_own, inv_other, piv_leaf, piv_parent)
    outs = [
        jax.ShapeDtypeStruct((count, cols), BF16),
        jax.ShapeDtypeStruct((rank, count), F32),
        jax.ShapeDtypeStruct((inv_own.shape[0], rank), F32),
        jax.ShapeDtypeStruct((piv_parent.shape[1], cols), BF16),
    ]
    return pl.pallas_call(
        tail_kernel,
        out_shape=outs,
        in_specs=[SCALAR] + [LOCAL] * len(args),
        out_specs=[LOCAL] * len(outs),
        scratch_shapes=[
            pltpu.VMEM((2, padded // UNIT, UNIT, cols), BF16),
            pltpu.VMEM((2, rank, cols), BF16),
        ],
        compiler_params=params(8),
        cost_estimate=cost(6 * padded * rank * cols, 6 * padded * cols),
        name="tail",
    )(pos, *args)


def moved(x, axis, to):
    return lax.ppermute(x, axis, [(i, to(i)) for i in range(lax.axis_size(axis))])


def along_x(shift):
    return lambda i: (i + NZ * shift) % (NX * NZ)


def along_z(shift):
    return lambda i: i // NZ * NZ + (i + shift) % NZ


def along_y(shift):
    return lambda i: (i + 2 * shift) % (2 * NY)


def on_device(front, test, child, child_group, child_block, inv_leaf, inv_parent, pivot_leaf, pivot_parent):
    row, column = lax.axis_index("frow"), lax.axis_index("fcol")
    leaves = lax.axis_size("fcol")
    blocks = front.shape[0] // BLK
    rank = pivot_leaf.shape[1]
    pos = jnp.stack([column // NZ, column % NZ, column, row // 2, row % 2]).astype(jnp.int32)

    packed = pack(child, child_group.T, child_block.reshape(1, CBD), pivot_leaf, blocks)
    mine = lax.all_to_all(packed, "fcol", 0, 0, tiled=True)

    x1, x2, x3, own_x, z1, z2, z3, own_z = front_products(pos, front, test)
    in_x = [moved(v, "fcol", along_x(s)) for s, v in ((1, x1), (3, x3), (2, x2))]
    in_z = [moved(v, "fcol", along_z(s)) for s, v in ((1, z1), (3, z3), (2, z2))]
    mine, own_x, own_z = lax.optimization_barrier((mine, own_x, own_z))

    other = moved(mine, "frow", lambda i: i ^ 1)
    inv_other = moved(inv_parent.T, "fcol", lambda i: i ^ 1)

    *out_y, own_y, piv_leaf = place(pos, mine, other, blocks)
    piv_leaf = piv_leaf[:, :rank]
    in_y = [moved(v, "frow", along_y(s)) for s, v in zip((1, 2, 3), out_y)]

    *out_x, own_x = partial_sum(pos, own_x, in_x, 1)
    in_x = [moved(v, "fcol", along_z(s)) for s, v in zip((1, 2, 3), out_x)]
    *out_z, own_z = partial_sum(pos, own_z, in_z, 0)
    in_z = [moved(v, "fcol", along_x(s)) for s, v in zip((1, 2, 3), out_z)]

    placed = finish(pos, [own_x, *in_x], [own_z, *in_z], [own_y, *in_y], leaves)
    arrived = lax.all_to_all(placed, "fcol", 0, 0, tiled=True)
    count = front.shape[0] // leaves
    samples, interp_leaf, interp_parent, skeleton_parent = tail(
        pos, arrived, inv_leaf.T, inv_parent.T, inv_other, piv_leaf, pivot_parent, count
    )
    return samples, interp_leaf.T, interp_parent.T, skeleton_parent


def solution(mesh):
    both = P(("frow", "fcol"), None)
    return jax.shard_map(
        on_device,
        mesh=mesh,
        in_specs=(P("frow", "fcol"), P("fcol", None), both, both, P(("frow", "fcol")), both, both, both, both),
        out_specs=(both,) * 4,
        check_vma=False,
    )
```

time: 285 us -> 117 us (0.41)
  blocking collectives: 169 us -> 0 us
  starting transfers between devices: 11.6 us -> 51.5 us
  matrix products: 26.2 us -> 0 us
  waiting for transfers between devices: 51.4 us -> 31.5 us
  Pallas kernels: 0 us -> 19 us
  local copies, waits for them, and re-layouts: 23.2 us -> 13.3 us
    psum x1 -> x0, blocking collectives: 169 us -> none  [on_device(): summed = lax.psum(partial_value, 'fcol')]
    all_to_all x2, waiting for transfers between devices: 45.8 us -> 5.45 us  [the longest x1 5.45 us: on_device(): arrived = lax.all_to_all(placed, 'fcol', 0, 0, tiled=True)]
    ppermute x2 -> x17, starting transfers between devices: 2.08 us -> 40 us  [moved(): lax.ppermute(x, axis, [(i, to(i)) for i in range(lax.axis_size(axis))])]
    dot_general x5 -> x0, matrix products: 26.2 us -> none  [the longest x1 14.7 us: on_device(): jnp.dot(front_matrix, test_matrix, preferred_element_type=jnp.float32)]
    ppermute x2 -> x17, waiting for transfers between devices: 5.67 us -> 26 us  [moved(): lax.ppermute(x, axis, [(i, to(i)) for i in range(lax.axis_size(axis))])]
    pallas_call x0 -> x7, Pallas kernels: none -> 19 us  [the longest x1 9.54 us: front_products(): pl.pallas_call(front_kernel, out_shape=[jax.ShapeDtypeStruct(*s) for s in...]
    unnamed x12 -> x28, local copies, waits for them, and re-layouts: 0.03 us -> 13.2 us
    all_to_all x3 -> x0, local copies, waits for them, and re-layouts: 11.1 us -> none  [the longest x2 10.5 us: on_device(): lax.all_to_all(payload, 'frow', split_axis=0, concat_axis=0, tiled=True)]
  transfers between devices with their start and end apart: 4 -> 19, of which waited for: 3 -> 6; matrix products, arithmetic and copies ran while one was open for 2% -> 0% of each run, Pallas kernels for 0% -> 12%
where the time goes in v1:
time: 117 us; the launch traced here: 116 us
  starting transfers between devices  51.5 us (44%)
  waiting for transfers between devices  31.5 us (27%)
  Pallas kernels  19 us (16%)
  local copies, waits for them, and re-layouts  13.3 us (11%)
    ppermute x17, starting transfers between devices, moved(): lax.ppermute(x, axis, [(i, to(i)) for i in range(lax.axis_size(axis))])  40 us
    ppermute x17, waiting for transfers between devices, moved(): lax.ppermute(x, axis, [(i, to(i)) for i in range(lax.axis_size(axis))])  26 us
    unnamed x28, local copies, waits for them, and re-layouts  13.2 us
    pallas_call x1, Pallas kernels, front_products(): pl.pallas_call(front_kernel, out_shape=[jax.ShapeDtypeStruct(*s) for s in...  9.54 us
    all_to_all x1, starting transfers between devices, on_device(): mine = lax.all_to_all(packed, 'fcol', 0, 0, tiled=True)  7.97 us
    all_to_all x1, waiting for transfers between devices, on_device(): arrived = lax.all_to_all(placed, 'fcol', 0, 0, tiled=True)  5.45 us
    all_to_all x1, starting transfers between devices, on_device(): arrived = lax.all_to_all(placed, 'fcol', 0, 0, tiled=True)  3.57 us
    pallas_call x1, Pallas kernels, place(): pl.pallas_call(place_kernel, out_shape=[jax.ShapeDtypeStruct(piece, BF16)...  2.97 us
  transfers between devices with their start and end apart: 19, of which 6 were waited for; matrix products, arithmetic and copies ran while one was open for 0% of the time, Pallas kernels for 12%

profile of v1, /device:TPU:0, one launch (start us, length us, event | category | flops | bytes accessed | tf_op | source)
XLA Modules:
  0.0 116.0 jit_solution(4283250316572459783)
XLA Ops:
  0.6 0.0 copy-start
  0.6 1.2 %copy-done = bf16[1024,512]{1,0:T(8,128)(2,1)S(1)} copy-done((bf16[1024,512]{1,0:T(8,128)(2,1)S(1)}, bf16[1024,512]{1,0:T(8,128)(2,1)}, u32[]{:S(2)}) %copy-start) | copy-done | bytes 1048600
  1.9 0.0 copy-start.3
  1.9 0.7 copy-done.3
  2.5 0.0 copy-start.4
  2.5 0.7 copy-done.4
  3.2 0.7 copy-done.5
  3.8 1.4 %pack.1 = bf16[16,9,32,128]{3,2,1,0:T(8,128)(2,1)} custom-call(bf16[8,128,512]{2,1,0:T(8,128)(2,1)S(1)} %bitcast.22, s32[1,8]{1,0:T(1,128)S(1)} %bitcast.35, s32[1,8]{1,0:T(1,128)S(1)} %bitcast.36, s32[1,96]{1,0:T(1,128)S(1)} %copy-done.5), custom_call_target="tpu_custom_call" | custom-call | bytes 2097152 | tf_op jit(solution)/shard_map/pack/pallas_call | solution.py:135
  5.2 8.0 %all-to-all-start = ((bf16[16,9,32,128]{3,2,1,0:T(8,128)(2,1)}), bf16[16,9,32,128]{3,2,1,0:T(8,128)(2,1)S(1)}, u32[]{:S(2)}, u32[]{:S(2)}) async-start(bf16[16,9,32,128]{3,2,1,0:T(8,128)(2,1)} %pack.1), calls=%async_computation | async-start | bytes 2359296 | tf_op jit(solution)/shard_map/all_to_all | solution.py:320
  13.3 0.1 stack.23.pos
  13.4 4.6 %copy-done.7 = bf16[3584,1792]{1,0:T(8,128)(2,1)S(1)} copy-done((bf16[3584,1792]{1,0:T(8,128)(2,1)S(1)}, bf16[3584,1792]{1,0:T(8,128)(2,1)}, u32[]{:S(2)}) %copy-start.7) | copy-done | bytes 12845080
  18.0 1.5 %copy-done.8 = bf16[1792,512]{1,0:T(8,128)(2,1)S(1)} copy-done((bf16[1792,512]{1,0:T(8,128)(2,1)S(1)}, bf16[1792,512]{1,0:T(8,128)(2,1)}, u32[]{:S(2)}) %copy-start.8) | copy-done | bytes 1835032
  19.5 9.5 %front.1 = (bf16[448,512]{1,0:T(8,128)(2,1)S(1)}, bf16[448,512]{1,0:T(8,128)(2,1)S(1)}, bf16[448,512]{1,0:T(8,128)(2,1)S(1)}, f32[448,512]{1,0:T(8,128)S(1)}, bf...) custom-call(s32[5]{0:T(128)S(1)} %stack.23.pos, ...), custom_call_target="tpu_custom_call" | custom-call | flops 6576668672 | bytes 23855104 | tf_op jit(solution)/shard_map/front/pallas_call | solution.py:74
  29.0 0.0 copy-start.9
  29.1 0.8 copy-done.9
  29.8 0.8 copy-done.10
  30.6 0.8 copy-done.11
  31.4 0.8 copy-done.12
  32.2 0.8 copy-done.13
  32.9 0.0 all-to-all-done.mine
  32.9 0.0 collective-permute-start.12
  32.9 1.9 %collective-permute-start = (bf16[448,512]{1,0:T(8,128)(2,1)}, bf16[448,512]{1,0:T(8,128)(2,1)S(1)}, u32[]{:S(2)}, u32[]{:S(2)}) collective-permute-start(bf16[448,512]{1,0:T(8,128)(2,1)} %copy-done.13), channel_id=1, source_target_pairs={{0,4},{1,5},{2,6},{3,7},{4,8},{5,9},{6,10},{7,11},{8,12},{9,13},{1... | collective-permute-start | bytes 1376264 | tf_op jit(solution)/shard_map/ppermute | solution.py:297
  34.8 1.4 %collective-permute-start.1 = (bf16[448,512]{1,0:T(8,128)(2,1)}, bf16[448,512]{1,0:T(8,128)(2,1)S(1)}, u32[]{:S(2)}, u32[]{:S(2)}) collective-permute-start(bf16[448,512]{1,0:T(8,128)(2,1)} %copy-done.12), channel_id=1, source_target_pairs={{0,12},{1,13},{2,14},{3,15},{4,0},{5,1},{6,2},{7,3},{8,4},{9,5},{1... | collective-permute-start | bytes 1376264 | tf_op jit(solution)/shard_map/ppermute | solution.py:297
  36.2 2.2 %collective-permute-start.2 = (bf16[448,512]{1,0:T(8,128)(2,1)}, bf16[448,512]{1,0:T(8,128)(2,1)S(1)}, u32[]{:S(2)}, u32[]{:S(2)}) collective-permute-start(bf16[448,512]{1,0:T(8,128)(2,1)} %copy-done.11), channel_id=1, source_target_pairs={{0,8},{1,9},{2,10},{3,11},{4,12},{5,13},{6,14},{7,15},{8,0},{9,1},... | collective-permute-start | bytes 1376264 | tf_op jit(solution)/shard_map/ppermute | solution.py:297
  38.4 1.5 %collective-permute-start.6 = (bf16[4,448,128]{2,1,0:T(8,128)(2,1)}, bf16[4,448,128]{2,1,0:T(8,128)(2,1)S(1)}, u32[]{:S(2)}, u32[]{:S(2)}) collective-permute-start(bf16[4,448,128]{2,1,0:T(8,128)(2,1)} %copy-done.10), channel_id=1, source_target_pairs={{0,1},{1,2},{2,3},{3,0},{4,5},{5,6},{6,7},{7,4},{8,9},{9,10},{10,1... | collective-permute-start | bytes 1376264 | tf_op jit(solution)/shard_map/ppermute | solution.py:297
  39.8 7.6 %collective-permute-done.r1 = bf16[448,512]{1,0:T(8,128)(2,1)S(1)} collective-permute-done((bf16[448,512]{1,0:T(8,128)(2,1)}, bf16[448,512]{1,0:T(8,128)(2,1)S(1)}, u32[]{:S(2)}, u32[]{:S(2)}) %collective-permute-start) | collective-permute-done | bytes 458784 | tf_op jit(solution)/shard_map/ppermute | solution.py:297
  47.4 3.0 %collective-permute-start.7 = (bf16[4,448,128]{2,1,0:T(8,128)(2,1)}, bf16[4,448,128]{2,1,0:T(8,128)(2,1)S(1)}, u32[]{:S(2)}, u32[]{:S(2)}) collective-permute-start(bf16[4,448,128]{2,1,0:T(8,128)(2,1)} %copy-done.9), channel_id=1, source_target_pairs={{0,3},{1,0},{2,1},{3,2},{4,7},{5,4},{6,5},{7,6},{8,11},{9,8},{10,9... | collective-permute-start | bytes 1376264 | tf_op jit(solution)/shard_map/ppermute | solution.py:297
  50.4 0.0 collective-permute-done.1.r2
  50.4 9.5 %collective-permute-start.8 = (bf16[4,448,128]{2,1,0:T(8,128)(2,1)S(1)}, bf16[4,448,128]{2,1,0:T(8,128)(2,1)S(1)}, u32[]{:S(2)}, u32[]{:S(2)}) collective-permute-start(bf16[4,448,128]{2,1,0:T(8,128)(2,1)S(1)} %get-tuple-element.45), channel_id=1, source_target_pairs={{0,2},{1,3},{2,0},{3,1},{4,6},{5,7},{6,4},{7,5},{8,10},{9,11},{10,... | collective-permute-start | bytes 1376264 | tf_op jit(solution)/shard_map/ppermute | solution.py:297
  59.9 0.0 collective-permute-done.2.r3
  59.9 0.8 sum_x.1
  60.8 0.6 collective-permute-start.3
  61.4 0.0 collective-permute-done.6.r1
  61.4 2.1 %collective-permute-start.4 = (f32[448,128]{1,0:T(8,128)S(1)}, f32[448,128]{1,0:T(8,128)S(1)}, u32[]{:S(2)}, u32[]{:S(2)}) collective-permute-start(f32[448,128]{1,0:T(8,128)S(1)} %get-tuple-element.40), channel_id=1, source_target_pairs={{0,2},{1,3},{2,0},{3,1},{4,6},{5,7},{6,4},{7,5},{8,10},{9,11},{10,... | collective-permute-start | bytes 688136 | tf_op jit(solution)/shard_map/ppermute | solution.py:297
  63.5 10.6 %collective-permute-done.7.r2 = bf16[4,448,128]{2,1,0:T(8,128)(2,1)S(1)} collective-permute-done((bf16[4,448,128]{2,1,0:T(8,128)(2,1)}, bf16[4,448,128]{2,1,0:T(8,128)(2,1)S(1)}, u32[]{:S(2)}, u32[]{:S(2)}) %collective-permute-start.7) | collective-permute-done | bytes 458784 | tf_op jit(solution)/shard_map/ppermute | solution.py:297
  74.1 3.7 %collective-permute-start.5 = (f32[448,128]{1,0:T(8,128)S(1)}, f32[448,128]{1,0:T(8,128)S(1)}, u32[]{:S(2)}, u32[]{:S(2)}) collective-permute-start(f32[448,128]{1,0:T(8,128)S(1)} %get-tuple-element.41), channel_id=1, source_target_pairs={{0,3},{1,0},{2,1},{3,2},{4,7},{5,4},{6,5},{7,6},{8,11},{9,8},{10,9... | collective-permute-start | bytes 688136 | tf_op jit(solution)/shard_map/ppermute | solution.py:297
  77.9 0.0 collective-permute-done.8.r3
  77.9 0.7 sum_z.1
  78.6 2.2 %collective-permute-start.9 = (f32[448,128]{1,0:T(8,128)S(1)}, f32[448,128]{1,0:T(8,128)S(1)}, u32[]{:S(2)}, u32[]{:S(2)}) collective-permute-start(f32[448,128]{1,0:T(8,128)S(1)} %get-tuple-element.47), channel_id=1, source_target_pairs={{0,4},{1,5},{2,6},{3,7},{4,8},{5,9},{6,10},{7,11},{8,12},{9,13},{1... | collective-permute-start | bytes 688136 | tf_op jit(solution)/shard_map/ppermute | solution.py:297
  80.8 0.0 collective-permute-done.12.other
  80.8 1.6 %collective-permute-start.10 = (f32[448,128]{1,0:T(8,128)S(1)}, f32[448,128]{1,0:T(8,128)S(1)}, u32[]{:S(2)}, u32[]{:S(2)}) collective-permute-start(f32[448,128]{1,0:T(8,128)S(1)} %get-tuple-element.48), channel_id=1, source_target_pairs={{0,8},{1,9},{2,10},{3,11},{4,12},{5,13},{6,14},{7,15},{8,0},{9,1},... | collective-permute-start | bytes 688136 | tf_op jit(solution)/shard_map/ppermute | solution.py:297
  82.4 3.0 %place.1 = (bf16[28,32,128]{2,1,0:T(8,128)(2,1)S(1)}, bf16[28,32,128]{2,1,0:T(8,128)(2,1)S(1)}, bf16[28,32,128]{2,1,0:T(8,128)(2,1)S(1)}, f32[28,32,128]{2,1,0:T(8,128)S(1)}, s32[2,128]{1,0:T(2,128)S(1)}) custom-call(s32[5]{0:T(128)S(1)} %stack.23.pos, bf16[16,9,32,128]{3,2,1,0:T(8,128)(2,1)S(1)} %all-to-all-done.mine, ...), custom_call_target="tpu_custom_call" | custom-call | flops 9437184 | bytes 4718592 | tf_op jit(solution)/shard_map/place/pallas_call | solution.py:178
  85.4 0.0 collective-permute-done.3
  85.4 2.6 %collective-permute-start.11 = (f32[448,128]{1,0:T(8,128)S(1)}, f32[448,128]{1,0:T(8,128)S(1)}, u32[]{:S(2)}, u32[]{:S(2)}) collective-permute-start(f32[448,128]{1,0:T(8,128)S(1)} %get-tuple-element.49), channel_id=1, source_target_pairs={{0,12},{1,13},{2,14},{3,15},{4,0},{5,1},{6,2},{7,3},{8,4},{9,5},{1... | collective-permute-start | bytes 688136 | tf_op jit(solution)/shard_map/ppermute | solution.py:297
  88.0 0.0 collective-permute-done.4
  88.0 1.6 %collective-permute-start.13 = (bf16[28,32,128]{2,1,0:T(8,128)(2,1)S(1)}, bf16[28,32,128]{2,1,0:T(8,128)(2,1)S(1)}, u32[]{:S(2)}, u32[]{:S(2)}) collective-permute-start(bf16[28,32,128]{2,1,0:T(8,128)(2,1)S(1)} %get-tuple-element.52), channel_id=1, source_target_pairs={{0,32},{16,48},{32,64},{48,80},{64,96},{80,112},{96,0},{112,16},{1... | collective-permute-start | bytes 688136 | tf_op jit(solution)/shard_map/ppermute | solution.py:297
  89.6 0.0 collective-permute-done.5
  89.6 2.9 %collective-permute-start.14 = (bf16[28,32,128]{2,1,0:T(8,128)(2,1)S(1)}, bf16[28,32,128]{2,1,0:T(8,128)(2,1)S(1)}, u32[]{:S(2)}, u32[]{:S(2)}) collective-permute-start(bf16[28,32,128]{2,1,0:T(8,128)(2,1)S(1)} %get-tuple-element.53), channel_id=1, source_target_pairs={{0,64},{16,80},{32,96},{48,112},{64,0},{80,16},{96,32},{112,48},{1... | collective-permute-start | bytes 688136 | tf_op jit(solution)/shard_map/ppermute | solution.py:297
  92.5 0.0 collective-permute-done.9
  92.5 1.4 %collective-permute-start.15 = (bf16[28,32,128]{2,1,0:T(8,128)(2,1)S(1)}, bf16[28,32,128]{2,1,0:T(8,128)(2,1)S(1)}, u32[]{:S(2)}, u32[]{:S(2)}) collective-permute-start(bf16[28,32,128]{2,1,0:T(8,128)(2,1)S(1)} %get-tuple-element.54), channel_id=1, source_target_pairs={{0,96},{16,112},{32,0},{48,16},{64,32},{80,48},{96,64},{112,80},{1... | collective-permute-start | bytes 688136 | tf_op jit(solution)/shard_map/ppermute | solution.py:297
  93.9 0.0 collective-permute-done.10
  93.9 0.0 collective-permute-done.11
  93.9 1.4 %collective-permute-done.13.refs_9_ = bf16[28,32,128]{2,1,0:T(8,128)(2,1)S(1)} collective-permute-done((bf16[28,32,128]{2,1,0:T(8,128)(2,1)S(1)}, bf16[28,32,128]{2,1,0:T(8,128)(2,1)S(1)}, u32[]{:S(2)}, u32[]{:S(2)}) %collective-permute-start.13) | collective-permute-done | bytes 229408 | tf_op jit(solution)/shard_map/ppermute | solution.py:297
  95.3 3.7 %collective-permute-done.14.refs_10_ = bf16[28,32,128]{2,1,0:T(8,128)(2,1)S(1)} collective-permute-done((bf16[28,32,128]{2,1,0:T(8,128)(2,1)S(1)}, bf16[28,32,128]{2,1,0:T(8,128)(2,1)S(1)}, u32[]{:S(2)}, u32[]{:S(2)}) %collective-permute-start.14) | collective-permute-done | bytes 229408 | tf_op jit(solution)/shard_map/ppermute | solution.py:297
  98.9 0.0 collective-permute-done.15.refs_11_
  99.0 1.7 %finish.1 = bf16[16,2,2,32,128]{4,3,2,1,0:T(8,128)(2,1)} custom-call(s32[5]{0:T(128)S(1)} %stack.23.pos, f32[14,32,128]{2,1,0:T(8,128)S(1)} %bitcast.23, f32[14,32,128]{2,1,0:T(8,128)S(1)} %bitcast.24, f32[14,32,128]{2,1,0:T(8,128)S(1)} %bitcast.25, f32[14,32,128]{2,1,0:T(8,128)S(1)} %bitcast.26, f32[14,32,128]{2,1,0:T(8,128)S(1)} %bitcast.27, ...), custom_call_target="tpu_custom_call" | custom-call | flops 917504 | bytes 3440640 | tf_op jit(solution)/shard_map/finish/pallas_call | solution.py:220
  100.7 3.6 %all-to-all-start.1 = ((bf16[16,2,2,32,128]{4,3,2,1,0:T(8,128)(2,1)}), bf16[16,2,2,32,128]{4,3,2,1,0:T(8,128)(2,1)S(1)}, u32[]{:S(2)}, u32[]{:S(2)}) async-start(bf16[16,2,2,32,128]{4,3,2,1,0:T(8,128)(2,1)} %finish.1), calls=%async_computation.1 | async-start | bytes 1048576 | tf_op jit(solution)/shard_map/all_to_all | solution.py:340
  104.3 0.0 copy-done.2
  104.3 1.9 %collective-permute-start.16 = (bf16[64,256]{1,0:T(8,128)(2,1)S(1)}, bf16[64,256]{1,0:T(8,128)(2,1)S(1)}, u32[]{:S(2)}, u32[]{:S(2)}) collective-permute-start(bf16[64,256]{1,0:T(8,128)(2,1)S(1)} %bitcast.32), channel_id=1, source_target_pairs={{0,1},{1,0},{2,3},{3,2},{4,5},{5,4},{6,7},{7,6},{8,9},{9,8},{10,11... | collective-permute-start | bytes 98312 | tf_op jit(solution)/shard_map/ppermute | solution.py:297
  106.1 2.7 %collective-permute-done.16.inv_other = bf16[64,256]{1,0:T(8,128)(2,1)S(1)} collective-permute-done((bf16[64,256]{1,0:T(8,128)(2,1)S(1)}, bf16[64,256]{1,0:T(8,128)(2,1)S(1)}, u32[]{:S(2)}, u32[]{:S(2)}) %collective-permute-start.16) | collective-permute-done | bytes 32800 | tf_op jit(solution)/shard_map/ppermute | solution.py:297
  108.9 5.5 %all-to-all-done.1.arrived = bf16[16,2,2,32,128]{4,3,2,1,0:T(8,128)(2,1)S(1)} async-done(((bf16[16,2,2,32,128]{4,3,2,1,0:T(8,128)(2,1)}), bf16[16,2,2,32,128]{4,3,2,1,0:T(8,128)(2,1)S(1)}, u32[]{:S(2)}, u32[]{:S(2)}) %all-to-all-start.1) | async-done | bytes 524320 | tf_op jit(solution)/shard_map/all_to_all | solution.py:340
  114.3 0.0 copy-done.1
  114.3 0.0 copy-done.6
  114.3 1.7 %tail.1 = (bf16[224,512]{1,0:T(8,128)(2,1)}, f32[96,224]{1,0:T(8,128)}, f32[64,96]{1,0:T(8,128)}, bf16[32,512]{1,0:T(8,128)(2,1)}) custom-call(s32[5]{0:T(128)S(1)} %stack.23.pos, bf16[16,2,2,32,128]{4,3,2,1,0:T(8,128)(2,1)S(1)} %all-to-all-done.1.arrived, bf16[96,512]{1,0:T(8,128)(2,1)S(1)} %bitcast.31, bf16[64,256]{1,0:T(8,128)(2,1)S(1)} %bitcast.33, ...), custom_call_target="tpu_custom_call" | custom-call | flops 75497472 | bytes 786432 | tf_op jit(solution)/shard_map/tail/pallas_call | solution.py:281
  (10 shorter events, 0.0 us)
Async XLA Ops:
  0.6 1.2 %copy-start = (bf16[1024,512]{1,0:T(8,128)(2,1)S(1)}, bf16[1024,512]{1,0:T(8,128)(2,1)}, u32[]{:S(2)}) copy-start(bf16[1024,512]{1,0:T(8,128)(2,1)} %param.11) | copy-start | bytes 3145732
  1.9 0.7 copy-start.3
  2.5 0.7 copy-start.4
  3.2 0.7 copy-start.5
  5.2 27.7 %all-to-all-start = ((bf16[16,9,32,128]{3,2,1,0:T(8,128)(2,1)}), bf16[16,9,32,128]{3,2,1,0:T(8,128)(2,1)S(1)}, u32[]{:S(2)}, u32[]{:S(2)}) async-start(bf16[16,9,32,128]{3,2,1,0:T(8,128)(2,1)} %pack.1), calls=%async_computation | async-start | bytes 2359296 | tf_op jit(solution)/shard_map/all_to_all | solution.py:320
  13.4 4.7 %copy-start.7 = (bf16[3584,1792]{1,0:T(8,128)(2,1)S(1)}, bf16[3584,1792]{1,0:T(8,128)(2,1)}, u32[]{:S(2)}) copy-start(bf16[3584,1792]{1,0:T(8,128)(2,1)} %param.9) | copy-start | bytes 38535172
  18.0 1.5 %copy-start.8 = (bf16[1792,512]{1,0:T(8,128)(2,1)S(1)}, bf16[1792,512]{1,0:T(8,128)(2,1)}, u32[]{:S(2)}) copy-start(bf16[1792,512]{1,0:T(8,128)(2,1)} %b_hbm.1) | copy-start | bytes 5505028
  29.0 0.8 copy-start.9
  29.8 0.8 copy-start.10
  30.6 0.8 copy-start.11
  31.4 0.8 copy-start.12
  32.2 0.8 copy-start.13
  32.9 47.9 %collective-permute-start.12 = (bf16[16,9,32,128]{3,2,1,0:T(8,128)(2,1)S(1)}, bf16[16,9,32,128]{3,2,1,0:T(8,128)(2,1)S(1)}, u32[]{:S(2)}, u32[]{:S(2)}) collective-permute-start(bf16[16,9,32,128]{3,2,1,0:T(8,128)(2,1)S(1)} %all-to-all-done.mine), channel_id=1, source_target_pairs={{0,16},{16,0},{32,48},{48,32},{64,80},{80,64},{96,112},{112,96},{1... | collective-permute-start | bytes 3538952 | tf_op jit(solution)/shard_map/ppermute | solution.py:297
  32.9 14.5 %collective-permute-start = (bf16[448,512]{1,0:T(8,128)(2,1)}, bf16[448,512]{1,0:T(8,128)(2,1)S(1)}, u32[]{:S(2)}, u32[]{:S(2)}) collective-permute-start(bf16[448,512]{1,0:T(8,128)(2,1)} %copy-done.13), channel_id=1, source_target_pairs={{0,4},{1,5},{2,6},{3,7},{4,8},{5,9},{6,10},{7,11},{8,12},{9,13},{1... | collective-permute-start | bytes 1376264 | tf_op jit(solution)/shard_map/ppermute | solution.py:297
  34.8 15.6 %collective-permute-start.1 = (bf16[448,512]{1,0:T(8,128)(2,1)}, bf16[448,512]{1,0:T(8,128)(2,1)S(1)}, u32[]{:S(2)}, u32[]{:S(2)}) collective-permute-start(bf16[448,512]{1,0:T(8,128)(2,1)} %copy-done.12), channel_id=1, source_target_pairs={{0,12},{1,13},{2,14},{3,15},{4,0},{5,1},{6,2},{7,3},{8,4},{9,5},{1... | collective-permute-start | bytes 1376264 | tf_op jit(solution)/shard_map/ppermute | solution.py:297
  36.2 23.7 %collective-permute-start.2 = (bf16[448,512]{1,0:T(8,128)(2,1)}, bf16[448,512]{1,0:T(8,128)(2,1)S(1)}, u32[]{:S(2)}, u32[]{:S(2)}) collective-permute-start(bf16[448,512]{1,0:T(8,128)(2,1)} %copy-done.11), channel_id=1, source_target_pairs={{0,8},{1,9},{2,10},{3,11},{4,12},{5,13},{6,14},{7,15},{8,0},{9,1},... | collective-permute-start | bytes 1376264 | tf_op jit(solution)/shard_map/ppermute | solution.py:297
  38.4 23.1 %collective-permute-start.6 = (bf16[4,448,128]{2,1,0:T(8,128)(2,1)}, bf16[4,448,128]{2,1,0:T(8,128)(2,1)S(1)}, u32[]{:S(2)}, u32[]{:S(2)}) collective-permute-start(bf16[4,448,128]{2,1,0:T(8,128)(2,1)} %copy-done.10), channel_id=1, source_target_pairs={{0,1},{1,2},{2,3},{3,0},{4,5},{5,6},{6,7},{7,4},{8,9},{9,10},{10,1... | collective-permute-start | bytes 1376264 | tf_op jit(solution)/shard_map/ppermute | solution.py:297
  47.4 26.7 %collective-permute-start.7 = (bf16[4,448,128]{2,1,0:T(8,128)(2,1)}, bf16[4,448,128]{2,1,0:T(8,128)(2,1)S(1)}, u32[]{:S(2)}, u32[]{:S(2)}) collective-permute-start(bf16[4,448,128]{2,1,0:T(8,128)(2,1)} %copy-done.9), channel_id=1, source_target_pairs={{0,3},{1,0},{2,1},{3,2},{4,7},{5,4},{6,5},{7,6},{8,11},{9,8},{10,9... | collective-permute-start | bytes 1376264 | tf_op jit(solution)/shard_map/ppermute | solution.py:297
  50.4 27.5 %collective-permute-start.8 = (bf16[4,448,128]{2,1,0:T(8,128)(2,1)S(1)}, bf16[4,448,128]{2,1,0:T(8,128)(2,1)S(1)}, u32[]{:S(2)}, u32[]{:S(2)}) collective-permute-start(bf16[4,448,128]{2,1,0:T(8,128)(2,1)S(1)} %get-tuple-element.45), channel_id=1, source_target_pairs={{0,2},{1,3},{2,0},{3,1},{4,6},{5,7},{6,4},{7,5},{8,10},{9,11},{10,... | collective-permute-start | bytes 1376264 | tf_op jit(solution)/shard_map/ppermute | solution.py:297
  60.8 24.6 %collective-permute-start.3 = (f32[448,128]{1,0:T(8,128)S(1)}, f32[448,128]{1,0:T(8,128)S(1)}, u32[]{:S(2)}, u32[]{:S(2)}) collective-permute-start(f32[448,128]{1,0:T(8,128)S(1)} %get-tuple-element.39), channel_id=1, source_target_pairs={{0,1},{1,2},{2,3},{3,0},{4,5},{5,6},{6,7},{7,4},{8,9},{9,10},{10,1... | collective-permute-start | bytes 688136 | tf_op jit(solution)/shard_map/ppermute | solution.py:297
  61.4 26.6 %collective-permute-start.4 = (f32[448,128]{1,0:T(8,128)S(1)}, f32[448,128]{1,0:T(8,128)S(1)}, u32[]{:S(2)}, u32[]{:S(2)}) collective-permute-start(f32[448,128]{1,0:T(8,128)S(1)} %get-tuple-element.40), channel_id=1, source_target_pairs={{0,2},{1,3},{2,0},{3,1},{4,6},{5,7},{6,4},{7,5},{8,10},{9,11},{10,... | collective-permute-start | bytes 688136 | tf_op jit(solution)/shard_map/ppermute | solution.py:297
  74.1 15.5 %collective-permute-start.5 = (f32[448,128]{1,0:T(8,128)S(1)}, f32[448,128]{1,0:T(8,128)S(1)}, u32[]{:S(2)}, u32[]{:S(2)}) collective-permute-start(f32[448,128]{1,0:T(8,128)S(1)} %get-tuple-element.41), channel_id=1, source_target_pairs={{0,3},{1,0},{2,1},{3,2},{4,7},{5,4},{6,5},{7,6},{8,11},{9,8},{10,9... | collective-permute-start | bytes 688136 | tf_op jit(solution)/shard_map/ppermute | solution.py:297
  78.6 13.9 %collective-permute-start.9 = (f32[448,128]{1,0:T(8,128)S(1)}, f32[448,128]{1,0:T(8,128)S(1)}, u32[]{:S(2)}, u32[]{:S(2)}) collective-permute-start(f32[448,128]{1,0:T(8,128)S(1)} %get-tuple-element.47), channel_id=1, source_target_pairs={{0,4},{1,5},{2,6},{3,7},{4,8},{5,9},{6,10},{7,11},{8,12},{9,13},{1... | collective-permute-start | bytes 688136 | tf_op jit(solution)/shard_map/ppermute | solution.py:297
  80.8 13.1 %collective-permute-start.10 = (f32[448,128]{1,0:T(8,128)S(1)}, f32[448,128]{1,0:T(8,128)S(1)}, u32[]{:S(2)}, u32[]{:S(2)}) collective-permute-start(f32[448,128]{1,0:T(8,128)S(1)} %get-tuple-element.48), channel_id=1, source_target_pairs={{0,8},{1,9},{2,10},{3,11},{4,12},{5,13},{6,14},{7,15},{8,0},{9,1},... | collective-permute-start | bytes 688136 | tf_op jit(solution)/shard_map/ppermute | solution.py:297
  85.4 8.5 %collective-permute-start.11 = (f32[448,128]{1,0:T(8,128)S(1)}, f32[448,128]{1,0:T(8,128)S(1)}, u32[]{:S(2)}, u32[]{:S(2)}) collective-permute-start(f32[448,128]{1,0:T(8,128)S(1)} %get-tuple-element.49), channel_id=1, source_target_pairs={{0,12},{1,13},{2,14},{3,15},{4,0},{5,1},{6,2},{7,3},{8,4},{9,5},{1... | collective-permute-start | bytes 688136 | tf_op jit(solution)/shard_map/ppermute | solution.py:297
  88.0 7.2 %collective-permute-start.13 = (bf16[28,32,128]{2,1,0:T(8,128)(2,1)S(1)}, bf16[28,32,128]{2,1,0:T(8,128)(2,1)S(1)}, u32[]{:S(2)}, u32[]{:S(2)}) collective-permute-start(bf16[28,32,128]{2,1,0:T(8,128)(2,1)S(1)} %get-tuple-element.52), channel_id=1, source_target_pairs={{0,32},{16,48},{32,64},{48,80},{64,96},{80,112},{96,0},{112,16},{1... | collective-permute-start | bytes 688136 | tf_op jit(solution)/shard_map/ppermute | solution.py:297
  89.6 9.3 %collective-permute-start.14 = (bf16[28,32,128]{2,1,0:T(8,128)(2,1)S(1)}, bf16[28,32,128]{2,1,0:T(8,128)(2,1)S(1)}, u32[]{:S(2)}, u32[]{:S(2)}) collective-permute-start(bf16[28,32,128]{2,1,0:T(8,128)(2,1)S(1)} %get-tuple-element.53), channel_id=1, source_target_pairs={{0,64},{16,80},{32,96},{48,112},{64,0},{80,16},{96,32},{112,48},{1... | collective-permute-start | bytes 688136 | tf_op jit(solution)/shard_map/ppermute | solution.py:297
  92.5 6.4 %collective-permute-start.15 = (bf16[28,32,128]{2,1,0:T(8,128)(2,1)S(1)}, bf16[28,32,128]{2,1,0:T(8,128)(2,1)S(1)}, u32[]{:S(2)}, u32[]{:S(2)}) collective-permute-start(bf16[28,32,128]{2,1,0:T(8,128)(2,1)S(1)} %get-tuple-element.54), channel_id=1, source_target_pairs={{0,96},{16,112},{32,0},{48,16},{64,32},{80,48},{96,64},{112,80},{1... | collective-permute-start | bytes 688136 | tf_op jit(solution)/shard_map/ppermute | solution.py:297
  98.9 5.3 %copy-start.2 = (bf16[256,64]{0,1:T(8,128)(2,1)S(1)}, bf16[256,64]{0,1:T(8,128)(2,1)}, u32[]{:S(2)}) copy-start(bf16[256,64]{0,1:T(8,128)(2,1)} %param.15) | copy-start | bytes 98308
  98.9 15.4 %copy-start.1 = (bf16[512,96]{0,1:T(8,128)(2,1)S(1)}, bf16[512,96]{0,1:T(8,128)(2,1)}, u32[]{:S(2)}) copy-start(bf16[512,96]{0,1:T(8,128)(2,1)} %param.14) | copy-start | bytes 294916
  98.9 15.4 %copy-start.6 = (s32[1,32]{1,0:T(1,128)S(1)}, s32[1,32]{1,0:T(1,128)}, u32[]{:S(2)}) copy-start(s32[1,32]{1,0:T(1,128)} %piv_parent.1) | copy-start | bytes 388
  100.7 13.6 %all-to-all-start.1 = ((bf16[16,2,2,32,128]{4,3,2,1,0:T(8,128)(2,1)}), bf16[16,2,2,32,128]{4,3,2,1,0:T(8,128)(2,1)S(1)}, u32[]{:S(2)}, u32[]{:S(2)}) async-start(bf16[16,2,2,32,128]{4,3,2,1,0:T(8,128)(2,1)} %finish.1), calls=%async_computation.1 | async-start | bytes 1048576 | tf_op jit(solution)/shard_map/all_to_all | solution.py:340
  104.3 4.6 %collective-permute-start.16 = (bf16[64,256]{1,0:T(8,128)(2,1)S(1)}, bf16[64,256]{1,0:T(8,128)(2,1)S(1)}, u32[]{:S(2)}, u32[]{:S(2)}) collective-permute-start(bf16[64,256]{1,0:T(8,128)(2,1)S(1)} %bitcast.32), channel_id=1, source_target_pairs={{0,1},{1,0},{2,3},{3,2},{4,5},{5,4},{6,7},{7,6},{8,9},{9,8},{10,11... | collective-permute-start | bytes 98312 | tf_op jit(solution)/shard_map/ppermute | solution.py:297

commit v2 on v1

v2 whole, which is shorter than its diff:
```python
import functools

import jax
import jax.numpy as jnp
from jax import lax
from jax.experimental import pallas as pl
from jax.experimental.pallas import tpu as pltpu
from jax.sharding import PartitionSpec as P

BF16 = jnp.bfloat16
F32 = jnp.float32
BLK = 128
CBD = 8
NX = 4
NZ = 4
NY = 4
UNIT = 32
SCALE = 1
COLS = 128
LOCAL = pl.BlockSpec(memory_space=pltpu.VMEM)
REMAIN = pl.BlockSpec(memory_space=pltpu.HBM)
ANY = pl.BlockSpec(memory_space=pl.ANY)


def params(mebibytes):
    return pltpu.CompilerParams(vmem_limit_bytes=mebibytes * 1024 * 1024)


def cost(flops, moved_bytes):
    return pl.CostEstimate(flops=flops // SCALE, bytes_accessed=moved_bytes // SCALE, transcendentals=0)


def place_in_mesh():
    row, column = lax.axis_index("frow"), lax.axis_index("fcol")
    return column // NZ, column % NZ, column, row // 2, row % 2


def remote(value):
    return pltpu.with_memory_space_constraint(value, pltpu.HBM)


def fetch(pairs, sems):
    copies = [pltpu.make_async_copy(src, dst, sems.at[i]) for i, (src, dst) in enumerate(pairs)]
    for copy in copies:
        copy.start()
    return copies


def front_kernel(a_hbm, b_hbm, x0, x1, x3, xa, xb, z0, z1, z3, za, zb,
                 a, b, turned, value, sx0, sx1, sx3, sz0, sz1, sz3, sems, out_sems, *, cuts):
    x, z = place_in_mesh()[:2]
    half = a.shape[0] // 2
    spans = list(zip(cuts[:-1], cuts[1:]))
    copies = [pltpu.make_async_copy(b_hbm, b, sems.at[0])]
    copies += [pltpu.make_async_copy(a_hbm.at[lo:hi], a.at[lo:hi], sems.at[i + 1]) for i, (lo, hi) in enumerate(spans)]
    for copy in copies[:3]:
        copy.start()

    def arrive(i):
        copies[i].wait()
        if i + 3 < len(copies):
            copies[i + 3].start()

    stores = []

    def store(staged, out, at):
        copy = pltpu.make_async_copy(staged.at[at], out.at[at], out_sems.at[len(stores)])
        copy.start()
        stores.append(copy)

    arrive(0)
    for s in range(NZ):
        at = pl.multiple_of((z + s) % NZ * COLS, COLS)
        turned[:, s * COLS : (s + 1) * COLS] = b[:, pl.ds(at, COLS)]
    for i, (lo, hi) in enumerate(spans):
        arrive(i + 1)
        rows = (hi - lo) * BLK
        block = a[lo:hi].reshape(rows, a.shape[-1])
        product = jnp.dot(block, turned[...], preferred_element_type=F32)
        product = product.reshape(hi - lo, NX, UNIT, NZ * COLS)
        if hi <= half:
            value[: hi - lo] = product
            for s, staged, out in ((0, sx0, x0), (1, sx1, x1), (3, sx3, x3)):
                staged[lo:hi] = value[: hi - lo, (x + s) % NX]
                store(staged, out, pl.ds(lo, hi - lo))
            out, at = (xa, lo) if hi <= half // 2 else (xb, lo - half // 2)
            out[at : at + hi - lo] = value[: hi - lo, (x + 2) % NX].astype(BF16)
        else:
            for jr in range(NX):
                at = jr * half + lo - half
                piece = product[:, jr]
                for s, staged, out in ((0, sz0, z0), (1, sz1, z1), (3, sz3, z3)):
                    staged[at : at + hi - lo] = piece[..., s * COLS : (s + 1) * COLS]
                    store(staged, out, pl.ds(at, hi - lo))
                out, at = (za, at) if jr < NX // 2 else (zb, at - NX // 2 * half)
                out[at : at + hi - lo] = piece[..., 2 * COLS : 3 * COLS].astype(BF16)
    for copy in stores:
        copy.wait()


def inverse_tiles(shape):
    return [
        (slice(i, i + UNIT), slice(j, j + COLS))
        for i in range(0, shape[0], UNIT)
        for j in range(0, shape[1], COLS)
    ]


def front_products(front, test):
    blocks, depth, cols = front.shape[0] // BLK, front.shape[1], test.shape[1]
    half = blocks // 2
    step = half // 2
    cuts = (0, step // 2, *range(step, blocks + 1, step))
    kinds = ((1, F32), (1, F32), (1, F32), (2, BF16), (2, BF16))
    shapes = [((half // n, UNIT, cols), t) for n, t in kinds]
    shapes += [((NX * half // n, UNIT, COLS), t) for n, t in kinds]
    return pl.pallas_call(
        functools.partial(front_kernel, cuts=cuts),
        out_shape=[(pltpu.HBM if s[1] == F32 else jax.ShapeDtypeStruct)(*s) for s in shapes],
        in_specs=[REMAIN, REMAIN],
        out_specs=([REMAIN] * 3 + [LOCAL] * 2) * 2,
        scratch_shapes=[
            pltpu.VMEM((blocks, BLK, depth), BF16),
            pltpu.VMEM(test.shape, BF16),
            pltpu.VMEM(test.shape, BF16),
            pltpu.VMEM((step, NX, UNIT, cols), F32),
            *[pltpu.VMEM(*shape) for shape in shapes if shape[1] == F32],
            pltpu.SemaphoreType.DMA((len(cuts),)),
            pltpu.SemaphoreType.DMA((3 * (len(cuts) - 1 + 2 * NX),)),
        ],
        compiler_params=params(30),
        cost_estimate=cost(
            2 * front.size * cols, 2 * (front.size + test.size) + 5 * blocks * BLK * cols
        ),
        name="front",
    )(remote(front.reshape(blocks, BLK, depth)), remote(test))


def relay_kernel(hx1, hx3, xa, xb, hz1, hz3, za, zb, inverse, _, x_up, x_down, z_up, z_down, __,
                 x1, x3, z1, z3, sems):
    copies = fetch([(hx1, x1), (hx3, x3), (hz1, z1), (hz3, z3)], sems)
    for copy, own, part, out, at in zip(
        copies, (x1, x3, z1, z3), (xa, xb, za, zb), (x_up, x_down, z_up, z_down),
        (0, xa.shape[0], 0, za.shape[0]),
    ):
        copy.wait()
        half = part.shape[0]
        rest = half - at
        out[at : at + half] = (own[at : at + half] + part[...].astype(F32)).astype(BF16)
        out[rest : rest + half] = own[rest : rest + half].astype(BF16)
    for out in (z_up, z_down):
        for i, (rows, columns) in enumerate(inverse_tiles(inverse.shape)):
            out[z1.shape[0] + i] = inverse[rows, columns]


def relay(x1, x3, xa, xb, z1, z3, za, zb, inverse, mine):
    extra = len(inverse_tiles(inverse.shape))
    z_shape = (z1.shape[0] + extra, *z1.shape[1:])
    shapes = [x1.shape, x1.shape, z_shape, z_shape, mine.shape]
    return pl.pallas_call(
        relay_kernel,
        out_shape=[jax.ShapeDtypeStruct(shape, BF16) for shape in shapes],
        in_specs=([REMAIN] * 2 + [LOCAL] * 2) * 2 + [LOCAL] * 2,
        out_specs=[LOCAL] * 5,
        scratch_shapes=[
            *[pltpu.VMEM(v.shape, F32) for v in (x1, x3, z1, z3)],
            pltpu.SemaphoreType.DMA((4,)),
        ],
        input_output_aliases={9: 4},
        compiler_params=params(8),
        cost_estimate=cost(4 * x1.size, 14 * x1.size),
        name="relay",
    )(remote(x1), remote(x3), xa, xb, remote(z1), remote(z3), za, zb, inverse, mine)


def sum_x_kernel(held, r1, r2, token, to1, to2, to3, keep, own, sems):
    fetch([(held, own)], sems)[0].wait()
    for s, out in ((1, to1), (2, to2), (3, to3), (0, keep)):
        at = (slice(None), slice(None), slice(s * COLS, (s + 1) * COLS))
        out[...] = own[at] + r1[at].astype(F32) + r2[at].astype(F32)


def sum_z_kernel(held, r1, r2, token, to1, to2, to3, keep, inverse, own, sems):
    fetch([(held, own)], sems)[0].wait()
    x, z = place_in_mesh()[:2]
    half = keep.shape[0]
    for s, out in ((1, to1), (2, to2), (3, to3), (0, keep)):
        at = pl.ds((x + s) % NX * half, half)
        out[...] = own[at] + r1[at].astype(F32) + r2[at].astype(F32)
    for i, (rows, columns) in enumerate(inverse_tiles(inverse.shape)):
        inverse[rows, columns] = lax.select(z % 2 == 0, r2[NX * half + i], r1[NX * half + i])


def partial_sum(kernel, own, arrived, token, half, extra):
    piece = jax.ShapeDtypeStruct((half, UNIT, COLS), F32)
    outs = [piece] * 4 + extra
    return pl.pallas_call(
        kernel,
        out_shape=outs,
        in_specs=[REMAIN] + [LOCAL] * 2 + [ANY],
        out_specs=[LOCAL] * len(outs),
        scratch_shapes=[pltpu.VMEM(own.shape, F32), pltpu.SemaphoreType.DMA((1,))],
        compiler_params=params(8),
        cost_estimate=cost(3 * own.size, 14 * own.size),
        name=kernel.__name__[:5],
    )(remote(own), *arrived, token)


def pack_kernel(child, group_hbm, block_hbm, pivots_hbm, out, group, block, pivots, facts, sems, *, blocks):
    copies = fetch(
        [(group_hbm, group), (block_hbm, block), (pivots_hbm, pivots)]
        + [
            (child.at[:, x * UNIT : (x + 1) * UNIT, z * COLS : (z + 1) * COLS], out.at[x * NZ + z, :CBD])
            for x in range(NX)
            for z in range(NZ)
        ],
        sems,
    )
    facts[...] = jnp.zeros_like(facts)
    for copy in copies[:3]:
        copy.wait()
    facts[0:1, : group.shape[1]] = (group[...] * blocks + block[...]).astype(F32)
    facts[1:2, : pivots.shape[1]] = pivots[...].astype(F32)
    told = facts[...].astype(BF16)
    for i in range(out.shape[0]):
        out[i, CBD] = told
    for copy in copies[3:]:
        copy.wait()


def pack(child, group, block, pivots, blocks):
    return pl.pallas_call(
        functools.partial(pack_kernel, blocks=blocks),
        out_shape=jax.ShapeDtypeStruct((NX * NZ, CBD + 1, UNIT, COLS), BF16),
        in_specs=[REMAIN] * 4,
        out_specs=LOCAL,
        scratch_shapes=[
            *[pltpu.VMEM(v.shape, v.dtype) for v in (group, block, pivots)],
            pltpu.VMEM((UNIT, COLS), F32),
            pltpu.SemaphoreType.DMA((NX * NZ + 3,)),
        ],
        compiler_params=params(60),
        cost_estimate=cost(0, 4 * child.size),
        name="pack",
    )(child.reshape(CBD, BLK, child.shape[1]), group, block, pivots)


def place_kernel(mine, other, out, own, pivots, total, facts, told, slots, sems):
    pos = place_in_mesh()
    blocks = own.shape[0]
    sources = mine.shape[0]
    for t, ref in ((0, mine), (1, other)):
        told[t * sources : (t + 1) * sources] = ref[:, CBD].astype(F32)
    dest = told[:, 0].astype(jnp.int32)
    group = dest // blocks
    facts[...] = jnp.where(
        group % 2 == pos[4], group // 2 * blocks + dest % blocks, NY * blocks
    )
    copy = pltpu.make_async_copy(facts, slots, sems.at[0])
    copy.start()
    pivots[...] = told[pl.ds(pos[2] // 2 * 2, 2), 1].astype(jnp.int32)
    total[...] = jnp.zeros_like(total)
    copy.wait()
    for t, ref in ((0, mine), (1, other)):
        def body(i, _, t=t, ref=ref):
            for j in range(CBD):
                at = slots[t * sources + i, j]
                total[at] += ref[i, j].astype(F32)
            return _

        lax.fori_loop(0, sources, body, 0)
    own[...] = total[pl.ds(pos[3] * blocks, blocks)]
    out[...] = total[: NY * blocks].reshape(out.shape).astype(BF16)


def place(mine, other, blocks):
    piece = (blocks, UNIT, COLS)
    sources = mine.shape[0]
    return pl.pallas_call(
        place_kernel,
        out_shape=[
            jax.ShapeDtypeStruct((NY, *piece), BF16),
            jax.ShapeDtypeStruct(piece, F32),
            jax.ShapeDtypeStruct((2, COLS), jnp.int32),
        ],
        in_specs=[LOCAL] * 2,
        out_specs=[LOCAL] * 3,
        scratch_shapes=[
            pltpu.VMEM((NY * blocks + 1, UNIT, COLS), F32),
            pltpu.VMEM((2 * sources, COLS), jnp.int32),
            pltpu.VMEM((2 * sources, UNIT, COLS), F32),
            pltpu.SMEM((2 * sources, COLS), jnp.int32),
            pltpu.SemaphoreType.DMA((1,)),
        ],
        compiler_params=params(8),
        cost_estimate=cost(16 * mine.size, 8 * mine.size),
        name="place",
    )(mine, other)


def finish_kernel(*refs):
    pos = place_in_mesh()
    fx, fz, own, arrived, out, total = refs[:4], refs[4:8], *refs[8:12]
    half = fx[0].shape[0]
    blocks = 2 * half
    for first, part in ((0, fx), (half, fz)):
        value = part[0][...] + part[1][...] + part[2][...] + part[3][...]
        span = slice(first, first + half)
        value = value + own[span]
        for shift in (1, 2, 3):
            value = value + arrived[(pos[3] + shift) % NY, span].astype(F32)
        total[span] = value.astype(BF16)
    units = blocks * NX // out.shape[0]
    for leaf in range(out.shape[0]):
        offset = (pos[0] - units * leaf) % NX
        for slot in range(2):
            unit = units * leaf + offset + NX * slot
            value = total[jnp.minimum(unit // NX, blocks - 1)]
            for dest in (leaf // 2 * 2, leaf // 2 * 2 + 1):
                out[dest, leaf % 2, slot] = value


def finish(fx, fz, own, arrived, leaves):
    blocks = own.shape[0]
    piece = (blocks // 2, UNIT, COLS)
    return pl.pallas_call(
        finish_kernel,
        out_shape=jax.ShapeDtypeStruct((leaves, 2, 2, UNIT, COLS), BF16),
        in_specs=[LOCAL] * 10,
        out_specs=LOCAL,
        scratch_shapes=[pltpu.VMEM(own.shape, BF16)],
        compiler_params=params(8),
        cost_estimate=cost(8 * own.size, 30 * own.size),
        name="finish",
    )(*[f.reshape(piece) for f in fx], *[f.reshape(piece) for f in fz], own, arrived)


def across(a, b):
    return lax.dot_general(a, b, (((1,), (1,)), ((), ())), preferred_element_type=F32)


def tail_kernel(arrived, inv_leaf, inv_own, inv_other, piv_leaf, piv_parent,
                samples, interp_leaf, interp_parent, skeleton_parent, rows, stacked):
    pos = place_in_mesh()
    leaf = pos[2]
    units = samples.shape[0] // UNIT
    parity = leaf % 2
    for x in range(NX):
        for z in range(NZ):
            for t in range(2):
                offset = (x - units * (leaf - parity + t)) % NX
                for slot in range(2):
                    rows[t, offset + NX * slot, :, z * COLS : (z + 1) * COLS] = arrived[x * NZ + z, t, slot]
    padded = rows.shape[1] * UNIT
    count = samples.shape[0]
    rank = interp_parent.shape[1]
    leaf_rows = rows[parity].reshape(padded, rows.shape[-1])
    samples[...] = leaf_rows[:count]
    interp_leaf[...] = across(inv_leaf[...], leaf_rows)[:, :count]

    def pick(pivots, source):
        hit = lax.broadcasted_iota(jnp.int32, (source.shape[0], pivots.shape[1]), 0) == pivots
        return lax.dot_general(
            hit.astype(F32).astype(BF16), source, (((0,), (0,)), ((), ())), preferred_element_type=F32
        ).astype(BF16)

    for t in range(2):
        stacked[t] = pick(piv_leaf[t : t + 1], rows[t].reshape(padded, rows.shape[-1]))
    both = stacked[...].reshape(2 * rank, stacked.shape[-1])
    skeleton_parent[...] = pick(piv_parent[...], both)
    depth = inv_own.shape[1]
    skeleton = stacked[parity]
    even = lax.select(parity == 0, inv_own[...], inv_other[...])
    odd = lax.select(parity == 0, inv_other[...], inv_own[...])
    interp_parent[...] = across(even, skeleton[:, :depth]) + across(odd, skeleton[:, depth:])


def tail(arrived, inv_leaf, inv_own, inv_other, piv_leaf, piv_parent, count):
    rank, cols = inv_leaf.shape
    padded = 2 * NX * UNIT
    args = (arrived, inv_leaf, inv_own, inv_other, piv_leaf, piv_parent)
    outs = [
        jax.ShapeDtypeStruct((count, cols), BF16),
        jax.ShapeDtypeStruct((rank, count), F32),
        jax.ShapeDtypeStruct((inv_own.shape[0], rank), F32),
        jax.ShapeDtypeStruct((piv_parent.shape[1], cols), BF16),
    ]
    return pl.pallas_call(
        tail_kernel,
        out_shape=outs,
        in_specs=[LOCAL] * len(args),
        out_specs=[LOCAL] * len(outs),
        scratch_shapes=[
            pltpu.VMEM((2, padded // UNIT, UNIT, cols), BF16),
            pltpu.VMEM((2, rank, cols), BF16),
        ],
        compiler_params=params(8),
        cost_estimate=cost(6 * padded * rank * cols, 6 * padded * cols),
        name="tail",
    )(*args)


def moved(x, axis, to):
    return lax.ppermute(x, axis, [(i, to(i)) for i in range(lax.axis_size(axis))])


def along_x(shift):
    return lambda i: (i + NZ * shift) % (NX * NZ)


def along_z(shift):
    return lambda i: i // NZ * NZ + (i + shift) % NZ


def on_device(front, test, child, child_group, child_block, inv_leaf, inv_parent, pivot_leaf, pivot_parent):
    row, column = lax.axis_index("frow"), lax.axis_index("fcol")
    leaves = lax.axis_size("fcol")
    blocks = front.shape[0] // BLK
    rank = pivot_leaf.shape[1]

    packed = pack(child, child_group.T, child_block.reshape(1, CBD), pivot_leaf, blocks)
    mine = lax.all_to_all(packed, "fcol", 0, 0, tiled=True)

    own_x, x1, x3, xa, xb, own_z, z1, z3, za, zb = front_products(front, test)
    xa, xb = moved(xa, "fcol", along_x(1)), moved(xb, "fcol", along_x(3))
    za, zb = moved(za, "fcol", along_z(1)), moved(zb, "fcol", along_z(3))
    x_up, x_down, z_up, z_down, mine = relay(x1, x3, xa, xb, z1, z3, za, zb, inv_parent.T, mine)
    other = moved(mine, "frow", lambda i: i ^ 1)
    in_x = [moved(x_up, "fcol", along_x(1)), moved(x_down, "fcol", along_x(3))]
    in_z = [moved(z_up, "fcol", along_z(1)), moved(z_down, "fcol", along_z(3))]

    out_y, own_y, piv_leaf = place(mine, other, blocks)
    in_y = lax.all_to_all(
        out_y, "frow", 0, 0, tiled=True, axis_index_groups=[[2 * i + core for i in range(NY)] for core in range(2)]
    )
    token, piv_leaf = piv_leaf, piv_leaf[:, :rank]

    half = blocks // 2
    *out_x, own_x = partial_sum(sum_x_kernel, own_x, in_x, token, half, [])
    in_x = [moved(v, "fcol", along_z(s)) for s, v in zip((1, 2, 3), out_x)]
    inverse = jax.ShapeDtypeStruct(inv_parent.T.shape, BF16)
    *out_z, own_z, inv_other = partial_sum(sum_z_kernel, own_z, in_z, token, half, [inverse])
    in_z = [moved(v, "fcol", along_x(s)) for s, v in zip((1, 2, 3), out_z)]

    placed = finish([own_x, *in_x], [own_z, *in_z], own_y, in_y, leaves)
    arrived = lax.all_to_all(placed, "fcol", 0, 0, tiled=True)
    count = front.shape[0] // leaves
    samples, interp_leaf, interp_parent, skeleton_parent = tail(
        arrived, inv_leaf.T, inv_parent.T, inv_other, piv_leaf, pivot_parent, count
    )
    return samples, interp_leaf.T, interp_parent.T, skeleton_parent


def solution(mesh):
    both = P(("frow", "fcol"), None)
    return jax.shard_map(
        on_device,
        mesh=mesh,
        in_specs=(P("frow", "fcol"), P("fcol", None), both, both, P(("frow", "fcol")), both, both, both, both),
        out_specs=(both,) * 4,
        check_vma=False,
    )
```

time: 117 us -> 91.1 us (0.78)
  waiting for transfers between devices: 31.5 us -> 12.3 us
  blocking collectives: 0 us -> 15.1 us
  starting transfers between devices: 51.5 us -> 37.2 us
  local copies, waits for them, and re-layouts: 13.3 us -> 0.63 us
  Pallas kernels: 19 us -> 24.7 us
    ppermute x17 -> x15, starting transfers between devices: 40 us -> 24.8 us  [moved(): lax.ppermute(x, axis, [(i, to(i)) for i in range(lax.axis_size(axis))])]
    all_to_all x0 -> x1, blocking collectives: none -> 15.1 us  [on_device(): arrived = lax.all_to_all(placed, 'fcol', 0, 0, tiled=True)]
    ppermute x17 -> x15, waiting for transfers between devices: 26 us -> 12.2 us  [moved(): lax.ppermute(x, axis, [(i, to(i)) for i in range(lax.axis_size(axis))])]
    unnamed x28 -> x12, local copies, waits for them, and re-layouts: 13.2 us -> 0.63 us
    pallas_call x5 -> x6, Pallas kernels: 15.8 us -> 21.8 us  [the longest x1 11.1 us: front_products(): pl.pallas_call(functools.partial(front_kernel, cuts=cuts), out_shape=[(pl...]
    all_to_all x1, waiting for transfers between devices: 5.45 us -> 0.01 us  [on_device(): lax.all_to_all(out_y, 'frow', 0, 0, tiled=True, axis_index_groups=[[2 * i...]
    pallas_call x1, Pallas kernels: 1.72 us -> 0.37 us  [finish(): pl.pallas_call(finish_kernel, out_shape=jax.ShapeDtypeStruct((leaves, 2,...]
  transfers between devices with their start and end apart: 19 -> 17, of which waited for: 6 -> 6; matrix products, arithmetic and copies ran while one was open for 0% -> 0% of each run, Pallas kernels for 12% -> 19%
where the time goes in v2:
time: 91.1 us; the launch traced here: 90.6 us
  starting transfers between devices  37.2 us (41%)
  Pallas kernels  24.7 us (27%)
  blocking collectives  15.1 us (17%)
  waiting for transfers between devices  12.3 us (14%)
    ppermute x15, starting transfers between devices, moved(): lax.ppermute(x, axis, [(i, to(i)) for i in range(lax.axis_size(axis))])  24.8 us
    all_to_all x1, blocking collectives, on_device(): arrived = lax.all_to_all(placed, 'fcol', 0, 0, tiled=True)  15.1 us
    ppermute x15, waiting for transfers between devices, moved(): lax.ppermute(x, axis, [(i, to(i)) for i in range(lax.axis_size(axis))])  12.2 us
    pallas_call x1, Pallas kernels, front_products(): pl.pallas_call(functools.partial(front_kernel, cuts=cuts), out_shape=[(pl...  11.1 us
    all_to_all x1, starting transfers between devices, on_device(): mine = lax.all_to_all(packed, 'fcol', 0, 0, tiled=True)  7.97 us
    all_to_all x1, starting transfers between devices, on_device(): lax.all_to_all(out_y, 'frow', 0, 0, tiled=True, axis_index_groups=[[2 * i...  4.46 us
    pallas_call x1, Pallas kernels, place(): pl.pallas_call(place_kernel, out_shape=[jax.ShapeDtypeStruct((NY, *piece)...  3.54 us
    pallas_call x1, Pallas kernels, relay(): pl.pallas_call(relay_kernel, out_shape=[jax.ShapeDtypeStruct(shape, BF16)...  3.29 us
  transfers between devices with their start and end apart: 17, of which 6 were waited for; matrix products, arithmetic and copies ran while one was open for 0% of the time, Pallas kernels for 19%

profile of v2, /device:TPU:0, one launch (start us, length us, event | category | flops | bytes accessed | tf_op | source)
XLA Modules:
  0.0 90.6 jit_solution(6028848660834117861)
XLA Ops:
  0.6 2.5 %pack.1 = bf16[16,9,32,128]{3,2,1,0:T(8,128)(2,1)} custom-call(bf16[8,128,512]{2,1,0:T(8,128)(2,1)} %bitcast.13, s32[1,8]{1,0:T(1,128)} %bitcast.14, s32[1,8]{1,0:T(1,128)} %bitcast.15, s32[1,96]{1,0:T(1,128)} %pivots_hbm.1), custom_call_target="tpu_custom_call" | custom-call | bytes 2097152 | tf_op jit(solution)/shard_map/pack/pallas_call | solution.py:232
  3.2 8.0 %all-to-all-start = ((bf16[16,9,32,128]{3,2,1,0:T(8,128)(2,1)}), bf16[16,9,32,128]{3,2,1,0:T(8,128)(2,1)S(1)}, u32[]{:S(2)}, u32[]{:S(2)}) async-start(bf16[16,9,32,128]{3,2,1,0:T(8,128)(2,1)} %pack.1), calls=%async_computation | async-start | bytes 2359296 | tf_op jit(solution)/shard_map/all_to_all | solution.py:422
  11.2 0.0 copy-start
  11.2 11.1 %front.1 = (f32[14,32,512]{2,1,0:T(8,128)}, f32[14,32,512]{2,1,0:T(8,128)}, f32[14,32,512]{2,1,0:T(8,128)}, bf16[7,32,512]{2,1,0:T(8,128)(2,1)S(1)}, bf16[7,32,5...) custom-call(bf16[28,128,1792]{2,1,0:T(8,128)(2,1)} %bitcast.16, ...), custom_call_target="tpu_custom_call" | custom-call | flops 6576668672 | bytes 23855104 | tf_op jit(solution)/shard_map/front/pallas_call | solution.py:117
  22.3 2.0 %collective-permute-start = (bf16[7,32,512]{2,1,0:T(8,128)(2,1)S(1)}, bf16[7,32,512]{2,1,0:T(8,128)(2,1)S(1)}, u32[]{:S(2)}, u32[]{:S(2)}) collective-permute-start(bf16[7,32,512]{2,1,0:T(8,128)(2,1)S(1)} %get-tuple-element.38), channel_id=1, source_target_pairs={{0,4},{1,5},{2,6},{3,7},{4,8},{5,9},{6,10},{7,11},{8,12},{9,13},{1... | collective-permute-start | bytes 688136 | tf_op jit(solution)/shard_map/ppermute | solution.py:404
  24.3 1.3 %collective-permute-start.1 = (bf16[7,32,512]{2,1,0:T(8,128)(2,1)S(1)}, bf16[7,32,512]{2,1,0:T(8,128)(2,1)S(1)}, u32[]{:S(2)}, u32[]{:S(2)}) collective-permute-start(bf16[7,32,512]{2,1,0:T(8,128)(2,1)S(1)} %get-tuple-element.39), channel_id=1, source_target_pairs={{0,12},{1,13},{2,14},{3,15},{4,0},{5,1},{6,2},{7,3},{8,4},{9,5},{1... | collective-permute-start | bytes 688136 | tf_op jit(solution)/shard_map/ppermute | solution.py:404
  25.6 1.9 %collective-permute-start.2 = (bf16[28,32,128]{2,1,0:T(8,128)(2,1)S(1)}, bf16[28,32,128]{2,1,0:T(8,128)(2,1)S(1)}, u32[]{:S(2)}, u32[]{:S(2)}) collective-permute-start(bf16[28,32,128]{2,1,0:T(8,128)(2,1)S(1)} %get-tuple-element.42), channel_id=1, source_target_pairs={{0,1},{1,2},{2,3},{3,0},{4,5},{5,6},{6,7},{7,4},{8,9},{9,10},{10,1... | collective-permute-start | bytes 688136 | tf_op jit(solution)/shard_map/ppermute | solution.py:404
  27.5 1.3 %collective-permute-start.3 = (bf16[28,32,128]{2,1,0:T(8,128)(2,1)S(1)}, bf16[28,32,128]{2,1,0:T(8,128)(2,1)S(1)}, u32[]{:S(2)}, u32[]{:S(2)}) collective-permute-start(bf16[28,32,128]{2,1,0:T(8,128)(2,1)S(1)} %get-tuple-element.43), channel_id=1, source_target_pairs={{0,3},{1,0},{2,1},{3,2},{4,7},{5,4},{6,5},{7,6},{8,11},{9,8},{10,9... | collective-permute-start | bytes 688136 | tf_op jit(solution)/shard_map/ppermute | solution.py:404
  28.8 3.6 %collective-permute-done.xa = bf16[7,32,512]{2,1,0:T(8,128)(2,1)S(1)} collective-permute-done((bf16[7,32,512]{2,1,0:T(8,128)(2,1)S(1)}, bf16[7,32,512]{2,1,0:T(8,128)(2,1)S(1)}, u32[]{:S(2)}, u32[]{:S(2)}) %collective-permute-start) | collective-permute-done | bytes 229408 | tf_op jit(solution)/shard_map/ppermute | solution.py:404
  32.4 0.0 collective-permute-done.1.xb
  32.4 1.7 %collective-permute-done.2.za = bf16[28,32,128]{2,1,0:T(8,128)(2,1)S(1)} collective-permute-done((bf16[28,32,128]{2,1,0:T(8,128)(2,1)S(1)}, bf16[28,32,128]{2,1,0:T(8,128)(2,1)S(1)}, u32[]{:S(2)}, u32[]{:S(2)}) %collective-permute-start.2) | collective-permute-done | bytes 229408 | tf_op jit(solution)/shard_map/ppermute | solution.py:404
  34.1 0.0 collective-permute-done.3.zb
  34.1 0.0 all-to-all-done._
  34.1 0.0 copy-done
  34.1 3.3 %relay.1 = (bf16[14,32,512]{2,1,0:T(8,128)(2,1)}, bf16[14,32,512]{2,1,0:T(8,128)(2,1)}, bf16[60,32,128]{2,1,0:T(8,128)(2,1)}, bf16[60,32,128]{2,1,0:T(8,128)(2,1)}, bf16[16,9,32,128]{3,2,1,0:T(8,128)(2,1)S(1)}) custom-call(f32[14,32,512]{2,1,0:T(8,128)} %get-tuple-element.36.hx1, ...), custom_call_target="tpu_custom_call", output_to_operand_aliasing={{4}: (9, {})} | custom-call | flops 917504 | bytes 3211264 | tf_op jit(solution)/shard_map/relay/pallas_call | solution.py:160
  37.4 0.1 collective-permute-start.6
  37.5 1.4 %collective-permute-start.10 = (bf16[60,32,128]{2,1,0:T(8,128)(2,1)}, bf16[60,32,128]{2,1,0:T(8,128)(2,1)S(1)}, u32[]{:S(2)}, u32[]{:S(2)}) collective-permute-start(bf16[60,32,128]{2,1,0:T(8,128)(2,1)} %get-tuple-element.53), channel_id=1, source_target_pairs={{0,1},{1,2},{2,3},{3,0},{4,5},{5,6},{6,7},{7,4},{8,9},{9,10},{10,1... | collective-permute-start | bytes 1474568 | tf_op jit(solution)/shard_map/ppermute | solution.py:404
  38.9 1.9 %collective-permute-start.11 = (bf16[60,32,128]{2,1,0:T(8,128)(2,1)}, bf16[60,32,128]{2,1,0:T(8,128)(2,1)S(1)}, u32[]{:S(2)}, u32[]{:S(2)}) collective-permute-start(bf16[60,32,128]{2,1,0:T(8,128)(2,1)} %get-tuple-element.54), channel_id=1, source_target_pairs={{0,3},{1,0},{2,1},{3,2},{4,7},{5,4},{6,5},{7,6},{8,11},{9,8},{10,9... | collective-permute-start | bytes 1474568 | tf_op jit(solution)/shard_map/ppermute | solution.py:404
  40.8 0.1 collective-permute-start.4
  40.9 3.1 %collective-permute-start.5 = (bf16[14,32,512]{2,1,0:T(8,128)(2,1)}, bf16[14,32,512]{2,1,0:T(8,128)(2,1)S(1)}, u32[]{:S(2)}, u32[]{:S(2)}) collective-permute-start(bf16[14,32,512]{2,1,0:T(8,128)(2,1)} %get-tuple-element.45), channel_id=1, source_target_pairs={{0,12},{1,13},{2,14},{3,15},{4,0},{5,1},{6,2},{7,3},{8,4},{9,5},{1... | collective-permute-start | bytes 1376264 | tf_op jit(solution)/shard_map/ppermute | solution.py:404
  44.0 0.0 collective-permute-done.6.other
  44.0 3.5 %place.1 = (bf16[4,28,32,128]{3,2,1,0:T(8,128)(2,1)}, f32[28,32,128]{2,1,0:T(8,128)S(1)}, s32[2,128]{1,0:T(2,128)S(1)}) custom-call(bf16[16,9,32,128]{3,2,1,0:T(8,128)(2,1)S(1)} %get-tuple-element.46.mine, bf16[16,9,32,128]{3,2,1,0:T(8,128)(2,1)S(1)} %collective-permute-done.6.other), custom_call_target="tpu_custom_call" | custom-call | flops 9437184 | bytes 4718592 | tf_op jit(solution)/shard_map/place/pallas_call | solution.py:279
  47.6 4.5 %all-to-all-start.1 = ((bf16[4,28,32,128]{3,2,1,0:T(8,128)(2,1)}), bf16[4,28,32,128]{3,2,1,0:T(8,128)(2,1)S(1)}, u32[]{:S(2)}, u32[]{:S(2)}) async-start(bf16[4,28,32,128]{3,2,1,0:T(8,128)(2,1)} %get-tuple-element.60), calls=%async_computation.1 | async-start | bytes 1835008 | tf_op jit(solution)/shard_map/all_to_all | solution.py:433
  52.0 0.5 collective-permute-done.10.r1
  52.5 0.0 collective-permute-done.11.r2
  52.5 1.3 %sum_z.1 = (f32[14,32,128]{2,1,0:T(8,128)S(1)}, f32[14,32,128]{2,1,0:T(8,128)S(1)}, f32[14,32,128]{2,1,0:T(8,128)S(1)}, f32[14,32,128]{2,1,0:T(8,128)S(1)}, bf16[64,256]{1,0:T(8,128)(2,1)S(1)}) custom-call(f32[56,32,128]{2,1,0:T(8,128)} %get-tuple-element.52.held, bf16[60,32,128]{2,1,0:T(8,128)(2,1)S(1)} %collective-permute-done.10.r1, ...), custom_call_target="tpu_custom_call" | custom-call | flops 688128 | bytes 3211264 | tf_op jit(solution)/shard_map/sum_z/pallas_call | solution.py:197
  53.8 0.0 copy-start.3
  53.9 0.6 copy-done.3
  54.5 0.1 collective-permute-start.12
  54.6 2.9 %collective-permute-start.13 = (f32[14,32,128]{2,1,0:T(8,128)S(1)}, f32[14,32,128]{2,1,0:T(8,128)S(1)}, u32[]{:S(2)}, u32[]{:S(2)}) collective-permute-start(f32[14,32,128]{2,1,0:T(8,128)S(1)} %get-tuple-element.57), channel_id=1, source_target_pairs={{0,8},{1,9},{2,10},{3,11},{4,12},{5,13},{6,14},{7,15},{8,0},{9,1},... | collective-permute-start | bytes 688136 | tf_op jit(solution)/shard_map/ppermute | solution.py:404
  57.5 1.4 %collective-permute-start.14 = (f32[14,32,128]{2,1,0:T(8,128)S(1)}, f32[14,32,128]{2,1,0:T(8,128)S(1)}, u32[]{:S(2)}, u32[]{:S(2)}) collective-permute-start(f32[14,32,128]{2,1,0:T(8,128)S(1)} %get-tuple-element.58), channel_id=1, source_target_pairs={{0,12},{1,13},{2,14},{3,15},{4,0},{5,1},{6,2},{7,3},{8,4},{9,5},{1... | collective-permute-start | bytes 688136 | tf_op jit(solution)/shard_map/ppermute | solution.py:404
  58.9 0.0 collective-permute-done.4.r1
  58.9 0.0 collective-permute-done.5.r2
  58.9 1.4 %sum_x.1 = (f32[14,32,128]{2,1,0:T(8,128)S(1)}, f32[14,32,128]{2,1,0:T(8,128)S(1)}, f32[14,32,128]{2,1,0:T(8,128)S(1)}, f32[14,32,128]{2,1,0:T(8,128)S(1)}) custom-call(f32[14,32,512]{2,1,0:T(8,128)} %get-tuple-element.35.held, bf16[14,32,512]{2,1,0:T(8,128)(2,1)S(1)} %collective-permute-done.4.r1, bf16[14,32,512]{2,1,0:T(8,128)(2,1)S(1)} %collective-permute-done.5.r2, ...), custom_call_target="tpu_custom_call" | custom-call | flops 688128 | bytes 3211264 | tf_op jit(solution)/shard_map/sum_x/pallas_call | solution.py:197
  60.3 0.6 collective-permute-start.7
  60.9 3.9 %collective-permute-start.8 = (f32[14,32,128]{2,1,0:T(8,128)S(1)}, f32[14,32,128]{2,1,0:T(8,128)S(1)}, u32[]{:S(2)}, u32[]{:S(2)}) collective-permute-start(f32[14,32,128]{2,1,0:T(8,128)S(1)} %get-tuple-element.50), channel_id=1, source_target_pairs={{0,2},{1,3},{2,0},{3,1},{4,6},{5,7},{6,4},{7,5},{8,10},{9,11},{10,... | collective-permute-start | bytes 688136 | tf_op jit(solution)/shard_map/ppermute | solution.py:404
  64.8 3.0 %collective-permute-done.12.refs_5_ = f32[14,32,128]{2,1,0:T(8,128)S(1)} collective-permute-done((f32[14,32,128]{2,1,0:T(8,128)S(1)}, f32[14,32,128]{2,1,0:T(8,128)S(1)}, u32[]{:S(2)}, u32[]{:S(2)}) %collective-permute-start.12) | collective-permute-done | bytes 229408 | tf_op jit(solution)/shard_map/ppermute | solution.py:404
  67.7 2.6 %collective-permute-start.9 = (f32[14,32,128]{2,1,0:T(8,128)S(1)}, f32[14,32,128]{2,1,0:T(8,128)S(1)}, u32[]{:S(2)}, u32[]{:S(2)}) collective-permute-start(f32[14,32,128]{2,1,0:T(8,128)S(1)} %get-tuple-element.51), channel_id=1, source_target_pairs={{0,3},{1,0},{2,1},{3,2},{4,7},{5,4},{6,5},{7,6},{8,11},{9,8},{10,9... | collective-permute-start | bytes 688136 | tf_op jit(solution)/shard_map/ppermute | solution.py:404
  70.4 0.0 collective-permute-done.13.refs_6_
  70.4 0.0 collective-permute-done.14.refs_7_
  70.4 0.0 collective-permute-done.7.refs_1_
  70.4 3.3 %collective-permute-done.8.refs_2_ = f32[14,32,128]{2,1,0:T(8,128)S(1)} collective-permute-done((f32[14,32,128]{2,1,0:T(8,128)S(1)}, f32[14,32,128]{2,1,0:T(8,128)S(1)}, u32[]{:S(2)}, u32[]{:S(2)}) %collective-permute-start.8) | collective-permute-done | bytes 229408 | tf_op jit(solution)/shard_map/ppermute | solution.py:404
  73.7 0.3 collective-permute-done.9.refs_3_
  73.9 0.0 all-to-all-done.1.refs_9_
  73.9 0.0 copy-start.1
  73.9 0.0 copy-start.2
  73.9 0.0 copy-start.4
  73.9 0.0 copy-start.5
  73.9 0.4 finish.1
  74.3 15.1 %all_to_all.15.arrived = bf16[16,2,2,32,128]{4,3,2,1,0:T(8,128)(2,1)S(1)} all-to-all(bf16[16,2,2,32,128]{4,3,2,1,0:T(8,128)(2,1)S(1)} %finish.1), channel_id=1, replica_groups=mesh['frow'=8,'fcol'=16] {'fcol'}, dimensions={0} | all-to-all | bytes 1048576 | tf_op jit(solution)/shard_map/all_to_all | solution.py:446
  89.4 0.0 copy-done.1
  89.4 0.0 copy-done.2
  89.4 0.0 copy-done.4
  89.4 0.0 copy-done.5
  89.4 1.2 %tail.1 = (bf16[224,512]{1,0:T(8,128)(2,1)}, f32[96,224]{1,0:T(8,128)}, f32[64,96]{1,0:T(8,128)}, bf16[32,512]{1,0:T(8,128)(2,1)}) custom-call(bf16[16,2,2,32,128]{4,3,2,1,0:T(8,128)(2,1)S(1)} %all_to_all.15.arrived, bf16[96,512]{1,0:T(8,128)(2,1)S(1)} %bitcast.11, bf16[64,256]{1,0:T(8,128)(2,1)S(1)} %bitcast.10, bf16[64,256]{1,0:T(8,128)(2,1)S(1)} %copy-done.4, ...), custom_call_target="tpu_custom_call" | custom-call | flops 75497472 | bytes 786432 | tf_op jit(solution)/shard_map/tail/pallas_call | solution.py:388
Async XLA Ops:
  3.2 30.9 %all-to-all-start = ((bf16[16,9,32,128]{3,2,1,0:T(8,128)(2,1)}), bf16[16,9,32,128]{3,2,1,0:T(8,128)(2,1)S(1)}, u32[]{:S(2)}, u32[]{:S(2)}) async-start(bf16[16,9,32,128]{3,2,1,0:T(8,128)(2,1)} %pack.1), calls=%async_computation | async-start | bytes 2359296 | tf_op jit(solution)/shard_map/all_to_all | solution.py:422
  11.2 22.9 %copy-start = (bf16[256,64]{0,1:T(8,128)(2,1)S(1)}, bf16[256,64]{0,1:T(8,128)(2,1)}, u32[]{:S(2)}) copy-start(bf16[256,64]{0,1:T(8,128)(2,1)} %param.15) | copy-start | bytes 98308
  22.3 10.1 %collective-permute-start = (bf16[7,32,512]{2,1,0:T(8,128)(2,1)S(1)}, bf16[7,32,512]{2,1,0:T(8,128)(2,1)S(1)}, u32[]{:S(2)}, u32[]{:S(2)}) collective-permute-start(bf16[7,32,512]{2,1,0:T(8,128)(2,1)S(1)} %get-tuple-element.38), channel_id=1, source_target_pairs={{0,4},{1,5},{2,6},{3,7},{4,8},{5,9},{6,10},{7,11},{8,12},{9,13},{1... | collective-permute-start | bytes 688136 | tf_op jit(solution)/shard_map/ppermute | solution.py:404
  24.3 8.1 %collective-permute-start.1 = (bf16[7,32,512]{2,1,0:T(8,128)(2,1)S(1)}, bf16[7,32,512]{2,1,0:T(8,128)(2,1)S(1)}, u32[]{:S(2)}, u32[]{:S(2)}) collective-permute-start(bf16[7,32,512]{2,1,0:T(8,128)(2,1)S(1)} %get-tuple-element.39), channel_id=1, source_target_pairs={{0,12},{1,13},{2,14},{3,15},{4,0},{5,1},{6,2},{7,3},{8,4},{9,5},{1... | collective-permute-start | bytes 688136 | tf_op jit(solution)/shard_map/ppermute | solution.py:404
  25.6 8.5 %collective-permute-start.2 = (bf16[28,32,128]{2,1,0:T(8,128)(2,1)S(1)}, bf16[28,32,128]{2,1,0:T(8,128)(2,1)S(1)}, u32[]{:S(2)}, u32[]{:S(2)}) collective-permute-start(bf16[28,32,128]{2,1,0:T(8,128)(2,1)S(1)} %get-tuple-element.42), channel_id=1, source_target_pairs={{0,1},{1,2},{2,3},{3,0},{4,5},{5,6},{6,7},{7,4},{8,9},{9,10},{10,1... | collective-permute-start | bytes 688136 | tf_op jit(solution)/shard_map/ppermute | solution.py:404
  27.5 6.5 %collective-permute-start.3 = (bf16[28,32,128]{2,1,0:T(8,128)(2,1)S(1)}, bf16[28,32,128]{2,1,0:T(8,128)(2,1)S(1)}, u32[]{:S(2)}, u32[]{:S(2)}) collective-permute-start(bf16[28,32,128]{2,1,0:T(8,128)(2,1)S(1)} %get-tuple-element.43), channel_id=1, source_target_pairs={{0,3},{1,0},{2,1},{3,2},{4,7},{5,4},{6,5},{7,6},{8,11},{9,8},{10,9... | collective-permute-start | bytes 688136 | tf_op jit(solution)/shard_map/ppermute | solution.py:404
  37.4 6.6 %collective-permute-start.6 = (bf16[16,9,32,128]{3,2,1,0:T(8,128)(2,1)S(1)}, bf16[16,9,32,128]{3,2,1,0:T(8,128)(2,1)S(1)}, u32[]{:S(2)}, u32[]{:S(2)}) collective-permute-start(bf16[16,9,32,128]{3,2,1,0:T(8,128)(2,1)S(1)} %get-tuple-element.46.mine), channel_id=1, source_target_pairs={{0,16},{16,0},{32,48},{48,32},{64,80},{80,64},{96,112},{112,96},{1... | collective-permute-start | bytes 3538952 | tf_op jit(solution)/shard_map/ppermute | solution.py:404
  37.5 15.1 %collective-permute-start.10 = (bf16[60,32,128]{2,1,0:T(8,128)(2,1)}, bf16[60,32,128]{2,1,0:T(8,128)(2,1)S(1)}, u32[]{:S(2)}, u32[]{:S(2)}) collective-permute-start(bf16[60,32,128]{2,1,0:T(8,128)(2,1)} %get-tuple-element.53), channel_id=1, source_target_pairs={{0,1},{1,2},{2,3},{3,0},{4,5},{5,6},{6,7},{7,4},{8,9},{9,10},{10,1... | collective-permute-start | bytes 1474568 | tf_op jit(solution)/shard_map/ppermute | solution.py:404
  38.9 13.6 %collective-permute-start.11 = (bf16[60,32,128]{2,1,0:T(8,128)(2,1)}, bf16[60,32,128]{2,1,0:T(8,128)(2,1)S(1)}, u32[]{:S(2)}, u32[]{:S(2)}) collective-permute-start(bf16[60,32,128]{2,1,0:T(8,128)(2,1)} %get-tuple-element.54), channel_id=1, source_target_pairs={{0,3},{1,0},{2,1},{3,2},{4,7},{5,4},{6,5},{7,6},{8,11},{9,8},{10,9... | collective-permute-start | bytes 1474568 | tf_op jit(solution)/shard_map/ppermute | solution.py:404
  40.8 18.2 %collective-permute-start.4 = (bf16[14,32,512]{2,1,0:T(8,128)(2,1)}, bf16[14,32,512]{2,1,0:T(8,128)(2,1)S(1)}, u32[]{:S(2)}, u32[]{:S(2)}) collective-permute-start(bf16[14,32,512]{2,1,0:T(8,128)(2,1)} %get-tuple-element.44), channel_id=1, source_target_pairs={{0,4},{1,5},{2,6},{3,7},{4,8},{5,9},{6,10},{7,11},{8,12},{9,13},{1... | collective-permute-start | bytes 1376264 | tf_op jit(solution)/shard_map/ppermute | solution.py:404
  40.9 18.0 %collective-permute-start.5 = (bf16[14,32,512]{2,1,0:T(8,128)(2,1)}, bf16[14,32,512]{2,1,0:T(8,128)(2,1)S(1)}, u32[]{:S(2)}, u32[]{:S(2)}) collective-permute-start(bf16[14,32,512]{2,1,0:T(8,128)(2,1)} %get-tuple-element.45), channel_id=1, source_target_pairs={{0,12},{1,13},{2,14},{3,15},{4,0},{5,1},{6,2},{7,3},{8,4},{9,5},{1... | collective-permute-start | bytes 1376264 | tf_op jit(solution)/shard_map/ppermute | solution.py:404
  47.6 26.4 %all-to-all-start.1 = ((bf16[4,28,32,128]{3,2,1,0:T(8,128)(2,1)}), bf16[4,28,32,128]{3,2,1,0:T(8,128)(2,1)S(1)}, u32[]{:S(2)}, u32[]{:S(2)}) async-start(bf16[4,28,32,128]{3,2,1,0:T(8,128)(2,1)} %get-tuple-element.60), calls=%async_computation.1 | async-start | bytes 1835008 | tf_op jit(solution)/shard_map/all_to_all | solution.py:433
  53.8 0.6 copy-start.3
  54.5 13.3 %collective-permute-start.12 = (f32[14,32,128]{2,1,0:T(8,128)S(1)}, f32[14,32,128]{2,1,0:T(8,128)S(1)}, u32[]{:S(2)}, u32[]{:S(2)}) collective-permute-start(f32[14,32,128]{2,1,0:T(8,128)S(1)} %get-tuple-element.56), channel_id=1, source_target_pairs={{0,4},{1,5},{2,6},{3,7},{4,8},{5,9},{6,10},{7,11},{8,12},{9,13},{1... | collective-permute-start | bytes 688136 | tf_op jit(solution)/shard_map/ppermute | solution.py:404
  54.6 15.8 %collective-permute-start.13 = (f32[14,32,128]{2,1,0:T(8,128)S(1)}, f32[14,32,128]{2,1,0:T(8,128)S(1)}, u32[]{:S(2)}, u32[]{:S(2)}) collective-permute-start(f32[14,32,128]{2,1,0:T(8,128)S(1)} %get-tuple-element.57), channel_id=1, source_target_pairs={{0,8},{1,9},{2,10},{3,11},{4,12},{5,13},{6,14},{7,15},{8,0},{9,1},... | collective-permute-start | bytes 688136 | tf_op jit(solution)/shard_map/ppermute | solution.py:404
  57.5 12.9 %collective-permute-start.14 = (f32[14,32,128]{2,1,0:T(8,128)S(1)}, f32[14,32,128]{2,1,0:T(8,128)S(1)}, u32[]{:S(2)}, u32[]{:S(2)}) collective-permute-start(f32[14,32,128]{2,1,0:T(8,128)S(1)} %get-tuple-element.58), channel_id=1, source_target_pairs={{0,12},{1,13},{2,14},{3,15},{4,0},{5,1},{6,2},{7,3},{8,4},{9,5},{1... | collective-permute-start | bytes 688136 | tf_op jit(solution)/shard_map/ppermute | solution.py:404
  60.3 10.1 %collective-permute-start.7 = (f32[14,32,128]{2,1,0:T(8,128)S(1)}, f32[14,32,128]{2,1,0:T(8,128)S(1)}, u32[]{:S(2)}, u32[]{:S(2)}) collective-permute-start(f32[14,32,128]{2,1,0:T(8,128)S(1)} %get-tuple-element.49), channel_id=1, source_target_pairs={{0,1},{1,2},{2,3},{3,0},{4,5},{5,6},{6,7},{7,4},{8,9},{9,10},{10,1... | collective-permute-start | bytes 688136 | tf_op jit(solution)/shard_map/ppermute | solution.py:404
  60.9 12.7 %collective-permute-start.8 = (f32[14,32,128]{2,1,0:T(8,128)S(1)}, f32[14,32,128]{2,1,0:T(8,128)S(1)}, u32[]{:S(2)}, u32[]{:S(2)}) collective-permute-start(f32[14,32,128]{2,1,0:T(8,128)S(1)} %get-tuple-element.50), channel_id=1, source_target_pairs={{0,2},{1,3},{2,0},{3,1},{4,6},{5,7},{6,4},{7,5},{8,10},{9,11},{10,... | collective-permute-start | bytes 688136 | tf_op jit(solution)/shard_map/ppermute | solution.py:404
  67.7 6.2 %collective-permute-start.9 = (f32[14,32,128]{2,1,0:T(8,128)S(1)}, f32[14,32,128]{2,1,0:T(8,128)S(1)}, u32[]{:S(2)}, u32[]{:S(2)}) collective-permute-start(f32[14,32,128]{2,1,0:T(8,128)S(1)} %get-tuple-element.51), channel_id=1, source_target_pairs={{0,3},{1,0},{2,1},{3,2},{4,7},{5,4},{6,5},{7,6},{8,11},{9,8},{10,9... | collective-permute-start | bytes 688136 | tf_op jit(solution)/shard_map/ppermute | solution.py:404
  73.9 15.5 %copy-start.1 = (bf16[256,64]{0,1:T(8,128)(2,1)S(1)}, bf16[256,64]{0,1:T(8,128)(2,1)}, u32[]{:S(2)}) copy-start(bf16[256,64]{0,1:T(8,128)(2,1)} %param.15) | copy-start | bytes 98308
  73.9 15.5 %copy-start.2 = (bf16[512,96]{0,1:T(8,128)(2,1)S(1)}, bf16[512,96]{0,1:T(8,128)(2,1)}, u32[]{:S(2)}) copy-start(bf16[512,96]{0,1:T(8,128)(2,1)} %param.14) | copy-start | bytes 294916
  73.9 15.5 %copy-start.4 = (bf16[64,256]{1,0:T(8,128)(2,1)S(1)}, bf16[64,256]{1,0:T(8,128)(2,1)}, u32[]{:S(2)}) copy-start(bf16[64,256]{1,0:T(8,128)(2,1)} %copy-done.3) | copy-start | bytes 98308
  73.9 15.5 %copy-start.5 = (s32[1,32]{1,0:T(1,128)S(1)}, s32[1,32]{1,0:T(1,128)}, u32[]{:S(2)}) copy-start(s32[1,32]{1,0:T(1,128)} %piv_parent.1) | copy-start | bytes 388

commit v3 on v2

--- a/solution.py
+++ b/solution.py
@@ -46,8 +46,8 @@
     return copies
 
 
-def front_kernel(a_hbm, b_hbm, x0, x1, x3, xa, xb, z0, z1, z3, za, zb,
-                 a, b, turned, value, sx0, sx1, sx3, sz0, sz1, sz3, sems, out_sems, *, cuts):
+def front_kernel(a_hbm, b_hbm, x0, x1, x3, u1, u3, xa, xb, z0, z1, z3, w1, w3, za, zb,
+                 a, b, turned, value, sx0, sx1, sx3, su1, su3, sz0, sz1, sz3, sw1, sw3, sems, out_sems, *, cuts):
     x, z = place_in_mesh()[:2]
     half = a.shape[0] // 2
     spans = list(zip(cuts[:-1], cuts[1:]))
@@ -80,20 +80,24 @@
         product = product.reshape(hi - lo, NX, UNIT, NZ * COLS)
         if hi <= half:
             value[: hi - lo] = product
-            for s, staged, out in ((0, sx0, x0), (1, sx1, x1), (3, sx3, x3)):
-                staged[lo:hi] = value[: hi - lo, (x + s) % NX]
-                store(staged, out, pl.ds(lo, hi - lo))
-            out, at = (xa, lo) if hi <= half // 2 else (xb, lo - half // 2)
-            out[at : at + hi - lo] = value[: hi - lo, (x + 2) % NX].astype(BF16)
+            first = hi <= half // 2
+            at = lo if first else lo - half // 2
+            one, three, two = ((sx1, x1), (su3, u3), xa) if first else ((su1, u1), (sx3, x3), xb)
+            for s, (staged, out), start in ((0, (sx0, x0), lo), (1, one, at), (3, three, at)):
+                staged[start : start + hi - lo] = value[: hi - lo, (x + s) % NX].astype(staged.dtype)
+                store(staged, out, pl.ds(start, hi - lo))
+            two[at : at + hi - lo] = value[: hi - lo, (x + 2) % NX].astype(BF16)
         else:
             for jr in range(NX):
                 at = jr * half + lo - half
                 piece = product[:, jr]
-                for s, staged, out in ((0, sz0, z0), (1, sz1, z1), (3, sz3, z3)):
-                    staged[at : at + hi - lo] = piece[..., s * COLS : (s + 1) * COLS]
-                    store(staged, out, pl.ds(at, hi - lo))
-                out, at = (za, at) if jr < NX // 2 else (zb, at - NX // 2 * half)
-                out[at : at + hi - lo] = piece[..., 2 * COLS : 3 * COLS].astype(BF16)
+                first = jr < NX // 2
+                near = at if first else at - NX // 2 * half
+                one, three, two = ((sz1, z1), (sw3, w3), za) if first else ((sw1, w1), (sz3, z3), zb)
+                for s, (staged, out), start in ((0, (sz0, z0), at), (1, one, near), (3, three, near)):
+                    staged[start : start + hi - lo] = piece[..., s * COLS : (s + 1) * COLS].astype(staged.dtype)
+                    store(staged, out, pl.ds(start, hi - lo))
+                two[near : near + hi - lo] = piece[..., 2 * COLS : 3 * COLS].astype(BF16)
     for copy in stores:
         copy.wait()
 
@@ -111,20 +115,21 @@
     half = blocks // 2
     step = half // 2
     cuts = (0, step // 2, *range(step, blocks + 1, step))
-    kinds = ((1, F32), (1, F32), (1, F32), (2, BF16), (2, BF16))
+    kinds = ((1, F32), (2, F32), (2, F32), (2, BF16), (2, BF16), (2, BF16), (2, BF16))
     shapes = [((half // n, UNIT, cols), t) for n, t in kinds]
     shapes += [((NX * half // n, UNIT, COLS), t) for n, t in kinds]
+    later = [i % 7 < 5 for i in range(14)]
     return pl.pallas_call(
         functools.partial(front_kernel, cuts=cuts),
-        out_shape=[(pltpu.HBM if s[1] == F32 else jax.ShapeDtypeStruct)(*s) for s in shapes],
+        out_shape=[(pltpu.HBM if l else jax.ShapeDtypeStruct)(*s) for s, l in zip(shapes, later)],
         in_specs=[REMAIN, REMAIN],
-        out_specs=([REMAIN] * 3 + [LOCAL] * 2) * 2,
+        out_specs=[REMAIN if l else LOCAL for l in later],
         scratch_shapes=[
             pltpu.VMEM((blocks, BLK, depth), BF16),
             pltpu.VMEM(test.shape, BF16),
             pltpu.VMEM(test.shape, BF16),
             pltpu.VMEM((step, NX, UNIT, cols), F32),
-            *[pltpu.VMEM(*shape) for shape in shapes if shape[1] == F32],
+            *[pltpu.VMEM(*s) for s, l in zip(shapes, later) if l],
             pltpu.SemaphoreType.DMA((len(cuts),)),
             pltpu.SemaphoreType.DMA((3 * (len(cuts) - 1 + 2 * NX),)),
         ],
@@ -136,84 +141,90 @@
     )(remote(front.reshape(blocks, BLK, depth)), remote(test))
 
 
-def relay_kernel(hx1, hx3, xa, xb, hz1, hz3, za, zb, inverse, _, x_up, x_down, z_up, z_down, __,
-                 x1, x3, z1, z3, sems):
-    copies = fetch([(hx1, x1), (hx3, x3), (hz1, z1), (hz3, z3)], sems)
-    for copy, own, part, out, at in zip(
-        copies, (x1, x3, z1, z3), (xa, xb, za, zb), (x_up, x_down, z_up, z_down),
-        (0, xa.shape[0], 0, za.shape[0]),
-    ):
-        copy.wait()
-        half = part.shape[0]
-        rest = half - at
-        out[at : at + half] = (own[at : at + half] + part[...].astype(F32)).astype(BF16)
-        out[rest : rest + half] = own[rest : rest + half].astype(BF16)
+def relay_kernel(hx1, hx3, hu1, hu3, xa, xb, hz1, hz3, hw1, hw3, za, zb, inverse, _,
+                 x_up, x_down, z_up, z_down, __, x1, x3, z1, z3, sems):
+    nx, nz = x1.shape[0], z1.shape[0]
+    copies = fetch(
+        [
+            (hx1, x1), (hx3, x3), (hz1, z1), (hz3, z3),
+            (hu1, x_up.at[nx : 2 * nx]), (hu3, x_down.at[:nx]),
+            (hw1, z_up.at[nz : 2 * nz]), (hw3, z_down.at[:nz]),
+        ],
+        sems,
+    )
     for out in (z_up, z_down):
         for i, (rows, columns) in enumerate(inverse_tiles(inverse.shape)):
-            out[z1.shape[0] + i] = inverse[rows, columns]
-
-
-def relay(x1, x3, xa, xb, z1, z3, za, zb, inverse, mine):
+            out[2 * nz + i] = inverse[rows, columns]
+    for copy, own, part, out, at in zip(
+        copies, (x1, x3, z1, z3), (xa, xb, za, zb), (x_up, x_down, z_up, z_down), (0, nx, 0, nz)
+    ):
+        copy.wait()
+        out[at : at + own.shape[0]] = (own[...] + part[...].astype(F32)).astype(BF16)
+    for copy in copies[4:]:
+        copy.wait()
+
+
+def relay(x_parts, xa, xb, z_parts, za, zb, inverse, mine):
     extra = len(inverse_tiles(inverse.shape))
-    z_shape = (z1.shape[0] + extra, *z1.shape[1:])
-    shapes = [x1.shape, x1.shape, z_shape, z_shape, mine.shape]
+    nx, nz = xa.shape[0], za.shape[0]
+    x_shape, z_shape = (2 * nx, *xa.shape[1:]), (2 * nz + extra, *za.shape[1:])
+    shapes = [x_shape, x_shape, z_shape, z_shape, mine.shape]
     return pl.pallas_call(
         relay_kernel,
         out_shape=[jax.ShapeDtypeStruct(shape, BF16) for shape in shapes],
-        in_specs=([REMAIN] * 2 + [LOCAL] * 2) * 2 + [LOCAL] * 2,
+        in_specs=([REMAIN] * 4 + [LOCAL] * 2) * 2 + [LOCAL] * 2,
         out_specs=[LOCAL] * 5,
         scratch_shapes=[
-            *[pltpu.VMEM(v.shape, F32) for v in (x1, x3, z1, z3)],
-            pltpu.SemaphoreType.DMA((4,)),
-        ],
-        input_output_aliases={9: 4},
+            *[pltpu.VMEM(v.shape, F32) for v in (xa, xb, za, zb)],
+            pltpu.SemaphoreType.DMA((8,)),
+        ],
+        input_output_aliases={13: 4},
         compiler_params=params(8),
-        cost_estimate=cost(4 * x1.size, 14 * x1.size),
+        cost_estimate=cost(4 * xa.size, 28 * xa.size),
         name="relay",
-    )(remote(x1), remote(x3), xa, xb, remote(z1), remote(z3), za, zb, inverse, mine)
+    )(*map(remote, x_parts), xa, xb, *map(remote, z_parts), za, zb, inverse, mine)
 
 
 def sum_x_kernel(held, r1, r2, token, to1, to2, to3, keep, own, sems):
-    fetch([(held, own)], sems)[0].wait()
-    for s, out in ((1, to1), (2, to2), (3, to3), (0, keep)):
-        at = (slice(None), slice(None), slice(s * COLS, (s + 1) * COLS))
-        out[...] = own[at] + r1[at].astype(F32) + r2[at].astype(F32)
+    outs = ((1, to1), (2, to2), (3, to3), (0, keep))
+    spans = [(slice(None), slice(None), slice(s * COLS, (s + 1) * COLS)) for s, _ in outs]
+    copies = fetch([(held.at[at], own.at[at]) for at in spans], sems)
+    for at, copy, (_, out) in zip(spans, copies, outs):
+        copy.wait()
+        out[...] = (own[at] + r1[at].astype(F32) + r2[at].astype(F32)).astype(out.dtype)
 
 
 def sum_z_kernel(held, r1, r2, token, to1, to2, to3, keep, inverse, own, sems):
-    fetch([(held, own)], sems)[0].wait()
     x, z = place_in_mesh()[:2]
     half = keep.shape[0]
-    for s, out in ((1, to1), (2, to2), (3, to3), (0, keep)):
-        at = pl.ds((x + s) % NX * half, half)
-        out[...] = own[at] + r1[at].astype(F32) + r2[at].astype(F32)
+    outs = ((1, to1), (2, to2), (3, to3), (0, keep))
+    spans = [pl.ds((x + s) % NX * half, half) for s, _ in outs]
+    copies = fetch([(held.at[at], own.at[at]) for at in spans], sems)
+    for at, copy, (_, out) in zip(spans, copies, outs):
+        copy.wait()
+        out[...] = (own[at] + r1[at].astype(F32) + r2[at].astype(F32)).astype(out.dtype)
     for i, (rows, columns) in enumerate(inverse_tiles(inverse.shape)):
         inverse[rows, columns] = lax.select(z % 2 == 0, r2[NX * half + i], r1[NX * half + i])
 
 
 def partial_sum(kernel, own, arrived, token, half, extra):
-    piece = jax.ShapeDtypeStruct((half, UNIT, COLS), F32)
-    outs = [piece] * 4 + extra
+    outs = [jax.ShapeDtypeStruct((half, UNIT, COLS), t) for t in (F32, BF16, F32, F32)] + extra
     return pl.pallas_call(
         kernel,
         out_shape=outs,
         in_specs=[REMAIN] + [LOCAL] * 2 + [ANY],
         out_specs=[LOCAL] * len(outs),
-        scratch_shapes=[pltpu.VMEM(own.shape, F32), pltpu.SemaphoreType.DMA((1,))],
+        scratch_shapes=[pltpu.VMEM(own.shape, F32), pltpu.SemaphoreType.DMA((4,))],
         compiler_params=params(8),
         cost_estimate=cost(3 * own.size, 14 * own.size),
         name=kernel.__name__[:5],
     )(remote(own), *arrived, token)
 
 
-def pack_kernel(child, group_hbm, block_hbm, pivots_hbm, out, group, block, pivots, facts, sems, *, blocks):
+def pack_kernel(child, group_hbm, block_hbm, pivots_hbm, out, group, block, pivots, facts, local, sems, *, blocks):
     copies = fetch(
         [(group_hbm, group), (block_hbm, block), (pivots_hbm, pivots)]
-        + [
-            (child.at[:, x * UNIT : (x + 1) * UNIT, z * COLS : (z + 1) * COLS], out.at[x * NZ + z, :CBD])
-            for x in range(NX)
-            for z in range(NZ)
-        ],
+        + [(child.at[i : i + 2], local.at[i : i + 2]) for i in range(0, CBD, 2)],
         sems,
     )
     facts[...] = jnp.zeros_like(facts)
@@ -224,11 +235,16 @@
     told = facts[...].astype(BF16)
     for i in range(out.shape[0]):
         out[i, CBD] = told
-    for copy in copies[3:]:
-        copy.wait()
+    for i in range(0, CBD, 2):
+        copies[3 + i // 2].wait()
+        for x in range(NX):
+            for z in range(NZ):
+                part = local[i : i + 2, x * UNIT : (x + 1) * UNIT, z * COLS : (z + 1) * COLS]
+                out[x * NZ + z, i : i + 2] = part
 
 
 def pack(child, group, block, pivots, blocks):
+    child = remote(child.reshape(CBD, BLK, child.shape[1]))
     return pl.pallas_call(
         functools.partial(pack_kernel, blocks=blocks),
         out_shape=jax.ShapeDtypeStruct((NX * NZ, CBD + 1, UNIT, COLS), BF16),
@@ -237,17 +253,18 @@
         scratch_shapes=[
             *[pltpu.VMEM(v.shape, v.dtype) for v in (group, block, pivots)],
             pltpu.VMEM((UNIT, COLS), F32),
-            pltpu.SemaphoreType.DMA((NX * NZ + 3,)),
+            pltpu.VMEM(child.shape, BF16),
+            pltpu.SemaphoreType.DMA((CBD // 2 + 3,)),
         ],
         compiler_params=params(60),
         cost_estimate=cost(0, 4 * child.size),
         name="pack",
-    )(child.reshape(CBD, BLK, child.shape[1]), group, block, pivots)
+    )(child, group, block, pivots)
 
 
 def place_kernel(mine, other, out, own, pivots, total, facts, told, slots, sems):
     pos = place_in_mesh()
-    blocks = own.shape[0]
+    blocks = out.shape[1]
     sources = mine.shape[0]
     for t, ref in ((0, mine), (1, other)):
         told[t * sources : (t + 1) * sources] = ref[:, CBD].astype(F32)
@@ -269,8 +286,10 @@
             return _
 
         lax.fori_loop(0, sources, body, 0)
-    own[...] = total[pl.ds(pos[3] * blocks, blocks)]
+    keep = pltpu.make_async_copy(total.at[pl.ds(pos[3] * blocks, blocks)], own, sems.at[0])
+    keep.start()
     out[...] = total[: NY * blocks].reshape(out.shape).astype(BF16)
+    keep.wait()
 
 
 def place(mine, other, blocks):
@@ -280,11 +299,11 @@
         place_kernel,
         out_shape=[
             jax.ShapeDtypeStruct((NY, *piece), BF16),
-            jax.ShapeDtypeStruct(piece, F32),
+            pltpu.HBM(piece, F32),
             jax.ShapeDtypeStruct((2, COLS), jnp.int32),
         ],
         in_specs=[LOCAL] * 2,
-        out_specs=[LOCAL] * 3,
+        out_specs=[LOCAL, REMAIN, LOCAL],
         scratch_shapes=[
             pltpu.VMEM((NY * blocks + 1, UNIT, COLS), F32),
             pltpu.VMEM((2 * sources, COLS), jnp.int32),
@@ -300,12 +319,15 @@
 
 def finish_kernel(*refs):
     pos = place_in_mesh()
-    fx, fz, own, arrived, out, total = refs[:4], refs[4:8], *refs[8:12]
+    fx, fz, held, arrived, out, total, own, sems = refs[:4], refs[4:8], *refs[8:14]
+    fetched = fetch([(held, own)], sems)[0]
     half = fx[0].shape[0]
     blocks = 2 * half
     for first, part in ((0, fx), (half, fz)):
-        value = part[0][...] + part[1][...] + part[2][...] + part[3][...]
+        value = part[0][...] + part[1][...] + part[2][...].astype(F32) + part[3][...]
         span = slice(first, first + half)
+        if first == 0:
+            fetched.wait()
         value = value + own[span]
         for shift in (1, 2, 3):
             value = value + arrived[(pos[3] + shift) % NY, span].astype(F32)
@@ -326,13 +348,17 @@
     return pl.pallas_call(
         finish_kernel,
         out_shape=jax.ShapeDtypeStruct((leaves, 2, 2, UNIT, COLS), BF16),
-        in_specs=[LOCAL] * 10,
+        in_specs=[LOCAL] * 8 + [REMAIN, LOCAL],
         out_specs=LOCAL,
-        scratch_shapes=[pltpu.VMEM(own.shape, BF16)],
+        scratch_shapes=[
+            pltpu.VMEM(own.shape, BF16),
+            pltpu.VMEM(own.shape, F32),
+            pltpu.SemaphoreType.DMA((1,)),
+        ],
         compiler_params=params(8),
         cost_estimate=cost(8 * own.size, 30 * own.size),
         name="finish",
-    )(*[f.reshape(piece) for f in fx], *[f.reshape(piece) for f in fz], own, arrived)
+    )(*[f.reshape(piece) for f in fx], *[f.reshape(piece) for f in fz], remote(own), arrived)
 
 
 def across(a, b):
@@ -421,10 +447,10 @@
     packed = pack(child, child_group.T, child_block.reshape(1, CBD), pivot_leaf, blocks)
     mine = lax.all_to_all(packed, "fcol", 0, 0, tiled=True)
 
-    own_x, x1, x3, xa, xb, own_z, z1, z3, za, zb = front_products(front, test)
+    own_x, *x_parts, xa, xb, own_z, z1, z3, w1, w3, za, zb = front_products(front, test)
     xa, xb = moved(xa, "fcol", along_x(1)), moved(xb, "fcol", along_x(3))
     za, zb = moved(za, "fcol", along_z(1)), moved(zb, "fcol", along_z(3))
-    x_up, x_down, z_up, z_down, mine = relay(x1, x3, xa, xb, z1, z3, za, zb, inv_parent.T, mine)
+    x_up, x_down, z_up, z_down, mine = relay(x_parts, xa, xb, (z1, z3, w1, w3), za, zb, inv_parent.T, mine)
     other = moved(mine, "frow", lambda i: i ^ 1)
     in_x = [moved(x_up, "fcol", along_x(1)), moved(x_down, "fcol", along_x(3))]
     in_z = [moved(z_up, "fcol", along_z(1)), moved(z_down, "fcol", along_z(3))]

time: 91.1 us -> 87.3 us (0.958)
  starting transfers between devices: 37.2 us -> 35.3 us
  blocking collectives: 15.1 us -> 13.3 us
  Pallas kernels: 24.7 us -> 25.7 us
    ppermute x15, starting transfers between devices: 24.8 us -> 22.9 us  [moved(): lax.ppermute(x, axis, [(i, to(i)) for i in range(lax.axis_size(axis))])]
    all_to_all x1, blocking collectives: 15.1 us -> 13.3 us  [on_device(): arrived = lax.all_to_all(placed, 'fcol', 0, 0, tiled=True)]
    pallas_call x1, Pallas kernels: 0.37 us -> 1.4 us  [finish(): pl.pallas_call(finish_kernel, out_shape=jax.ShapeDtypeStruct((leaves, 2,...]
  transfers between devices with their start and end apart: 17 -> 17, of which waited for: 6 -> 3; matrix products, arithmetic and copies ran while one was open for 0% -> 0% of each run, Pallas kernels for 19% -> 20%
where the time goes in v3:
time: 87.3 us; the launch traced here: 86.9 us
  starting transfers between devices  35.3 us (40%)
  Pallas kernels  25.7 us (29%)
  blocking collectives  13.3 us (15%)
  waiting for transfers between devices  11.7 us (13%)
    ppermute x15, starting transfers between devices, moved(): lax.ppermute(x, axis, [(i, to(i)) for i in range(lax.axis_size(axis))])  22.9 us
    all_to_all x1, blocking collectives, on_device(): arrived = lax.all_to_all(placed, 'fcol', 0, 0, tiled=True)  13.3 us
    ppermute x15, waiting for transfers between devices, moved(): lax.ppermute(x, axis, [(i, to(i)) for i in range(lax.axis_size(axis))])  11.7 us
    pallas_call x1, Pallas kernels, front_products(): pl.pallas_call(functools.partial(front_kernel, cuts=cuts), out_shape=[(pl...  11 us
    all_to_all x1, starting transfers between devices, on_device(): mine = lax.all_to_all(packed, 'fcol', 0, 0, tiled=True)  7.97 us
    all_to_all x1, starting transfers between devices, on_device(): lax.all_to_all(out_y, 'frow', 0, 0, tiled=True, axis_index_groups=[[2 * i...  4.48 us
    pallas_call x1, Pallas kernels, place(): pl.pallas_call(place_kernel, out_shape=[jax.ShapeDtypeStruct((NY, *piece)...  4 us
    pallas_call x1, Pallas kernels, relay(): pl.pallas_call(relay_kernel, out_shape=[jax.ShapeDtypeStruct(shape, BF16)...  3.03 us
  transfers between devices with their start and end apart: 17, of which 3 were waited for; matrix products, arithmetic and copies ran while one was open for 0% of the time, Pallas kernels for 20%

profile of v3, /device:TPU:0, one launch (start us, length us, event | category | flops | bytes accessed | tf_op | source)
XLA Modules:
  0.0 86.9 jit_solution(5461638708500997969)
XLA Ops:
  0.6 2.4 %pack.1 = bf16[16,9,32,128]{3,2,1,0:T(8,128)(2,1)} custom-call(bf16[8,128,512]{2,1,0:T(8,128)(2,1)} %bitcast.13, s32[1,8]{1,0:T(1,128)} %bitcast.14, s32[1,8]{1,0:T(1,128)} %bitcast.15, s32[1,96]{1,0:T(1,128)} %pivots_hbm.1), custom_call_target="tpu_custom_call" | custom-call | bytes 2097152 | tf_op jit(solution)/shard_map/pack/pallas_call | solution.py:248
  3.0 8.0 %all-to-all-start = ((bf16[16,9,32,128]{3,2,1,0:T(8,128)(2,1)}), bf16[16,9,32,128]{3,2,1,0:T(8,128)(2,1)S(1)}, u32[]{:S(2)}, u32[]{:S(2)}) async-start(bf16[16,9,32,128]{3,2,1,0:T(8,128)(2,1)} %pack.1), calls=%async_computation | async-start | bytes 2359296 | tf_op jit(solution)/shard_map/all_to_all | solution.py:448
  11.0 0.0 copy-start
  11.0 11.0 %front.1 = (f32[14,32,512]{2,1,0:T(8,128)}, f32[7,32,512]{2,1,0:T(8,128)}, f32[7,32,512]{2,1,0:T(8,128)}, bf16[7,32,512]{2,1,0:T(8,128)(2,1)}, bf16[7,32,512]{2,...) custom-call(bf16[28,128,1792]{2,1,0:T(8,128)(2,1)} %bitcast.16, ...), custom_call_target="tpu_custom_call" | custom-call | flops 6576668672 | bytes 23855104 | tf_op jit(solution)/shard_map/front/pallas_call | solution.py:122
  22.0 2.0 %collective-permute-start = (bf16[7,32,512]{2,1,0:T(8,128)(2,1)S(1)}, bf16[7,32,512]{2,1,0:T(8,128)(2,1)S(1)}, u32[]{:S(2)}, u32[]{:S(2)}) collective-permute-start(bf16[7,32,512]{2,1,0:T(8,128)(2,1)S(1)} %get-tuple-element.44), channel_id=1, source_target_pairs={{0,4},{1,5},{2,6},{3,7},{4,8},{5,9},{6,10},{7,11},{8,12},{9,13},{1... | collective-permute-start | bytes 688136 | tf_op jit(solution)/shard_map/ppermute | solution.py:430
  24.0 1.3 %collective-permute-start.1 = (bf16[7,32,512]{2,1,0:T(8,128)(2,1)S(1)}, bf16[7,32,512]{2,1,0:T(8,128)(2,1)S(1)}, u32[]{:S(2)}, u32[]{:S(2)}) collective-permute-start(bf16[7,32,512]{2,1,0:T(8,128)(2,1)S(1)} %get-tuple-element.45), channel_id=1, source_target_pairs={{0,12},{1,13},{2,14},{3,15},{4,0},{5,1},{6,2},{7,3},{8,4},{9,5},{1... | collective-permute-start | bytes 688136 | tf_op jit(solution)/shard_map/ppermute | solution.py:430
  25.3 1.9 %collective-permute-start.2 = (bf16[28,32,128]{2,1,0:T(8,128)(2,1)S(1)}, bf16[28,32,128]{2,1,0:T(8,128)(2,1)S(1)}, u32[]{:S(2)}, u32[]{:S(2)}) collective-permute-start(bf16[28,32,128]{2,1,0:T(8,128)(2,1)S(1)} %get-tuple-element.50), channel_id=1, source_target_pairs={{0,1},{1,2},{2,3},{3,0},{4,5},{5,6},{6,7},{7,4},{8,9},{9,10},{10,1... | collective-permute-start | bytes 688136 | tf_op jit(solution)/shard_map/ppermute | solution.py:430
  27.3 1.3 %collective-permute-start.3 = (bf16[28,32,128]{2,1,0:T(8,128)(2,1)S(1)}, bf16[28,32,128]{2,1,0:T(8,128)(2,1)S(1)}, u32[]{:S(2)}, u32[]{:S(2)}) collective-permute-start(bf16[28,32,128]{2,1,0:T(8,128)(2,1)S(1)} %get-tuple-element.51), channel_id=1, source_target_pairs={{0,3},{1,0},{2,1},{3,2},{4,7},{5,4},{6,5},{7,6},{8,11},{9,8},{10,9... | collective-permute-start | bytes 688136 | tf_op jit(solution)/shard_map/ppermute | solution.py:430
  28.6 3.6 %collective-permute-done.xa = bf16[7,32,512]{2,1,0:T(8,128)(2,1)S(1)} collective-permute-done((bf16[7,32,512]{2,1,0:T(8,128)(2,1)S(1)}, bf16[7,32,512]{2,1,0:T(8,128)(2,1)S(1)}, u32[]{:S(2)}, u32[]{:S(2)}) %collective-permute-start) | collective-permute-done | bytes 229408 | tf_op jit(solution)/shard_map/ppermute | solution.py:430
  32.2 0.0 collective-permute-done.1.xb
  32.2 1.6 %collective-permute-done.2.za = bf16[28,32,128]{2,1,0:T(8,128)(2,1)S(1)} collective-permute-done((bf16[28,32,128]{2,1,0:T(8,128)(2,1)S(1)}, bf16[28,32,128]{2,1,0:T(8,128)(2,1)S(1)}, u32[]{:S(2)}, u32[]{:S(2)}) %collective-permute-start.2) | collective-permute-done | bytes 229408 | tf_op jit(solution)/shard_map/ppermute | solution.py:430
  33.8 0.0 collective-permute-done.3.zb
  33.8 0.0 all-to-all-done._
  33.8 0.0 copy-done
  33.9 3.0 %relay.1 = (bf16[14,32,512]{2,1,0:T(8,128)(2,1)}, bf16[14,32,512]{2,1,0:T(8,128)(2,1)}, bf16[60,32,128]{2,1,0:T(8,128)(2,1)}, bf16[60,32,128]{2,1,0:T(8,128)(2,1)}, bf16[16,9,32,128]{3,2,1,0:T(8,128)(2,1)S(1)}) custom-call(f32[7,32,512]{2,1,0:T(8,128)} %get-tuple-element.40.hx1, ...), custom_call_target="tpu_custom_call", output_to_operand_aliasing={{4}: (13, {})} | custom-call | flops 458752 | bytes 3211264 | tf_op jit(solution)/shard_map/relay/pallas_call | solution.py:172
  36.9 0.1 collective-permute-start.6
  37.0 1.4 %collective-permute-start.10 = (bf16[60,32,128]{2,1,0:T(8,128)(2,1)}, bf16[60,32,128]{2,1,0:T(8,128)(2,1)S(1)}, u32[]{:S(2)}, u32[]{:S(2)}) collective-permute-start(bf16[60,32,128]{2,1,0:T(8,128)(2,1)} %get-tuple-element.61), channel_id=1, source_target_pairs={{0,1},{1,2},{2,3},{3,0},{4,5},{5,6},{6,7},{7,4},{8,9},{9,10},{10,1... | collective-permute-start | bytes 1474568 | tf_op jit(solution)/shard_map/ppermute | solution.py:430
  38.4 1.9 %collective-permute-start.11 = (bf16[60,32,128]{2,1,0:T(8,128)(2,1)}, bf16[60,32,128]{2,1,0:T(8,128)(2,1)S(1)}, u32[]{:S(2)}, u32[]{:S(2)}) collective-permute-start(bf16[60,32,128]{2,1,0:T(8,128)(2,1)} %get-tuple-element.62), channel_id=1, source_target_pairs={{0,3},{1,0},{2,1},{3,2},{4,7},{5,4},{6,5},{7,6},{8,11},{9,8},{10,9... | collective-permute-start | bytes 1474568 | tf_op jit(solution)/shard_map/ppermute | solution.py:430
  40.3 0.2 collective-permute-start.4
  40.5 3.0 %collective-permute-start.5 = (bf16[14,32,512]{2,1,0:T(8,128)(2,1)}, bf16[14,32,512]{2,1,0:T(8,128)(2,1)S(1)}, u32[]{:S(2)}, u32[]{:S(2)}) collective-permute-start(bf16[14,32,512]{2,1,0:T(8,128)(2,1)} %get-tuple-element.53), channel_id=1, source_target_pairs={{0,12},{1,13},{2,14},{3,15},{4,0},{5,1},{6,2},{7,3},{8,4},{9,5},{1... | collective-permute-start | bytes 1376264 | tf_op jit(solution)/shard_map/ppermute | solution.py:430
  43.5 0.0 collective-permute-done.6.other
  43.5 4.0 %place.1 = (bf16[4,28,32,128]{3,2,1,0:T(8,128)(2,1)}, f32[28,32,128]{2,1,0:T(8,128)}, s32[2,128]{1,0:T(2,128)S(1)}) custom-call(bf16[16,9,32,128]{3,2,1,0:T(8,128)(2,1)S(1)} %get-tuple-element.54.mine, bf16[16,9,32,128]{3,2,1,0:T(8,128)(2,1)S(1)} %collective-permute-done.6.other), custom_call_target="tpu_custom_call" | custom-call | flops 9437184 | bytes 4718592 | tf_op jit(solution)/shard_map/place/pallas_call | solution.py:298
  47.5 4.5 %all-to-all-start.1 = ((bf16[4,28,32,128]{3,2,1,0:T(8,128)(2,1)}), bf16[4,28,32,128]{3,2,1,0:T(8,128)(2,1)S(1)}, u32[]{:S(2)}, u32[]{:S(2)}) async-start(bf16[4,28,32,128]{3,2,1,0:T(8,128)(2,1)} %get-tuple-element.68), calls=%async_computation.1 | async-start | bytes 1835008 | tf_op jit(solution)/shard_map/all_to_all | solution.py:459
  52.0 0.0 collective-permute-done.10.r1
  52.0 0.0 collective-permute-done.11.r2
  52.0 1.4 %sum_z.1 = (f32[14,32,128]{2,1,0:T(8,128)S(1)}, bf16[14,32,128]{2,1,0:T(8,128)(2,1)S(1)}, f32[14,32,128]{2,1,0:T(8,128)S(1)}, f32[14,32,128]{2,1,0:T(8,128)S(1)}, bf16[64,256]{1,0:T(8,128)(2,1)S(1)}) custom-call(f32[56,32,128]{2,1,0:T(8,128)} %get-tuple-element.60.held, bf16[60,32,128]{2,1,0:T(8,128)(2,1)S(1)} %collective-permute-done.10.r1, ...), custom_call_target="tpu_custom_call" | custom-call | flops 688128 | bytes 3211264 | tf_op jit(solution)/shard_map/sum_z/pallas_call | solution.py:212
  53.4 2.0 %collective-permute-start.13 = (bf16[14,32,128]{2,1,0:T(8,128)(2,1)S(1)}, bf16[14,32,128]{2,1,0:T(8,128)(2,1)S(1)}, u32[]{:S(2)}, u32[]{:S(2)}) collective-permute-start(bf16[14,32,128]{2,1,0:T(8,128)(2,1)S(1)} %get-tuple-element.65), channel_id=1, source_target_pairs={{0,8},{1,9},{2,10},{3,11},{4,12},{5,13},{6,14},{7,15},{8,0},{9,1},... | collective-permute-start | bytes 344072 | tf_op jit(solution)/shard_map/ppermute | solution.py:430
  55.4 0.6 collective-permute-start.12
  56.0 2.7 %collective-permute-start.14 = (f32[14,32,128]{2,1,0:T(8,128)S(1)}, f32[14,32,128]{2,1,0:T(8,128)S(1)}, u32[]{:S(2)}, u32[]{:S(2)}) collective-permute-start(f32[14,32,128]{2,1,0:T(8,128)S(1)} %get-tuple-element.66), channel_id=1, source_target_pairs={{0,12},{1,13},{2,14},{3,15},{4,0},{5,1},{6,2},{7,3},{8,4},{9,5},{1... | collective-permute-start | bytes 688136 | tf_op jit(solution)/shard_map/ppermute | solution.py:430
  58.6 0.0 collective-permute-done.4.r1
  58.6 0.0 collective-permute-done.5.r2
  58.6 1.4 %sum_x.1 = (f32[14,32,128]{2,1,0:T(8,128)S(1)}, bf16[14,32,128]{2,1,0:T(8,128)(2,1)S(1)}, f32[14,32,128]{2,1,0:T(8,128)S(1)}, f32[14,32,128]{2,1,0:T(8,128)S(1)}) custom-call(f32[14,32,512]{2,1,0:T(8,128)} %get-tuple-element.39.held, bf16[14,32,512]{2,1,0:T(8,128)(2,1)S(1)} %collective-permute-done.4.r1, bf16[14,32,512]{2,1,0:T(8,128)(2,1)S(1)} %collective-permute-done.5.r2, ...), custom_call_target="tpu_custom_call" | custom-call | flops 688128 | bytes 3211264 | tf_op jit(solution)/shard_map/sum_x/pallas_call | solution.py:212
  60.0 0.5 collective-permute-start.7
  60.5 2.8 %collective-permute-start.9 = (f32[14,32,128]{2,1,0:T(8,128)S(1)}, f32[14,32,128]{2,1,0:T(8,128)S(1)}, u32[]{:S(2)}, u32[]{:S(2)}) collective-permute-start(f32[14,32,128]{2,1,0:T(8,128)S(1)} %get-tuple-element.59), channel_id=1, source_target_pairs={{0,3},{1,0},{2,1},{3,2},{4,7},{5,4},{6,5},{7,6},{8,11},{9,8},{10,9... | collective-permute-start | bytes 688136 | tf_op jit(solution)/shard_map/ppermute | solution.py:430
  63.3 0.0 collective-permute-done.13.refs_6_
  63.3 1.2 %collective-permute-start.8 = (bf16[14,32,128]{2,1,0:T(8,128)(2,1)S(1)}, bf16[14,32,128]{2,1,0:T(8,128)(2,1)S(1)}, u32[]{:S(2)}, u32[]{:S(2)}) collective-permute-start(bf16[14,32,128]{2,1,0:T(8,128)(2,1)S(1)} %get-tuple-element.58), channel_id=1, source_target_pairs={{0,2},{1,3},{2,0},{3,1},{4,6},{5,7},{6,4},{7,5},{8,10},{9,11},{10,... | collective-permute-start | bytes 344072 | tf_op jit(solution)/shard_map/ppermute | solution.py:430
  64.5 6.4 %collective-permute-done.8.refs_2_ = bf16[14,32,128]{2,1,0:T(8,128)(2,1)S(1)} collective-permute-done((bf16[14,32,128]{2,1,0:T(8,128)(2,1)S(1)}, bf16[14,32,128]{2,1,0:T(8,128)(2,1)S(1)}, u32[]{:S(2)}, u32[]{:S(2)}) %collective-permute-start.8) | collective-permute-done | bytes 114720 | tf_op jit(solution)/shard_map/ppermute | solution.py:430
  70.9 0.0 collective-permute-done.12.refs_5_
  70.9 0.0 collective-permute-done.14.refs_7_
  70.9 0.0 collective-permute-done.7.refs_1_
  71.0 0.0 collective-permute-done.9.refs_3_
  71.0 0.0 all-to-all-done.1.refs_9_
  71.0 0.0 copy-start.1
  71.0 0.0 copy-start.2
  71.0 1.4 %finish.1 = bf16[16,2,2,32,128]{4,3,2,1,0:T(8,128)(2,1)S(1)} custom-call(f32[14,32,128]{2,1,0:T(8,128)S(1)} %get-tuple-element.56.refs_0_, f32[14,32,128]{2,1,0:T(8,128)S(1)} %collective-permute-done.7.refs_1_, bf16[14,32,128]{2,1,0:T(8,128)(2,1)S(1)} %collective-permute-done.8.refs_2_, f32[14,32,128]{2,1,0:T(8,128)S(1)} %collective-permute-done.9.refs_3_, ...), custom_call_target="tpu_custom_call" | custom-call | flops 917504 | bytes 3440640 | tf_op jit(solution)/shard_map/finish/pallas_call | solution.py:348
  72.4 13.3 %all_to_all.15.arrived = bf16[16,2,2,32,128]{4,3,2,1,0:T(8,128)(2,1)S(1)} all-to-all(bf16[16,2,2,32,128]{4,3,2,1,0:T(8,128)(2,1)S(1)} %finish.1), channel_id=1, replica_groups=mesh['frow'=8,'fcol'=16] {'fcol'}, dimensions={0} | all-to-all | bytes 1048576 | tf_op jit(solution)/shard_map/all_to_all | solution.py:472
  85.7 0.0 copy-done.1
  85.7 0.0 copy-done.2
  85.7 1.2 %tail.1 = (bf16[224,512]{1,0:T(8,128)(2,1)}, f32[96,224]{1,0:T(8,128)}, f32[64,96]{1,0:T(8,128)}, bf16[32,512]{1,0:T(8,128)(2,1)}) custom-call(bf16[16,2,2,32,128]{4,3,2,1,0:T(8,128)(2,1)S(1)} %all_to_all.15.arrived, bf16[96,512]{1,0:T(8,128)(2,1)S(1)} %bitcast.11, bf16[64,256]{1,0:T(8,128)(2,1)S(1)} %bitcast.10, ...), custom_call_target="tpu_custom_call" | custom-call | flops 75497472 | bytes 786432 | tf_op jit(solution)/shard_map/tail/pallas_call | solution.py:414
Async XLA Ops:
  3.0 30.8 %all-to-all-start = ((bf16[16,9,32,128]{3,2,1,0:T(8,128)(2,1)}), bf16[16,9,32,128]{3,2,1,0:T(8,128)(2,1)S(1)}, u32[]{:S(2)}, u32[]{:S(2)}) async-start(bf16[16,9,32,128]{3,2,1,0:T(8,128)(2,1)} %pack.1), calls=%async_computation | async-start | bytes 2359296 | tf_op jit(solution)/shard_map/all_to_all | solution.py:448
  11.0 22.8 %copy-start = (bf16[256,64]{0,1:T(8,128)(2,1)S(1)}, bf16[256,64]{0,1:T(8,128)(2,1)}, u32[]{:S(2)}) copy-start(bf16[256,64]{0,1:T(8,128)(2,1)} %param.15) | copy-start | bytes 98308
  22.0 10.2 %collective-permute-start = (bf16[7,32,512]{2,1,0:T(8,128)(2,1)S(1)}, bf16[7,32,512]{2,1,0:T(8,128)(2,1)S(1)}, u32[]{:S(2)}, u32[]{:S(2)}) collective-permute-start(bf16[7,32,512]{2,1,0:T(8,128)(2,1)S(1)} %get-tuple-element.44), channel_id=1, source_target_pairs={{0,4},{1,5},{2,6},{3,7},{4,8},{5,9},{6,10},{7,11},{8,12},{9,13},{1... | collective-permute-start | bytes 688136 | tf_op jit(solution)/shard_map/ppermute | solution.py:430
  24.0 8.2 %collective-permute-start.1 = (bf16[7,32,512]{2,1,0:T(8,128)(2,1)S(1)}, bf16[7,32,512]{2,1,0:T(8,128)(2,1)S(1)}, u32[]{:S(2)}, u32[]{:S(2)}) collective-permute-start(bf16[7,32,512]{2,1,0:T(8,128)(2,1)S(1)} %get-tuple-element.45), channel_id=1, source_target_pairs={{0,12},{1,13},{2,14},{3,15},{4,0},{5,1},{6,2},{7,3},{8,4},{9,5},{1... | collective-permute-start | bytes 688136 | tf_op jit(solution)/shard_map/ppermute | solution.py:430
  25.3 8.5 %collective-permute-start.2 = (bf16[28,32,128]{2,1,0:T(8,128)(2,1)S(1)}, bf16[28,32,128]{2,1,0:T(8,128)(2,1)S(1)}, u32[]{:S(2)}, u32[]{:S(2)}) collective-permute-start(bf16[28,32,128]{2,1,0:T(8,128)(2,1)S(1)} %get-tuple-element.50), channel_id=1, source_target_pairs={{0,1},{1,2},{2,3},{3,0},{4,5},{5,6},{6,7},{7,4},{8,9},{9,10},{10,1... | collective-permute-start | bytes 688136 | tf_op jit(solution)/shard_map/ppermute | solution.py:430
  27.3 6.6 %collective-permute-start.3 = (bf16[28,32,128]{2,1,0:T(8,128)(2,1)S(1)}, bf16[28,32,128]{2,1,0:T(8,128)(2,1)S(1)}, u32[]{:S(2)}, u32[]{:S(2)}) collective-permute-start(bf16[28,32,128]{2,1,0:T(8,128)(2,1)S(1)} %get-tuple-element.51), channel_id=1, source_target_pairs={{0,3},{1,0},{2,1},{3,2},{4,7},{5,4},{6,5},{7,6},{8,11},{9,8},{10,9... | collective-permute-start | bytes 688136 | tf_op jit(solution)/shard_map/ppermute | solution.py:430
  36.9 6.6 %collective-permute-start.6 = (bf16[16,9,32,128]{3,2,1,0:T(8,128)(2,1)S(1)}, bf16[16,9,32,128]{3,2,1,0:T(8,128)(2,1)S(1)}, u32[]{:S(2)}, u32[]{:S(2)}) collective-permute-start(bf16[16,9,32,128]{3,2,1,0:T(8,128)(2,1)S(1)} %get-tuple-element.54.mine), channel_id=1, source_target_pairs={{0,16},{16,0},{32,48},{48,32},{64,80},{80,64},{96,112},{112,96},{1... | collective-permute-start | bytes 3538952 | tf_op jit(solution)/shard_map/ppermute | solution.py:430
  37.0 15.1 %collective-permute-start.10 = (bf16[60,32,128]{2,1,0:T(8,128)(2,1)}, bf16[60,32,128]{2,1,0:T(8,128)(2,1)S(1)}, u32[]{:S(2)}, u32[]{:S(2)}) collective-permute-start(bf16[60,32,128]{2,1,0:T(8,128)(2,1)} %get-tuple-element.61), channel_id=1, source_target_pairs={{0,1},{1,2},{2,3},{3,0},{4,5},{5,6},{6,7},{7,4},{8,9},{9,10},{10,1... | collective-permute-start | bytes 1474568 | tf_op jit(solution)/shard_map/ppermute | solution.py:430
  38.4 13.6 %collective-permute-start.11 = (bf16[60,32,128]{2,1,0:T(8,128)(2,1)}, bf16[60,32,128]{2,1,0:T(8,128)(2,1)S(1)}, u32[]{:S(2)}, u32[]{:S(2)}) collective-permute-start(bf16[60,32,128]{2,1,0:T(8,128)(2,1)} %get-tuple-element.62), channel_id=1, source_target_pairs={{0,3},{1,0},{2,1},{3,2},{4,7},{5,4},{6,5},{7,6},{8,11},{9,8},{10,9... | collective-permute-start | bytes 1474568 | tf_op jit(solution)/shard_map/ppermute | solution.py:430
  40.3 18.3 %collective-permute-start.4 = (bf16[14,32,512]{2,1,0:T(8,128)(2,1)}, bf16[14,32,512]{2,1,0:T(8,128)(2,1)S(1)}, u32[]{:S(2)}, u32[]{:S(2)}) collective-permute-start(bf16[14,32,512]{2,1,0:T(8,128)(2,1)} %get-tuple-element.52), channel_id=1, source_target_pairs={{0,4},{1,5},{2,6},{3,7},{4,8},{5,9},{6,10},{7,11},{8,12},{9,13},{1... | collective-permute-start | bytes 1376264 | tf_op jit(solution)/shard_map/ppermute | solution.py:430
  40.5 18.1 %collective-permute-start.5 = (bf16[14,32,512]{2,1,0:T(8,128)(2,1)}, bf16[14,32,512]{2,1,0:T(8,128)(2,1)S(1)}, u32[]{:S(2)}, u32[]{:S(2)}) collective-permute-start(bf16[14,32,512]{2,1,0:T(8,128)(2,1)} %get-tuple-element.53), channel_id=1, source_target_pairs={{0,12},{1,13},{2,14},{3,15},{4,0},{5,1},{6,2},{7,3},{8,4},{9,5},{1... | collective-permute-start | bytes 1376264 | tf_op jit(solution)/shard_map/ppermute | solution.py:430
  47.5 23.4 %all-to-all-start.1 = ((bf16[4,28,32,128]{3,2,1,0:T(8,128)(2,1)}), bf16[4,28,32,128]{3,2,1,0:T(8,128)(2,1)S(1)}, u32[]{:S(2)}, u32[]{:S(2)}) async-start(bf16[4,28,32,128]{3,2,1,0:T(8,128)(2,1)} %get-tuple-element.68), calls=%async_computation.1 | async-start | bytes 1835008 | tf_op jit(solution)/shard_map/all_to_all | solution.py:459
  53.4 9.9 %collective-permute-start.13 = (bf16[14,32,128]{2,1,0:T(8,128)(2,1)S(1)}, bf16[14,32,128]{2,1,0:T(8,128)(2,1)S(1)}, u32[]{:S(2)}, u32[]{:S(2)}) collective-permute-start(bf16[14,32,128]{2,1,0:T(8,128)(2,1)S(1)} %get-tuple-element.65), channel_id=1, source_target_pairs={{0,8},{1,9},{2,10},{3,11},{4,12},{5,13},{6,14},{7,15},{8,0},{9,1},... | collective-permute-start | bytes 344072 | tf_op jit(solution)/shard_map/ppermute | solution.py:430
  55.4 15.6 %collective-permute-start.12 = (f32[14,32,128]{2,1,0:T(8,128)S(1)}, f32[14,32,128]{2,1,0:T(8,128)S(1)}, u32[]{:S(2)}, u32[]{:S(2)}) collective-permute-start(f32[14,32,128]{2,1,0:T(8,128)S(1)} %get-tuple-element.64), channel_id=1, source_target_pairs={{0,4},{1,5},{2,6},{3,7},{4,8},{5,9},{6,10},{7,11},{8,12},{9,13},{1... | collective-permute-start | bytes 688136 | tf_op jit(solution)/shard_map/ppermute | solution.py:430
  56.0 15.0 %collective-permute-start.14 = (f32[14,32,128]{2,1,0:T(8,128)S(1)}, f32[14,32,128]{2,1,0:T(8,128)S(1)}, u32[]{:S(2)}, u32[]{:S(2)}) collective-permute-start(f32[14,32,128]{2,1,0:T(8,128)S(1)} %get-tuple-element.66), channel_id=1, source_target_pairs={{0,12},{1,13},{2,14},{3,15},{4,0},{5,1},{6,2},{7,3},{8,4},{9,5},{1... | collective-permute-start | bytes 688136 | tf_op jit(solution)/shard_map/ppermute | solution.py:430
  60.0 10.9 %collective-permute-start.7 = (f32[14,32,128]{2,1,0:T(8,128)S(1)}, f32[14,32,128]{2,1,0:T(8,128)S(1)}, u32[]{:S(2)}, u32[]{:S(2)}) collective-permute-start(f32[14,32,128]{2,1,0:T(8,128)S(1)} %get-tuple-element.57), channel_id=1, source_target_pairs={{0,1},{1,2},{2,3},{3,0},{4,5},{5,6},{6,7},{7,4},{8,9},{9,10},{10,1... | collective-permute-start | bytes 688136 | tf_op jit(solution)/shard_map/ppermute | solution.py:430
  60.5 10.4 %collective-permute-start.9 = (f32[14,32,128]{2,1,0:T(8,128)S(1)}, f32[14,32,128]{2,1,0:T(8,128)S(1)}, u32[]{:S(2)}, u32[]{:S(2)}) collective-permute-start(f32[14,32,128]{2,1,0:T(8,128)S(1)} %get-tuple-element.59), channel_id=1, source_target_pairs={{0,3},{1,0},{2,1},{3,2},{4,7},{5,4},{6,5},{7,6},{8,11},{9,8},{10,9... | collective-permute-start | bytes 688136 | tf_op jit(solution)/shard_map/ppermute | solution.py:430
  63.3 7.6 %collective-permute-start.8 = (bf16[14,32,128]{2,1,0:T(8,128)(2,1)S(1)}, bf16[14,32,128]{2,1,0:T(8,128)(2,1)S(1)}, u32[]{:S(2)}, u32[]{:S(2)}) collective-permute-start(bf16[14,32,128]{2,1,0:T(8,128)(2,1)S(1)} %get-tuple-element.58), channel_id=1, source_target_pairs={{0,2},{1,3},{2,0},{3,1},{4,6},{5,7},{6,4},{7,5},{8,10},{9,11},{10,... | collective-permute-start | bytes 344072 | tf_op jit(solution)/shard_map/ppermute | solution.py:430
  71.0 14.8 %copy-start.1 = (bf16[512,96]{0,1:T(8,128)(2,1)S(1)}, bf16[512,96]{0,1:T(8,128)(2,1)}, u32[]{:S(2)}) copy-start(bf16[512,96]{0,1:T(8,128)(2,1)} %param.14) | copy-start | bytes 294916
  71.0 14.7 %copy-start.2 = (s32[1,32]{1,0:T(1,128)S(1)}, s32[1,32]{1,0:T(1,128)}, u32[]{:S(2)}) copy-start(s32[1,32]{1,0:T(1,128)} %piv_parent.1) | copy-start | bytes 388

commit v4 on v3

--- a/solution.py
+++ b/solution.py
@@ -15,7 +15,7 @@
 NZ = 4
 NY = 4
 UNIT = 32
-SCALE = 1
+TOLD = 16
 COLS = 128
 LOCAL = pl.BlockSpec(memory_space=pltpu.VMEM)
 REMAIN = pl.BlockSpec(memory_space=pltpu.HBM)
@@ -27,7 +27,7 @@
 
 
 def cost(flops, moved_bytes):
-    return pl.CostEstimate(flops=flops // SCALE, bytes_accessed=moved_bytes // SCALE, transcendentals=0)
+    return pl.CostEstimate(flops=flops, bytes_accessed=moved_bytes, transcendentals=0)
 
 
 def place_in_mesh():
@@ -46,60 +46,128 @@
     return copies
 
 
-def front_kernel(a_hbm, b_hbm, x0, x1, x3, u1, u3, xa, xb, z0, z1, z3, w1, w3, za, zb,
-                 a, b, turned, value, sx0, sx1, sx3, su1, su3, sz0, sz1, sz3, sw1, sw3, sems, out_sems, *, cuts):
+def put_parts(products, stores, out_sems):
+    for (ref, out), at, value in products:
+        ref[at : at + value.shape[0]] = value.astype(ref.dtype)
+        if out is not None:
+            span = pl.ds(at, value.shape[0])
+            stores.append(pltpu.make_async_copy(ref.at[span], out.at[span], out_sems.at[len(stores)]))
+            stores[-1].start()
+
+
+def part_products(rows_x, rows_z, weights, weights_z, x_targets, z_targets, ready, out_sems):
+    half, depth = rows_z.shape[0], rows_z.shape[-1]
+    step = half // 2
+    stores = []
+    for i, target in enumerate(x_targets):
+        ready(i)
+        product = jnp.dot(rows_x[i].reshape(half * UNIT, depth), weights[...], preferred_element_type=F32)
+        product = product.reshape(half, UNIT, NZ * COLS)
+        put_parts([(target[t], 0, product[t * step : (t + 1) * step]) for t in range(2)], stores, out_sems)
+    for part in range(2):
+        ready(len(x_targets) + part)
+        rows = rows_z[part * step : (part + 1) * step].reshape(step * BLK, depth)
+        product = jnp.dot(rows, weights_z[...], preferred_element_type=F32)
+        product = product.reshape(step, NX, UNIT, 2 * COLS)
+        for jr in range(NX):
+            at = jr % (NX // 2) * half + part * step
+            put_parts(
+                [
+                    (target[jr // (NX // 2)], at, product[:, jr, :, i * COLS : (i + 1) * COLS])
+                    for i, target in enumerate(z_targets)
+                ],
+                stores, out_sems,
+            )
+    for store in stores:
+        store.wait()
+
+
+def far_kernel(a_hbm, b_hbm, token, xa, xb, za, zb, oz_low, oz_high, near_x, rows_z, turned, turned_z,
+               ax, b, bz, sz_low, sz_high, sems, out_sems):
     x, z = place_in_mesh()[:2]
-    half = a.shape[0] // 2
-    spans = list(zip(cuts[:-1], cuts[1:]))
-    copies = [pltpu.make_async_copy(b_hbm, b, sems.at[0])]
-    copies += [pltpu.make_async_copy(a_hbm.at[lo:hi], a.at[lo:hi], sems.at[i + 1]) for i, (lo, hi) in enumerate(spans)]
-    for copy in copies[:3]:
-        copy.start()
-
-    def arrive(i):
-        copies[i].wait()
-        if i + 3 < len(copies):
-            copies[i + 3].start()
-
-    stores = []
-
-    def store(staged, out, at):
-        copy = pltpu.make_async_copy(staged.at[at], out.at[at], out_sems.at[len(stores)])
-        copy.start()
-        stores.append(copy)
-
-    arrive(0)
+    half = rows_z.shape[0]
+    step = half // 2
+    pairs = [(b_hbm, b)]
+    pairs += [(a_hbm.at[:half, (x + 2) % NX], ax.at[0])]
+    pairs += [
+        (a_hbm.at[half + i * step : half + (i + 1) * step], rows_z.at[i * step : (i + 1) * step]) for i in range(2)
+    ]
+    pairs += [(a_hbm.at[:half, (x + s) % NX], near_x.at[i]) for i, s in enumerate((1, 3, 0))]
+    loads = [pltpu.make_async_copy(src, dst, sems.at[i]) for i, (src, dst) in enumerate(pairs)]
+    for load in loads[:3]:
+        load.start()
+
+    def ready(i):
+        loads[i + 1].wait()
+        if i + 4 < len(loads):
+            loads[i + 4].start()
+
+    ready(-1)
     for s in range(NZ):
-        at = pl.multiple_of((z + s) % NZ * COLS, COLS)
-        turned[:, s * COLS : (s + 1) * COLS] = b[:, pl.ds(at, COLS)]
-    for i, (lo, hi) in enumerate(spans):
-        arrive(i + 1)
-        rows = (hi - lo) * BLK
-        block = a[lo:hi].reshape(rows, a.shape[-1])
-        product = jnp.dot(block, turned[...], preferred_element_type=F32)
-        product = product.reshape(hi - lo, NX, UNIT, NZ * COLS)
-        if hi <= half:
-            value[: hi - lo] = product
-            first = hi <= half // 2
-            at = lo if first else lo - half // 2
-            one, three, two = ((sx1, x1), (su3, u3), xa) if first else ((su1, u1), (sx3, x3), xb)
-            for s, (staged, out), start in ((0, (sx0, x0), lo), (1, one, at), (3, three, at)):
-                staged[start : start + hi - lo] = value[: hi - lo, (x + s) % NX].astype(staged.dtype)
-                store(staged, out, pl.ds(start, hi - lo))
-            two[at : at + hi - lo] = value[: hi - lo, (x + 2) % NX].astype(BF16)
-        else:
-            for jr in range(NX):
-                at = jr * half + lo - half
-                piece = product[:, jr]
-                first = jr < NX // 2
-                near = at if first else at - NX // 2 * half
-                one, three, two = ((sz1, z1), (sw3, w3), za) if first else ((sw1, w1), (sz3, z3), zb)
-                for s, (staged, out), start in ((0, (sz0, z0), at), (1, one, near), (3, three, near)):
-                    staged[start : start + hi - lo] = piece[..., s * COLS : (s + 1) * COLS].astype(staged.dtype)
-                    store(staged, out, pl.ds(start, hi - lo))
-                two[near : near + hi - lo] = piece[..., 2 * COLS : 3 * COLS].astype(BF16)
-    for copy in stores:
-        copy.wait()
+        piece = b[:, pl.ds(pl.multiple_of((z + s) % NZ * COLS, COLS), COLS)]
+        turned[:, s * COLS : (s + 1) * COLS] = piece
+        out, at = (bz, (2 - s) // 2 * COLS) if s % 2 == 0 else (turned_z, s // 2 * COLS)
+        out[:, at : at + COLS] = piece
+    part_products(
+        ax, rows_z, turned, bz,
+        (((xa, None), (xb, None)),),
+        (((za, None), (zb, None)), ((sz_low, oz_low), (sz_high, oz_high))),
+        ready, out_sems,
+    )
+    for load in loads[4:]:
+        load.wait()
+
+
+def near_kernel(near_x, rows_z, turned, turned_z, x1, u1, u3, x3, ox_low, ox_high, z1, w1, w3, z3,
+                sx1, su1, su3, sx3, sx_low, sx_high, sz1, sw1, sw3, sz3, out_sems):
+    part_products(
+        near_x, rows_z, turned, turned_z,
+        (((sx1, x1), (su1, u1)), ((su3, u3), (sx3, x3)), ((sx_low, ox_low), (sx_high, ox_high))),
+        (((sz1, z1), (sw1, w1)), ((sw3, w3), (sz3, z3))),
+        lambda i: None, out_sems,
+    )
+
+
+def far_products(front, test, token):
+    blocks, depth, cols = front.shape[0] // BLK, front.shape[1], test.shape[1]
+    half = blocks // 2
+    x_shape, z_shape = (half // 2, UNIT, cols), (NX // 2 * half, UNIT, COLS)
+    sent = [jax.ShapeDtypeStruct(shape, BF16) for shape in (x_shape, x_shape, z_shape, z_shape)]
+    kept = [((3, half, UNIT, depth), BF16), ((half, NX, UNIT, depth), BF16), (test.shape, BF16), ((depth, 2 * COLS), BF16)]
+    return pl.pallas_call(
+        far_kernel,
+        out_shape=sent + [pltpu.HBM(z_shape, F32)] * 2 + [pltpu.VMEM(*k) for k in kept],
+        in_specs=[REMAIN] * 2 + [ANY],
+        out_specs=[LOCAL] * 4 + [REMAIN] * 2 + [LOCAL] * 4,
+        scratch_shapes=[
+            pltpu.VMEM((1, half, UNIT, depth), BF16),
+            pltpu.VMEM(test.shape, BF16),
+            pltpu.VMEM((depth, 2 * COLS), BF16),
+            *[pltpu.VMEM(z_shape, F32)] * 2,
+            pltpu.SemaphoreType.DMA((7,)),
+            pltpu.SemaphoreType.DMA((12,)),
+        ],
+        compiler_params=params(18),
+        cost_estimate=cost(front.size * cols, 2 * (front.size + test.size) + 3 * blocks * BLK * cols),
+        name="far",
+    )(remote(front.reshape(blocks, NX, UNIT, depth)), remote(test), token)
+
+
+def near_products(near_x, rows_z, turned, turned_z):
+    half, cols = rows_z.shape[0], turned.shape[1]
+    kinds = (F32, BF16, BF16, F32)
+    shapes = [((half // 2, UNIT, cols), t) for t in (*kinds, F32, F32)]
+    shapes += [((NX // 2 * half, UNIT, COLS), t) for t in kinds]
+    return pl.pallas_call(
+        near_kernel,
+        out_shape=[pltpu.HBM(*s) for s in shapes],
+        in_specs=[LOCAL] * 4,
+        out_specs=[REMAIN] * 10,
+        scratch_shapes=[*[pltpu.VMEM(*s) for s in shapes], pltpu.SemaphoreType.DMA((22,))],
+        compiler_params=params(12),
+        cost_estimate=cost(8 * half * BLK * turned.size, 20 * half * BLK * cols),
+        name="near",
+    )(*[pltpu.with_memory_space_constraint(v, pltpu.VMEM) for v in (near_x, rows_z, turned, turned_z)])
 
 
 def inverse_tiles(shape):
@@ -108,37 +176,6 @@
         for i in range(0, shape[0], UNIT)
         for j in range(0, shape[1], COLS)
     ]
-
-
-def front_products(front, test):
-    blocks, depth, cols = front.shape[0] // BLK, front.shape[1], test.shape[1]
-    half = blocks // 2
-    step = half // 2
-    cuts = (0, step // 2, *range(step, blocks + 1, step))
-    kinds = ((1, F32), (2, F32), (2, F32), (2, BF16), (2, BF16), (2, BF16), (2, BF16))
-    shapes = [((half // n, UNIT, cols), t) for n, t in kinds]
-    shapes += [((NX * half // n, UNIT, COLS), t) for n, t in kinds]
-    later = [i % 7 < 5 for i in range(14)]
-    return pl.pallas_call(
-        functools.partial(front_kernel, cuts=cuts),
-        out_shape=[(pltpu.HBM if l else jax.ShapeDtypeStruct)(*s) for s, l in zip(shapes, later)],
-        in_specs=[REMAIN, REMAIN],
-        out_specs=[REMAIN if l else LOCAL for l in later],
-        scratch_shapes=[
-            pltpu.VMEM((blocks, BLK, depth), BF16),
-            pltpu.VMEM(test.shape, BF16),
-            pltpu.VMEM(test.shape, BF16),
-            pltpu.VMEM((step, NX, UNIT, cols), F32),
-            *[pltpu.VMEM(*s) for s, l in zip(shapes, later) if l],
-            pltpu.SemaphoreType.DMA((len(cuts),)),
-            pltpu.SemaphoreType.DMA((3 * (len(cuts) - 1 + 2 * NX),)),
-        ],
-        compiler_params=params(30),
-        cost_estimate=cost(
-            2 * front.size * cols, 2 * (front.size + test.size) + 5 * blocks * BLK * cols
-        ),
-        name="front",
-    )(remote(front.reshape(blocks, BLK, depth)), remote(test))
 
 
 def relay_kernel(hx1, hx3, hu1, hu3, xa, xb, hz1, hz3, hw1, hw3, za, zb, inverse, _,
@@ -185,23 +222,25 @@
     )(*map(remote, x_parts), xa, xb, *map(remote, z_parts), za, zb, inverse, mine)
 
 
-def sum_x_kernel(held, r1, r2, token, to1, to2, to3, keep, own, sems):
-    outs = ((1, to1), (2, to2), (3, to3), (0, keep))
-    spans = [(slice(None), slice(None), slice(s * COLS, (s + 1) * COLS)) for s, _ in outs]
-    copies = fetch([(held.at[at], own.at[at]) for at in spans], sems)
-    for at, copy, (_, out) in zip(spans, copies, outs):
+def sum_x_kernel(low, high, r1, r2, token, to1, to2, to3, keep, own, sems):
+    half = low.shape[0]
+    copies = fetch([(low, own.at[:half]), (high, own.at[half:])], sems)
+    for i, copy in enumerate(copies):
         copy.wait()
-        out[...] = (own[at] + r1[at].astype(F32) + r2[at].astype(F32)).astype(out.dtype)
-
-
-def sum_z_kernel(held, r1, r2, token, to1, to2, to3, keep, inverse, own, sems):
+        for s, out in ((1, to1), (2, to2), (3, to3), (0, keep)):
+            at = (slice(i * half, (i + 1) * half), slice(None), slice(s * COLS, (s + 1) * COLS))
+            out[at[0]] = (own[at] + r1[at].astype(F32) + r2[at].astype(F32)).astype(out.dtype)
+
+
+def sum_z_kernel(low, high, r1, r2, token, to1, to2, to3, keep, inverse, own, sems):
     x, z = place_in_mesh()[:2]
     half = keep.shape[0]
-    outs = ((1, to1), (2, to2), (3, to3), (0, keep))
-    spans = [pl.ds((x + s) % NX * half, half) for s, _ in outs]
-    copies = fetch([(held.at[at], own.at[at]) for at in spans], sems)
-    for at, copy, (_, out) in zip(spans, copies, outs):
+    size = low.shape[0]
+    copies = fetch([(low, own.at[:size]), (high, own.at[size:])], sems)
+    for copy in copies:
         copy.wait()
+    for s, out in ((1, to1), (2, to2), (3, to3), (0, keep)):
+        at = pl.ds((x + s) % NX * half, half)
         out[...] = (own[at] + r1[at].astype(F32) + r2[at].astype(F32)).astype(out.dtype)
     for i, (rows, columns) in enumerate(inverse_tiles(inverse.shape)):
         inverse[rows, columns] = lax.select(z % 2 == 0, r2[NX * half + i], r1[NX * half + i])
@@ -212,13 +251,16 @@
     return pl.pallas_call(
         kernel,
         out_shape=outs,
-        in_specs=[REMAIN] + [LOCAL] * 2 + [ANY],
+        in_specs=[REMAIN] * 2 + [LOCAL] * 2 + [ANY],
         out_specs=[LOCAL] * len(outs),
-        scratch_shapes=[pltpu.VMEM(own.shape, F32), pltpu.SemaphoreType.DMA((4,))],
+        scratch_shapes=[
+            pltpu.VMEM((2 * own[0].shape[0], *own[0].shape[1:]), F32),
+            pltpu.SemaphoreType.DMA((2,)),
+        ],
         compiler_params=params(8),
-        cost_estimate=cost(3 * own.size, 14 * own.size),
+        cost_estimate=cost(6 * own[0].size, 28 * own[0].size),
         name=kernel.__name__[:5],
-    )(remote(own), *arrived, token)
+    )(*map(remote, own), *arrived, token)
 
 
 def pack_kernel(child, group_hbm, block_hbm, pivots_hbm, out, group, block, pivots, facts, local, sems, *, blocks):
@@ -234,25 +276,25 @@
     facts[1:2, : pivots.shape[1]] = pivots[...].astype(F32)
     told = facts[...].astype(BF16)
     for i in range(out.shape[0]):
-        out[i, CBD] = told
+        out[i, CBD * UNIT :] = told
     for i in range(0, CBD, 2):
         copies[3 + i // 2].wait()
         for x in range(NX):
             for z in range(NZ):
                 part = local[i : i + 2, x * UNIT : (x + 1) * UNIT, z * COLS : (z + 1) * COLS]
-                out[x * NZ + z, i : i + 2] = part
+                out[x * NZ + z, i * UNIT : (i + 2) * UNIT] = part.reshape(2 * UNIT, COLS)
 
 
 def pack(child, group, block, pivots, blocks):
     child = remote(child.reshape(CBD, BLK, child.shape[1]))
     return pl.pallas_call(
         functools.partial(pack_kernel, blocks=blocks),
-        out_shape=jax.ShapeDtypeStruct((NX * NZ, CBD + 1, UNIT, COLS), BF16),
+        out_shape=jax.ShapeDtypeStruct((NX * NZ, CBD * UNIT + TOLD, COLS), BF16),
         in_specs=[REMAIN] * 4,
         out_specs=LOCAL,
         scratch_shapes=[
             *[pltpu.VMEM(v.shape, v.dtype) for v in (group, block, pivots)],
-            pltpu.VMEM((UNIT, COLS), F32),
+            pltpu.VMEM((TOLD, COLS), F32),
             pltpu.VMEM(child.shape, BF16),
             pltpu.SemaphoreType.DMA((CBD // 2 + 3,)),
         ],
@@ -267,7 +309,7 @@
     blocks = out.shape[1]
     sources = mine.shape[0]
     for t, ref in ((0, mine), (1, other)):
-        told[t * sources : (t + 1) * sources] = ref[:, CBD].astype(F32)
+        told[t * sources : (t + 1) * sources] = ref[:, CBD * UNIT :].astype(F32)
     dest = told[:, 0].astype(jnp.int32)
     group = dest // blocks
     facts[...] = jnp.where(
@@ -282,7 +324,7 @@
         def body(i, _, t=t, ref=ref):
             for j in range(CBD):
                 at = slots[t * sources + i, j]
-                total[at] += ref[i, j].astype(F32)
+                total[at] += ref[i, j * UNIT : (j + 1) * UNIT].astype(F32)
             return _
 
         lax.fori_loop(0, sources, body, 0)
@@ -307,7 +349,7 @@
         scratch_shapes=[
             pltpu.VMEM((NY * blocks + 1, UNIT, COLS), F32),
             pltpu.VMEM((2 * sources, COLS), jnp.int32),
-            pltpu.VMEM((2 * sources, UNIT, COLS), F32),
+            pltpu.VMEM((2 * sources, TOLD, COLS), F32),
             pltpu.SMEM((2 * sources, COLS), jnp.int32),
             pltpu.SemaphoreType.DMA((1,)),
         ],
@@ -447,10 +489,14 @@
     packed = pack(child, child_group.T, child_block.reshape(1, CBD), pivot_leaf, blocks)
     mine = lax.all_to_all(packed, "fcol", 0, 0, tiled=True)
 
-    own_x, *x_parts, xa, xb, own_z, z1, z3, w1, w3, za, zb = front_products(front, test)
+    xa, xb, za, zb, z_low, z_high, near_x, rows_z, turned, turned_z = far_products(front, test, packed)
     xa, xb = moved(xa, "fcol", along_x(1)), moved(xb, "fcol", along_x(3))
     za, zb = moved(za, "fcol", along_z(1)), moved(zb, "fcol", along_z(3))
-    x_up, x_down, z_up, z_down, mine = relay(x_parts, xa, xb, (z1, z3, w1, w3), za, zb, inv_parent.T, mine)
+    x1, u1, u3, x3, x_low, x_high, z1, w1, w3, z3 = near_products(near_x, rows_z, turned, turned_z)
+    own_x, own_z = (x_low, x_high), (z_low, z_high)
+    x_up, x_down, z_up, z_down, mine = relay(
+        (x1, x3, u1, u3), xa, xb, (z1, z3, w1, w3), za, zb, inv_parent.T, mine
+    )
     other = moved(mine, "frow", lambda i: i ^ 1)
     in_x = [moved(x_up, "fcol", along_x(1)), moved(x_down, "fcol", along_x(3))]
     in_z = [moved(z_up, "fcol", along_z(1)), moved(z_down, "fcol", along_z(3))]

time: 87.3 us -> 86 us (0.985)
  waiting for transfers between devices: 11.7 us -> 7.2 us
  Pallas kernels: 25.7 us -> 29.1 us
    ppermute x15, waiting for transfers between devices: 11.7 us -> 7.2 us  [moved(): lax.ppermute(x, axis, [(i, to(i)) for i in range(lax.axis_size(axis))])]
    pallas_call x3 -> x4, Pallas kernels: 13.8 us -> 16.9 us  [the longest x1 8.19 us: far_products(): pl.pallas_call(far_kernel, out_shape=sent + [pltpu.HBM(z_shape, F32)] * 2...]
  transfers between devices with their start and end apart: 17 -> 17, of which waited for: 3 -> 2; matrix products, arithmetic and copies ran while one was open for 0% -> 0% of each run, Pallas kernels for 20% -> 25%
where the time goes in v4:
time: 86 us; the launch traced here: 85.6 us
  starting transfers between devices  35 us (41%)
  Pallas kernels  29.1 us (34%)
  blocking collectives  13.5 us (16%)
  waiting for transfers between devices  7.2 us (8%)
    ppermute x15, starting transfers between devices, moved(): lax.ppermute(x, axis, [(i, to(i)) for i in range(lax.axis_size(axis))])  22.4 us
    all_to_all x1, blocking collectives, on_device(): arrived = lax.all_to_all(placed, 'fcol', 0, 0, tiled=True)  13.5 us
    pallas_call x1, Pallas kernels, far_products(): pl.pallas_call(far_kernel, out_shape=sent + [pltpu.HBM(z_shape, F32)] * 2...  8.19 us
    all_to_all x1, starting transfers between devices, on_device(): mine = lax.all_to_all(packed, 'fcol', 0, 0, tiled=True)  8.1 us
    ppermute x15, waiting for transfers between devices, moved(): lax.ppermute(x, axis, [(i, to(i)) for i in range(lax.axis_size(axis))])  7.2 us
    pallas_call x1, Pallas kernels, near_products(): pl.pallas_call(near_kernel, out_shape=[pltpu.HBM(*s) for s in shapes], in...  6.19 us
    all_to_all x1, starting transfers between devices, on_device(): lax.all_to_all(out_y, 'frow', 0, 0, tiled=True, axis_index_groups=[[2 * i...  4.5 us
    pallas_call x1, Pallas kernels, place(): pl.pallas_call(place_kernel, out_shape=[jax.ShapeDtypeStruct((NY, *piece)...  4.16 us
  transfers between devices with their start and end apart: 17, of which 2 were waited for; matrix products, arithmetic and copies ran while one was open for 0% of the time, Pallas kernels for 25%

profile of v4, /device:TPU:0, one launch (start us, length us, event | category | flops | bytes accessed | tf_op | source)
XLA Modules:
  0.0 85.6 jit_solution(6128162730997207480)
XLA Ops:
  0.6 2.3 %pack.1.token = bf16[16,272,128]{2,1,0:T(8,128)(2,1)} custom-call(bf16[8,128,512]{2,1,0:T(8,128)(2,1)} %bitcast.14, s32[1,8]{1,0:T(1,128)} %bitcast.15, s32[1,8]{1,0:T(1,128)} %bitcast.16, s32[1,96]{1,0:T(1,128)} %pivots_hbm.1), custom_call_target="tpu_custom_call" | custom-call | bytes 2097152 | tf_op jit(solution)/shard_map/pack/pallas_call | solution.py:290
  3.0 0.0 copy-start
  3.0 8.1 %all-to-all-start = ((bf16[16,272,128]{2,1,0:T(8,128)(2,1)}), bf16[16,272,128]{2,1,0:T(8,128)(2,1)S(1)}, u32[]{:S(2)}, u32[]{:S(2)}) async-start(bf16[16,272,128]{2,1,0:T(8,128)(2,1)} %pack.1.token), calls=%async_computation | async-start | bytes 2228224 | tf_op jit(solution)/shard_map/all_to_all | solution.py:490
  11.1 0.0 copy-done
  11.1 8.2 %far.1 = (bf16[7,32,512]{2,1,0:T(8,128)(2,1)S(1)}, bf16[7,32,512]{2,1,0:T(8,128)(2,1)S(1)}, bf16[28,32,128]{2,1,0:T(8,128)(2,1)S(1)}, bf16[28,32,128]{2,1,0:T(8,...) custom-call(bf16[28,4,32,1792]{3,2,1,0:T(8,128)(2,1)} %bitcast.13, ...), custom_call_target="tpu_custom_call" | custom-call | flops 3288334336 | bytes 20185088 | tf_op jit(solution)/shard_map/far/pallas_call | solution.py:137
  19.3 2.0 %collective-permute-start = (bf16[7,32,512]{2,1,0:T(8,128)(2,1)S(1)}, bf16[7,32,512]{2,1,0:T(8,128)(2,1)S(1)}, u32[]{:S(2)}, u32[]{:S(2)}) collective-permute-start(bf16[7,32,512]{2,1,0:T(8,128)(2,1)S(1)} %get-tuple-element.55), channel_id=1, source_target_pairs={{0,4},{1,5},{2,6},{3,7},{4,8},{5,9},{6,10},{7,11},{8,12},{9,13},{1... | collective-permute-start | bytes 688136 | tf_op jit(solution)/shard_map/ppermute | solution.py:472
  21.3 1.3 %collective-permute-start.1 = (bf16[7,32,512]{2,1,0:T(8,128)(2,1)S(1)}, bf16[7,32,512]{2,1,0:T(8,128)(2,1)S(1)}, u32[]{:S(2)}, u32[]{:S(2)}) collective-permute-start(bf16[7,32,512]{2,1,0:T(8,128)(2,1)S(1)} %get-tuple-element.56), channel_id=1, source_target_pairs={{0,12},{1,13},{2,14},{3,15},{4,0},{5,1},{6,2},{7,3},{8,4},{9,5},{1... | collective-permute-start | bytes 688136 | tf_op jit(solution)/shard_map/ppermute | solution.py:472
  22.6 1.9 %collective-permute-start.2 = (bf16[28,32,128]{2,1,0:T(8,128)(2,1)S(1)}, bf16[28,32,128]{2,1,0:T(8,128)(2,1)S(1)}, u32[]{:S(2)}, u32[]{:S(2)}) collective-permute-start(bf16[28,32,128]{2,1,0:T(8,128)(2,1)S(1)} %get-tuple-element.61), channel_id=1, source_target_pairs={{0,1},{1,2},{2,3},{3,0},{4,5},{5,6},{6,7},{7,4},{8,9},{9,10},{10,1... | collective-permute-start | bytes 688136 | tf_op jit(solution)/shard_map/ppermute | solution.py:472
  24.5 1.3 %collective-permute-start.3 = (bf16[28,32,128]{2,1,0:T(8,128)(2,1)S(1)}, bf16[28,32,128]{2,1,0:T(8,128)(2,1)S(1)}, u32[]{:S(2)}, u32[]{:S(2)}) collective-permute-start(bf16[28,32,128]{2,1,0:T(8,128)(2,1)S(1)} %get-tuple-element.62), channel_id=1, source_target_pairs={{0,3},{1,0},{2,1},{3,2},{4,7},{5,4},{6,5},{7,6},{8,11},{9,8},{10,9... | collective-permute-start | bytes 688136 | tf_op jit(solution)/shard_map/ppermute | solution.py:472
  25.9 0.0 copy-start.1
  25.9 6.2 %near.1 = (f32[7,32,512]{2,1,0:T(8,128)}, bf16[7,32,512]{2,1,0:T(8,128)(2,1)}, bf16[7,32,512]{2,1,0:T(8,128)(2,1)}, f32[7,32,512]{2,1,0:T(8,128)}, f32[7,32,512]...) custom-call(bf16[3,14,32,1792]{3,2,1,0:T(8,128)(2,1)S(1)} %get-tuple, ...), custom_call_target="tpu_custom_call" | custom-call | flops 13153337344 | bytes 18350080 | tf_op jit(solution)/shard_map/near/pallas_call | solution.py:161
  32.1 0.0 collective-permute-done.xa
  32.1 0.0 collective-permute-done.1.xb
  32.1 0.7 collective-permute-done.2.za
  32.8 0.0 collective-permute-done.3.zb
  32.8 0.0 all-to-all-done._
  32.8 0.0 copy-done.1
  32.8 3.0 %relay.1 = (bf16[14,32,512]{2,1,0:T(8,128)(2,1)}, bf16[14,32,512]{2,1,0:T(8,128)(2,1)}, bf16[60,32,128]{2,1,0:T(8,128)(2,1)}, bf16[60,32,128]{2,1,0:T(8,128)(2,1)}, bf16[16,272,128]{2,1,0:T(8,128)(2,1)S(1)}) custom-call(f32[7,32,512]{2,1,0:T(8,128)} %get-tuple-element.51.hx1, f32[7,32,512]{2,1,0:T(8,128)} %get-tuple-element.52.hx3, ...), custom_call_target="tpu_custom_call", output_to_operand_aliasing={{4}: (13, {})} | custom-call | flops 458752 | bytes 3211264 | tf_op jit(solution)/shard_map/relay/pallas_call | solution.py:209
  35.9 0.1 collective-permute-start.6
  36.0 0.8 collective-permute-start.10
  36.7 2.6 %collective-permute-start.11 = (bf16[60,32,128]{2,1,0:T(8,128)(2,1)}, bf16[60,32,128]{2,1,0:T(8,128)(2,1)S(1)}, u32[]{:S(2)}, u32[]{:S(2)}) collective-permute-start(bf16[60,32,128]{2,1,0:T(8,128)(2,1)} %get-tuple-element.74), channel_id=1, source_target_pairs={{0,3},{1,0},{2,1},{3,2},{4,7},{5,4},{6,5},{7,6},{8,11},{9,8},{10,9... | collective-permute-start | bytes 1474568 | tf_op jit(solution)/shard_map/ppermute | solution.py:472
  39.3 0.2 collective-permute-start.4
  39.5 3.0 %collective-permute-start.5 = (bf16[14,32,512]{2,1,0:T(8,128)(2,1)}, bf16[14,32,512]{2,1,0:T(8,128)(2,1)S(1)}, u32[]{:S(2)}, u32[]{:S(2)}) collective-permute-start(bf16[14,32,512]{2,1,0:T(8,128)(2,1)} %get-tuple-element.64), channel_id=1, source_target_pairs={{0,12},{1,13},{2,14},{3,15},{4,0},{5,1},{6,2},{7,3},{8,4},{9,5},{1... | collective-permute-start | bytes 1376264 | tf_op jit(solution)/shard_map/ppermute | solution.py:472
  42.5 0.0 collective-permute-done.6.other
  42.5 4.2 %place.1 = (bf16[4,28,32,128]{3,2,1,0:T(8,128)(2,1)}, f32[28,32,128]{2,1,0:T(8,128)}, s32[2,128]{1,0:T(2,128)S(1)}) custom-call(bf16[16,272,128]{2,1,0:T(8,128)(2,1)S(1)} %get-tuple-element.65.mine, bf16[16,272,128]{2,1,0:T(8,128)(2,1)S(1)} %collective-permute-done.6.other), custom_call_target="tpu_custom_call" | custom-call | flops 8912896 | bytes 4456448 | tf_op jit(solution)/shard_map/place/pallas_call | solution.py:340
  46.7 4.5 %all-to-all-start.1 = ((bf16[4,28,32,128]{3,2,1,0:T(8,128)(2,1)}), bf16[4,28,32,128]{3,2,1,0:T(8,128)(2,1)S(1)}, u32[]{:S(2)}, u32[]{:S(2)}) async-start(bf16[4,28,32,128]{3,2,1,0:T(8,128)(2,1)} %get-tuple-element.80), calls=%async_computation.1 | async-start | bytes 1835008 | tf_op jit(solution)/shard_map/all_to_all | solution.py:505
  51.2 0.0 collective-permute-done.10.r1
  51.2 0.0 collective-permute-done.11.r2
  51.2 1.3 %sum_z.1 = (f32[14,32,128]{2,1,0:T(8,128)S(1)}, bf16[14,32,128]{2,1,0:T(8,128)(2,1)S(1)}, f32[14,32,128]{2,1,0:T(8,128)S(1)}, f32[14,32,128]{2,1,0:T(8,128)S(1)}, bf16[64,256]{1,0:T(8,128)(2,1)S(1)}) custom-call(f32[28,32,128]{2,1,0:T(8,128)} %get-tuple-element.71.low, f32[28,32,128]{2,1,0:T(8,128)} %get-tuple-element.72.high, ...), custom_call_target="tpu_custom_call" | custom-call | flops 688128 | bytes 3211264 | tf_op jit(solution)/shard_map/sum_z/pallas_call | solution.py:251
  52.5 1.5 %collective-permute-start.13 = (bf16[14,32,128]{2,1,0:T(8,128)(2,1)S(1)}, bf16[14,32,128]{2,1,0:T(8,128)(2,1)S(1)}, u32[]{:S(2)}, u32[]{:S(2)}) collective-permute-start(bf16[14,32,128]{2,1,0:T(8,128)(2,1)S(1)} %get-tuple-element.77), channel_id=1, source_target_pairs={{0,8},{1,9},{2,10},{3,11},{4,12},{5,13},{6,14},{7,15},{8,0},{9,1},... | collective-permute-start | bytes 344072 | tf_op jit(solution)/shard_map/ppermute | solution.py:472
  54.0 0.6 collective-permute-start.12
  54.6 2.7 %collective-permute-start.14 = (f32[14,32,128]{2,1,0:T(8,128)S(1)}, f32[14,32,128]{2,1,0:T(8,128)S(1)}, u32[]{:S(2)}, u32[]{:S(2)}) collective-permute-start(f32[14,32,128]{2,1,0:T(8,128)S(1)} %get-tuple-element.78), channel_id=1, source_target_pairs={{0,12},{1,13},{2,14},{3,15},{4,0},{5,1},{6,2},{7,3},{8,4},{9,5},{1... | collective-permute-start | bytes 688136 | tf_op jit(solution)/shard_map/ppermute | solution.py:472
  57.2 0.0 collective-permute-done.4.r1
  57.2 0.0 collective-permute-done.5.r2
  57.2 1.3 %sum_x.1 = (f32[14,32,128]{2,1,0:T(8,128)S(1)}, bf16[14,32,128]{2,1,0:T(8,128)(2,1)S(1)}, f32[14,32,128]{2,1,0:T(8,128)S(1)}, f32[14,32,128]{2,1,0:T(8,128)S(1)}) custom-call(f32[7,32,512]{2,1,0:T(8,128)} %get-tuple-element.49.low, f32[7,32,512]{2,1,0:T(8,128)} %get-tuple-element.50.high, bf16[14,32,512]{2,1,0:T(8,128)(2,1)S(1)} %collective-permute-done.4.r1, ...), custom_call_target="tpu_custom_call" | custom-call | flops 688128 | bytes 3211264 | tf_op jit(solution)/shard_map/sum_x/pallas_call | solution.py:251
  58.5 1.2 %collective-permute-start.7 = (f32[14,32,128]{2,1,0:T(8,128)S(1)}, f32[14,32,128]{2,1,0:T(8,128)S(1)}, u32[]{:S(2)}, u32[]{:S(2)}) collective-permute-start(f32[14,32,128]{2,1,0:T(8,128)S(1)} %get-tuple-element.68), channel_id=1, source_target_pairs={{0,1},{1,2},{2,3},{3,0},{4,5},{5,6},{6,7},{7,4},{8,9},{9,10},{10,1... | collective-permute-start | bytes 688136 | tf_op jit(solution)/shard_map/ppermute | solution.py:472
  59.7 2.1 %collective-permute-start.9 = (f32[14,32,128]{2,1,0:T(8,128)S(1)}, f32[14,32,128]{2,1,0:T(8,128)S(1)}, u32[]{:S(2)}, u32[]{:S(2)}) collective-permute-start(f32[14,32,128]{2,1,0:T(8,128)S(1)} %get-tuple-element.70), channel_id=1, source_target_pairs={{0,3},{1,0},{2,1},{3,2},{4,7},{5,4},{6,5},{7,6},{8,11},{9,8},{10,9... | collective-permute-start | bytes 688136 | tf_op jit(solution)/shard_map/ppermute | solution.py:472
  61.8 0.0 collective-permute-done.13.refs_6_
  61.8 1.2 %collective-permute-start.8 = (bf16[14,32,128]{2,1,0:T(8,128)(2,1)S(1)}, bf16[14,32,128]{2,1,0:T(8,128)(2,1)S(1)}, u32[]{:S(2)}, u32[]{:S(2)}) collective-permute-start(bf16[14,32,128]{2,1,0:T(8,128)(2,1)S(1)} %get-tuple-element.69), channel_id=1, source_target_pairs={{0,2},{1,3},{2,0},{3,1},{4,6},{5,7},{6,4},{7,5},{8,10},{9,11},{10,... | collective-permute-start | bytes 344072 | tf_op jit(solution)/shard_map/ppermute | solution.py:472
  63.0 6.4 %collective-permute-done.8.refs_2_ = bf16[14,32,128]{2,1,0:T(8,128)(2,1)S(1)} collective-permute-done((bf16[14,32,128]{2,1,0:T(8,128)(2,1)S(1)}, bf16[14,32,128]{2,1,0:T(8,128)(2,1)S(1)}, u32[]{:S(2)}, u32[]{:S(2)}) %collective-permute-start.8) | collective-permute-done | bytes 114720 | tf_op jit(solution)/shard_map/ppermute | solution.py:472
  69.4 0.0 collective-permute-done.12.refs_5_
  69.4 0.0 collective-permute-done.14.refs_7_
  69.4 0.0 collective-permute-done.7.refs_1_
  69.4 0.0 collective-permute-done.9.refs_3_
  69.4 0.0 all-to-all-done.1.refs_9_
  69.5 0.0 copy-start.2
  69.5 0.0 copy-start.3
  69.5 1.4 %finish.1 = bf16[16,2,2,32,128]{4,3,2,1,0:T(8,128)(2,1)S(1)} custom-call(f32[14,32,128]{2,1,0:T(8,128)S(1)} %get-tuple-element.67.refs_0_, f32[14,32,128]{2,1,0:T(8,128)S(1)} %collective-permute-done.7.refs_1_, bf16[14,32,128]{2,1,0:T(8,128)(2,1)S(1)} %collective-permute-done.8.refs_2_, f32[14,32,128]{2,1,0:T(8,128)S(1)} %collective-permute-done.9.refs_3_, ...), custom_call_target="tpu_custom_call" | custom-call | flops 917504 | bytes 3440640 | tf_op jit(solution)/shard_map/finish/pallas_call | solution.py:390
  70.9 13.5 %all_to_all.15.arrived = bf16[16,2,2,32,128]{4,3,2,1,0:T(8,128)(2,1)S(1)} all-to-all(bf16[16,2,2,32,128]{4,3,2,1,0:T(8,128)(2,1)S(1)} %finish.1), channel_id=1, replica_groups=mesh['frow'=8,'fcol'=16] {'fcol'}, dimensions={0} | all-to-all | bytes 1048576 | tf_op jit(solution)/shard_map/all_to_all | solution.py:518
  84.4 0.0 copy-done.2
  84.4 0.0 copy-done.3
  84.4 1.2 %tail.1 = (bf16[224,512]{1,0:T(8,128)(2,1)}, f32[96,224]{1,0:T(8,128)}, f32[64,96]{1,0:T(8,128)}, bf16[32,512]{1,0:T(8,128)(2,1)}) custom-call(bf16[16,2,2,32,128]{4,3,2,1,0:T(8,128)(2,1)S(1)} %all_to_all.15.arrived, bf16[96,512]{1,0:T(8,128)(2,1)S(1)} %bitcast.11, bf16[64,256]{1,0:T(8,128)(2,1)S(1)} %bitcast.10, ...), custom_call_target="tpu_custom_call" | custom-call | flops 75497472 | bytes 786432 | tf_op jit(solution)/shard_map/tail/pallas_call | solution.py:456
Async XLA Ops:
  3.0 8.1 %copy-start = (bf16[16,272,128]{2,1,0:T(8,128)(2,1)S(1)}, bf16[16,272,128]{2,1,0:T(8,128)(2,1)}, u32[]{:S(2)}) copy-start(bf16[16,272,128]{2,1,0:T(8,128)(2,1)} %pack.1.token) | copy-start | bytes 3342340
  3.0 29.8 %all-to-all-start = ((bf16[16,272,128]{2,1,0:T(8,128)(2,1)}), bf16[16,272,128]{2,1,0:T(8,128)(2,1)S(1)}, u32[]{:S(2)}, u32[]{:S(2)}) async-start(bf16[16,272,128]{2,1,0:T(8,128)(2,1)} %pack.1.token), calls=%async_computation | async-start | bytes 2228224 | tf_op jit(solution)/shard_map/all_to_all | solution.py:490
  19.3 12.7 %collective-permute-start = (bf16[7,32,512]{2,1,0:T(8,128)(2,1)S(1)}, bf16[7,32,512]{2,1,0:T(8,128)(2,1)S(1)}, u32[]{:S(2)}, u32[]{:S(2)}) collective-permute-start(bf16[7,32,512]{2,1,0:T(8,128)(2,1)S(1)} %get-tuple-element.55), channel_id=1, source_target_pairs={{0,4},{1,5},{2,6},{3,7},{4,8},{5,9},{6,10},{7,11},{8,12},{9,13},{1... | collective-permute-start | bytes 688136 | tf_op jit(solution)/shard_map/ppermute | solution.py:472
  21.3 10.8 %collective-permute-start.1 = (bf16[7,32,512]{2,1,0:T(8,128)(2,1)S(1)}, bf16[7,32,512]{2,1,0:T(8,128)(2,1)S(1)}, u32[]{:S(2)}, u32[]{:S(2)}) collective-permute-start(bf16[7,32,512]{2,1,0:T(8,128)(2,1)S(1)} %get-tuple-element.56), channel_id=1, source_target_pairs={{0,12},{1,13},{2,14},{3,15},{4,0},{5,1},{6,2},{7,3},{8,4},{9,5},{1... | collective-permute-start | bytes 688136 | tf_op jit(solution)/shard_map/ppermute | solution.py:472
  22.6 10.2 %collective-permute-start.2 = (bf16[28,32,128]{2,1,0:T(8,128)(2,1)S(1)}, bf16[28,32,128]{2,1,0:T(8,128)(2,1)S(1)}, u32[]{:S(2)}, u32[]{:S(2)}) collective-permute-start(bf16[28,32,128]{2,1,0:T(8,128)(2,1)S(1)} %get-tuple-element.61), channel_id=1, source_target_pairs={{0,1},{1,2},{2,3},{3,0},{4,5},{5,6},{6,7},{7,4},{8,9},{9,10},{10,1... | collective-permute-start | bytes 688136 | tf_op jit(solution)/shard_map/ppermute | solution.py:472
  24.5 8.3 %collective-permute-start.3 = (bf16[28,32,128]{2,1,0:T(8,128)(2,1)S(1)}, bf16[28,32,128]{2,1,0:T(8,128)(2,1)S(1)}, u32[]{:S(2)}, u32[]{:S(2)}) collective-permute-start(bf16[28,32,128]{2,1,0:T(8,128)(2,1)S(1)} %get-tuple-element.62), channel_id=1, source_target_pairs={{0,3},{1,0},{2,1},{3,2},{4,7},{5,4},{6,5},{7,6},{8,11},{9,8},{10,9... | collective-permute-start | bytes 688136 | tf_op jit(solution)/shard_map/ppermute | solution.py:472
  25.9 7.0 %copy-start.1 = (bf16[256,64]{0,1:T(8,128)(2,1)S(1)}, bf16[256,64]{0,1:T(8,128)(2,1)}, u32[]{:S(2)}) copy-start(bf16[256,64]{0,1:T(8,128)(2,1)} %param.15) | copy-start | bytes 98308
  35.9 6.6 %collective-permute-start.6 = (bf16[16,272,128]{2,1,0:T(8,128)(2,1)S(1)}, bf16[16,272,128]{2,1,0:T(8,128)(2,1)S(1)}, u32[]{:S(2)}, u32[]{:S(2)}) collective-permute-start(bf16[16,272,128]{2,1,0:T(8,128)(2,1)S(1)} %get-tuple-element.65.mine), channel_id=1, source_target_pairs={{0,16},{16,0},{32,48},{48,32},{64,80},{80,64},{96,112},{112,96},{1... | collective-permute-start | bytes 3342344 | tf_op jit(solution)/shard_map/ppermute | solution.py:472
  36.0 15.2 %collective-permute-start.10 = (bf16[60,32,128]{2,1,0:T(8,128)(2,1)}, bf16[60,32,128]{2,1,0:T(8,128)(2,1)S(1)}, u32[]{:S(2)}, u32[]{:S(2)}) collective-permute-start(bf16[60,32,128]{2,1,0:T(8,128)(2,1)} %get-tuple-element.73), channel_id=1, source_target_pairs={{0,1},{1,2},{2,3},{3,0},{4,5},{5,6},{6,7},{7,4},{8,9},{9,10},{10,1... | collective-permute-start | bytes 1474568 | tf_op jit(solution)/shard_map/ppermute | solution.py:472
  36.7 14.5 %collective-permute-start.11 = (bf16[60,32,128]{2,1,0:T(8,128)(2,1)}, bf16[60,32,128]{2,1,0:T(8,128)(2,1)S(1)}, u32[]{:S(2)}, u32[]{:S(2)}) collective-permute-start(bf16[60,32,128]{2,1,0:T(8,128)(2,1)} %get-tuple-element.74), channel_id=1, source_target_pairs={{0,3},{1,0},{2,1},{3,2},{4,7},{5,4},{6,5},{7,6},{8,11},{9,8},{10,9... | collective-permute-start | bytes 1474568 | tf_op jit(solution)/shard_map/ppermute | solution.py:472
  39.3 18.0 %collective-permute-start.4 = (bf16[14,32,512]{2,1,0:T(8,128)(2,1)}, bf16[14,32,512]{2,1,0:T(8,128)(2,1)S(1)}, u32[]{:S(2)}, u32[]{:S(2)}) collective-permute-start(bf16[14,32,512]{2,1,0:T(8,128)(2,1)} %get-tuple-element.63), channel_id=1, source_target_pairs={{0,4},{1,5},{2,6},{3,7},{4,8},{5,9},{6,10},{7,11},{8,12},{9,13},{1... | collective-permute-start | bytes 1376264 | tf_op jit(solution)/shard_map/ppermute | solution.py:472
  39.5 17.7 %collective-permute-start.5 = (bf16[14,32,512]{2,1,0:T(8,128)(2,1)}, bf16[14,32,512]{2,1,0:T(8,128)(2,1)S(1)}, u32[]{:S(2)}, u32[]{:S(2)}) collective-permute-start(bf16[14,32,512]{2,1,0:T(8,128)(2,1)} %get-tuple-element.64), channel_id=1, source_target_pairs={{0,12},{1,13},{2,14},{3,15},{4,0},{5,1},{6,2},{7,3},{8,4},{9,5},{1... | collective-permute-start | bytes 1376264 | tf_op jit(solution)/shard_map/ppermute | solution.py:472
  46.7 22.8 %all-to-all-start.1 = ((bf16[4,28,32,128]{3,2,1,0:T(8,128)(2,1)}), bf16[4,28,32,128]{3,2,1,0:T(8,128)(2,1)S(1)}, u32[]{:S(2)}, u32[]{:S(2)}) async-start(bf16[4,28,32,128]{3,2,1,0:T(8,128)(2,1)} %get-tuple-element.80), calls=%async_computation.1 | async-start | bytes 1835008 | tf_op jit(solution)/shard_map/all_to_all | solution.py:505
  52.5 9.3 %collective-permute-start.13 = (bf16[14,32,128]{2,1,0:T(8,128)(2,1)S(1)}, bf16[14,32,128]{2,1,0:T(8,128)(2,1)S(1)}, u32[]{:S(2)}, u32[]{:S(2)}) collective-permute-start(bf16[14,32,128]{2,1,0:T(8,128)(2,1)S(1)} %get-tuple-element.77), channel_id=1, source_target_pairs={{0,8},{1,9},{2,10},{3,11},{4,12},{5,13},{6,14},{7,15},{8,0},{9,1},... | collective-permute-start | bytes 344072 | tf_op jit(solution)/shard_map/ppermute | solution.py:472
  54.0 15.4 %collective-permute-start.12 = (f32[14,32,128]{2,1,0:T(8,128)S(1)}, f32[14,32,128]{2,1,0:T(8,128)S(1)}, u32[]{:S(2)}, u32[]{:S(2)}) collective-permute-start(f32[14,32,128]{2,1,0:T(8,128)S(1)} %get-tuple-element.76), channel_id=1, source_target_pairs={{0,4},{1,5},{2,6},{3,7},{4,8},{5,9},{6,10},{7,11},{8,12},{9,13},{1... | collective-permute-start | bytes 688136 | tf_op jit(solution)/shard_map/ppermute | solution.py:472
  54.6 14.9 %collective-permute-start.14 = (f32[14,32,128]{2,1,0:T(8,128)S(1)}, f32[14,32,128]{2,1,0:T(8,128)S(1)}, u32[]{:S(2)}, u32[]{:S(2)}) collective-permute-start(f32[14,32,128]{2,1,0:T(8,128)S(1)} %get-tuple-element.78), channel_id=1, source_target_pairs={{0,12},{1,13},{2,14},{3,15},{4,0},{5,1},{6,2},{7,3},{8,4},{9,5},{1... | collective-permute-start | bytes 688136 | tf_op jit(solution)/shard_map/ppermute | solution.py:472
  58.5 10.9 %collective-permute-start.7 = (f32[14,32,128]{2,1,0:T(8,128)S(1)}, f32[14,32,128]{2,1,0:T(8,128)S(1)}, u32[]{:S(2)}, u32[]{:S(2)}) collective-permute-start(f32[14,32,128]{2,1,0:T(8,128)S(1)} %get-tuple-element.68), channel_id=1, source_target_pairs={{0,1},{1,2},{2,3},{3,0},{4,5},{5,6},{6,7},{7,4},{8,9},{9,10},{10,1... | collective-permute-start | bytes 688136 | tf_op jit(solution)/shard_map/ppermute | solution.py:472
  59.7 9.8 %collective-permute-start.9 = (f32[14,32,128]{2,1,0:T(8,128)S(1)}, f32[14,32,128]{2,1,0:T(8,128)S(1)}, u32[]{:S(2)}, u32[]{:S(2)}) collective-permute-start(f32[14,32,128]{2,1,0:T(8,128)S(1)} %get-tuple-element.70), channel_id=1, source_target_pairs={{0,3},{1,0},{2,1},{3,2},{4,7},{5,4},{6,5},{7,6},{8,11},{9,8},{10,9... | collective-permute-start | bytes 688136 | tf_op jit(solution)/shard_map/ppermute | solution.py:472
  61.8 7.6 %collective-permute-start.8 = (bf16[14,32,128]{2,1,0:T(8,128)(2,1)S(1)}, bf16[14,32,128]{2,1,0:T(8,128)(2,1)S(1)}, u32[]{:S(2)}, u32[]{:S(2)}) collective-permute-start(bf16[14,32,128]{2,1,0:T(8,128)(2,1)S(1)} %get-tuple-element.69), channel_id=1, source_target_pairs={{0,2},{1,3},{2,0},{3,1},{4,6},{5,7},{6,4},{7,5},{8,10},{9,11},{10,... | collective-permute-start | bytes 344072 | tf_op jit(solution)/shard_map/ppermute | solution.py:472
  69.5 14.9 %copy-start.2 = (bf16[512,96]{0,1:T(8,128)(2,1)S(1)}, bf16[512,96]{0,1:T(8,128)(2,1)}, u32[]{:S(2)}) copy-start(bf16[512,96]{0,1:T(8,128)(2,1)} %param.14) | copy-start | bytes 294916
  69.5 14.9 %copy-start.3 = (s32[1,32]{1,0:T(1,128)S(1)}, s32[1,32]{1,0:T(1,128)}, u32[]{:S(2)}) copy-start(s32[1,32]{1,0:T(1,128)} %piv_parent.1) | copy-start | bytes 388

commit v5 on v4

--- a/solution.py
+++ b/solution.py
@@ -304,7 +304,7 @@
     )(child, group, block, pivots)
 
 
-def place_kernel(mine, other, out, own, pivots, total, facts, told, slots, sems):
+def place_kernel(mine, other, out, own, pivots, total, kept, facts, told, slots, sems):
     pos = place_in_mesh()
     blocks = out.shape[1]
     sources = mine.shape[0]
@@ -320,17 +320,20 @@
     pivots[...] = told[pl.ds(pos[2] // 2 * 2, 2), 1].astype(jnp.int32)
     total[...] = jnp.zeros_like(total)
     copy.wait()
-    for t, ref in ((0, mine), (1, other)):
-        def body(i, _, t=t, ref=ref):
-            for j in range(CBD):
-                at = slots[t * sources + i, j]
-                total[at] += ref[i, j * UNIT : (j + 1) * UNIT].astype(F32)
-            return _
-
-        lax.fori_loop(0, sources, body, 0)
-    keep = pltpu.make_async_copy(total.at[pl.ds(pos[3] * blocks, blocks)], own, sems.at[0])
+
+    def body(i, carry):
+        for j in range(CBD):
+            for t, ref in ((0, mine), (1, other)):
+                total[t, slots[t * sources + i, j]] += ref[i, j * UNIT : (j + 1) * UNIT].astype(F32)
+        return carry
+
+    lax.fori_loop(0, sources, body, 0)
+    span = pl.ds(pos[3] * blocks, blocks)
+    kept[...] = total[0, span] + total[1, span]
+    keep = pltpu.make_async_copy(kept, own, sems.at[0])
     keep.start()
-    out[...] = total[: NY * blocks].reshape(out.shape).astype(BF16)
+    places = NY * blocks
+    out[...] = (total[0, :places] + total[1, :places]).reshape(out.shape).astype(BF16)
     keep.wait()
 
 
@@ -347,7 +350,8 @@
         in_specs=[LOCAL] * 2,
         out_specs=[LOCAL, REMAIN, LOCAL],
         scratch_shapes=[
-            pltpu.VMEM((NY * blocks + 1, UNIT, COLS), F32),
+            pltpu.VMEM((2, NY * blocks + 1, UNIT, COLS), F32),
+            pltpu.VMEM(piece, F32),
             pltpu.VMEM((2 * sources, COLS), jnp.int32),
             pltpu.VMEM((2 * sources, TOLD, COLS), F32),
             pltpu.SMEM((2 * sources, COLS), jnp.int32),

time: 86 us -> 86 us (level)
  no operation moved by 1% of the time
where the time goes in v5:
time: 86 us; the launch traced here: 85.6 us
  starting transfers between devices  35.1 us (41%)
  Pallas kernels  29 us (34%)
  blocking collectives  13.5 us (16%)
  waiting for transfers between devices  7.2 us (8%)
    ppermute x15, starting transfers between devices, moved(): lax.ppermute(x, axis, [(i, to(i)) for i in range(lax.axis_size(axis))])  22.5 us
    all_to_all x1, blocking collectives, on_device(): arrived = lax.all_to_all(placed, 'fcol', 0, 0, tiled=True)  13.5 us
    pallas_call x1, Pallas kernels, far_products(): pl.pallas_call(far_kernel, out_shape=sent + [pltpu.HBM(z_shape, F32)] * 2...  8.19 us
    all_to_all x1, starting transfers between devices, on_device(): mine = lax.all_to_all(packed, 'fcol', 0, 0, tiled=True)  8.1 us
    ppermute x15, waiting for transfers between devices, moved(): lax.ppermute(x, axis, [(i, to(i)) for i in range(lax.axis_size(axis))])  7.2 us
    pallas_call x1, Pallas kernels, near_products(): pl.pallas_call(near_kernel, out_shape=[pltpu.HBM(*s) for s in shapes], in...  6.19 us
    all_to_all x1, starting transfers between devices, on_device(): lax.all_to_all(out_y, 'frow', 0, 0, tiled=True, axis_index_groups=[[2 * i...  4.47 us
    pallas_call x1, Pallas kernels, place(): pl.pallas_call(place_kernel, out_shape=[jax.ShapeDtypeStruct((NY, *piece)...  4.07 us
  transfers between devices with their start and end apart: 17, of which 2 were waited for; matrix products, arithmetic and copies ran while one was open for 0% of the time, Pallas kernels for 25%

profile of v5, /device:TPU:0, one launch (start us, length us, event | category | flops | bytes accessed | tf_op | source)
XLA Modules:
  0.0 85.6 jit_solution(3538783629153154659)
XLA Ops:
  0.6 2.3 %pack.1.token = bf16[16,272,128]{2,1,0:T(8,128)(2,1)} custom-call(bf16[8,128,512]{2,1,0:T(8,128)(2,1)} %bitcast.14, s32[1,8]{1,0:T(1,128)} %bitcast.15, s32[1,8]{1,0:T(1,128)} %bitcast.16, s32[1,96]{1,0:T(1,128)} %pivots_hbm.1), custom_call_target="tpu_custom_call" | custom-call | bytes 2097152 | tf_op jit(solution)/shard_map/pack/pallas_call | solution.py:290
  3.0 0.0 copy-start
  3.0 8.1 %all-to-all-start = ((bf16[16,272,128]{2,1,0:T(8,128)(2,1)}), bf16[16,272,128]{2,1,0:T(8,128)(2,1)S(1)}, u32[]{:S(2)}, u32[]{:S(2)}) async-start(bf16[16,272,128]{2,1,0:T(8,128)(2,1)} %pack.1.token), calls=%async_computation | async-start | bytes 2228224 | tf_op jit(solution)/shard_map/all_to_all | solution.py:494
  11.1 0.0 copy-done
  11.1 8.2 %far.1 = (bf16[7,32,512]{2,1,0:T(8,128)(2,1)S(1)}, bf16[7,32,512]{2,1,0:T(8,128)(2,1)S(1)}, bf16[28,32,128]{2,1,0:T(8,128)(2,1)S(1)}, bf16[28,32,128]{2,1,0:T(8,...) custom-call(bf16[28,4,32,1792]{3,2,1,0:T(8,128)(2,1)} %bitcast.13, ...), custom_call_target="tpu_custom_call" | custom-call | flops 3288334336 | bytes 20185088 | tf_op jit(solution)/shard_map/far/pallas_call | solution.py:137
  19.3 2.0 %collective-permute-start = (bf16[7,32,512]{2,1,0:T(8,128)(2,1)S(1)}, bf16[7,32,512]{2,1,0:T(8,128)(2,1)S(1)}, u32[]{:S(2)}, u32[]{:S(2)}) collective-permute-start(bf16[7,32,512]{2,1,0:T(8,128)(2,1)S(1)} %get-tuple-element.55), channel_id=1, source_target_pairs={{0,4},{1,5},{2,6},{3,7},{4,8},{5,9},{6,10},{7,11},{8,12},{9,13},{1... | collective-permute-start | bytes 688136 | tf_op jit(solution)/shard_map/ppermute | solution.py:476
  21.3 1.3 %collective-permute-start.1 = (bf16[7,32,512]{2,1,0:T(8,128)(2,1)S(1)}, bf16[7,32,512]{2,1,0:T(8,128)(2,1)S(1)}, u32[]{:S(2)}, u32[]{:S(2)}) collective-permute-start(bf16[7,32,512]{2,1,0:T(8,128)(2,1)S(1)} %get-tuple-element.56), channel_id=1, source_target_pairs={{0,12},{1,13},{2,14},{3,15},{4,0},{5,1},{6,2},{7,3},{8,4},{9,5},{1... | collective-permute-start | bytes 688136 | tf_op jit(solution)/shard_map/ppermute | solution.py:476
  22.6 1.9 %collective-permute-start.2 = (bf16[28,32,128]{2,1,0:T(8,128)(2,1)S(1)}, bf16[28,32,128]{2,1,0:T(8,128)(2,1)S(1)}, u32[]{:S(2)}, u32[]{:S(2)}) collective-permute-start(bf16[28,32,128]{2,1,0:T(8,128)(2,1)S(1)} %get-tuple-element.61), channel_id=1, source_target_pairs={{0,1},{1,2},{2,3},{3,0},{4,5},{5,6},{6,7},{7,4},{8,9},{9,10},{10,1... | collective-permute-start | bytes 688136 | tf_op jit(solution)/shard_map/ppermute | solution.py:476
  24.5 1.3 %collective-permute-start.3 = (bf16[28,32,128]{2,1,0:T(8,128)(2,1)S(1)}, bf16[28,32,128]{2,1,0:T(8,128)(2,1)S(1)}, u32[]{:S(2)}, u32[]{:S(2)}) collective-permute-start(bf16[28,32,128]{2,1,0:T(8,128)(2,1)S(1)} %get-tuple-element.62), channel_id=1, source_target_pairs={{0,3},{1,0},{2,1},{3,2},{4,7},{5,4},{6,5},{7,6},{8,11},{9,8},{10,9... | collective-permute-start | bytes 688136 | tf_op jit(solution)/shard_map/ppermute | solution.py:476
  25.9 0.0 copy-start.1
  25.9 6.2 %near.1 = (f32[7,32,512]{2,1,0:T(8,128)}, bf16[7,32,512]{2,1,0:T(8,128)(2,1)}, bf16[7,32,512]{2,1,0:T(8,128)(2,1)}, f32[7,32,512]{2,1,0:T(8,128)}, f32[7,32,512]...) custom-call(bf16[3,14,32,1792]{3,2,1,0:T(8,128)(2,1)S(1)} %get-tuple, ...), custom_call_target="tpu_custom_call" | custom-call | flops 13153337344 | bytes 18350080 | tf_op jit(solution)/shard_map/near/pallas_call | solution.py:161
  32.1 0.0 collective-permute-done.xa
  32.1 0.0 collective-permute-done.1.xb
  32.1 0.7 collective-permute-done.2.za
  32.8 0.0 collective-permute-done.3.zb
  32.8 0.0 all-to-all-done._
  32.8 0.0 copy-done.1
  32.8 3.0 %relay.1 = (bf16[14,32,512]{2,1,0:T(8,128)(2,1)}, bf16[14,32,512]{2,1,0:T(8,128)(2,1)}, bf16[60,32,128]{2,1,0:T(8,128)(2,1)}, bf16[60,32,128]{2,1,0:T(8,128)(2,1)}, bf16[16,272,128]{2,1,0:T(8,128)(2,1)S(1)}) custom-call(f32[7,32,512]{2,1,0:T(8,128)} %get-tuple-element.51.hx1, f32[7,32,512]{2,1,0:T(8,128)} %get-tuple-element.52.hx3, ...), custom_call_target="tpu_custom_call", output_to_operand_aliasing={{4}: (13, {})} | custom-call | flops 458752 | bytes 3211264 | tf_op jit(solution)/shard_map/relay/pallas_call | solution.py:209
  35.9 0.1 collective-permute-start.6
  36.0 0.8 collective-permute-start.10
  36.7 2.6 %collective-permute-start.11 = (bf16[60,32,128]{2,1,0:T(8,128)(2,1)}, bf16[60,32,128]{2,1,0:T(8,128)(2,1)S(1)}, u32[]{:S(2)}, u32[]{:S(2)}) collective-permute-start(bf16[60,32,128]{2,1,0:T(8,128)(2,1)} %get-tuple-element.74), channel_id=1, source_target_pairs={{0,3},{1,0},{2,1},{3,2},{4,7},{5,4},{6,5},{7,6},{8,11},{9,8},{10,9... | collective-permute-start | bytes 1474568 | tf_op jit(solution)/shard_map/ppermute | solution.py:476
  39.3 0.2 collective-permute-start.4
  39.5 3.0 %collective-permute-start.5 = (bf16[14,32,512]{2,1,0:T(8,128)(2,1)}, bf16[14,32,512]{2,1,0:T(8,128)(2,1)S(1)}, u32[]{:S(2)}, u32[]{:S(2)}) collective-permute-start(bf16[14,32,512]{2,1,0:T(8,128)(2,1)} %get-tuple-element.64), channel_id=1, source_target_pairs={{0,12},{1,13},{2,14},{3,15},{4,0},{5,1},{6,2},{7,3},{8,4},{9,5},{1... | collective-permute-start | bytes 1376264 | tf_op jit(solution)/shard_map/ppermute | solution.py:476
  42.5 0.0 collective-permute-done.6.other
  42.5 4.1 %place.1 = (bf16[4,28,32,128]{3,2,1,0:T(8,128)(2,1)}, f32[28,32,128]{2,1,0:T(8,128)}, s32[2,128]{1,0:T(2,128)S(1)}) custom-call(bf16[16,272,128]{2,1,0:T(8,128)(2,1)S(1)} %get-tuple-element.65.mine, bf16[16,272,128]{2,1,0:T(8,128)(2,1)S(1)} %collective-permute-done.6.other), custom_call_target="tpu_custom_call" | custom-call | flops 8912896 | bytes 4456448 | tf_op jit(solution)/shard_map/place/pallas_call | solution.py:343
  46.6 4.5 %all-to-all-start.1 = ((bf16[4,28,32,128]{3,2,1,0:T(8,128)(2,1)}), bf16[4,28,32,128]{3,2,1,0:T(8,128)(2,1)S(1)}, u32[]{:S(2)}, u32[]{:S(2)}) async-start(bf16[4,28,32,128]{3,2,1,0:T(8,128)(2,1)} %get-tuple-element.80), calls=%async_computation.1 | async-start | bytes 1835008 | tf_op jit(solution)/shard_map/all_to_all | solution.py:509
  51.1 0.0 collective-permute-done.10.r1
  51.1 0.0 collective-permute-done.11.r2
  51.1 1.3 %sum_z.1 = (f32[14,32,128]{2,1,0:T(8,128)S(1)}, bf16[14,32,128]{2,1,0:T(8,128)(2,1)S(1)}, f32[14,32,128]{2,1,0:T(8,128)S(1)}, f32[14,32,128]{2,1,0:T(8,128)S(1)}, bf16[64,256]{1,0:T(8,128)(2,1)S(1)}) custom-call(f32[28,32,128]{2,1,0:T(8,128)} %get-tuple-element.71.low, f32[28,32,128]{2,1,0:T(8,128)} %get-tuple-element.72.high, ...), custom_call_target="tpu_custom_call" | custom-call | flops 688128 | bytes 3211264 | tf_op jit(solution)/shard_map/sum_z/pallas_call | solution.py:251
  52.4 1.6 %collective-permute-start.13 = (bf16[14,32,128]{2,1,0:T(8,128)(2,1)S(1)}, bf16[14,32,128]{2,1,0:T(8,128)(2,1)S(1)}, u32[]{:S(2)}, u32[]{:S(2)}) collective-permute-start(bf16[14,32,128]{2,1,0:T(8,128)(2,1)S(1)} %get-tuple-element.77), channel_id=1, source_target_pairs={{0,8},{1,9},{2,10},{3,11},{4,12},{5,13},{6,14},{7,15},{8,0},{9,1},... | collective-permute-start | bytes 344072 | tf_op jit(solution)/shard_map/ppermute | solution.py:476
  54.0 0.6 collective-permute-start.12
  54.6 2.7 %collective-permute-start.14 = (f32[14,32,128]{2,1,0:T(8,128)S(1)}, f32[14,32,128]{2,1,0:T(8,128)S(1)}, u32[]{:S(2)}, u32[]{:S(2)}) collective-permute-start(f32[14,32,128]{2,1,0:T(8,128)S(1)} %get-tuple-element.78), channel_id=1, source_target_pairs={{0,12},{1,13},{2,14},{3,15},{4,0},{5,1},{6,2},{7,3},{8,4},{9,5},{1... | collective-permute-start | bytes 688136 | tf_op jit(solution)/shard_map/ppermute | solution.py:476
  57.2 0.0 collective-permute-done.4.r1
  57.2 0.0 collective-permute-done.5.r2
  57.2 1.3 %sum_x.1 = (f32[14,32,128]{2,1,0:T(8,128)S(1)}, bf16[14,32,128]{2,1,0:T(8,128)(2,1)S(1)}, f32[14,32,128]{2,1,0:T(8,128)S(1)}, f32[14,32,128]{2,1,0:T(8,128)S(1)}) custom-call(f32[7,32,512]{2,1,0:T(8,128)} %get-tuple-element.49.low, f32[7,32,512]{2,1,0:T(8,128)} %get-tuple-element.50.high, bf16[14,32,512]{2,1,0:T(8,128)(2,1)S(1)} %collective-permute-done.4.r1, ...), custom_call_target="tpu_custom_call" | custom-call | flops 688128 | bytes 3211264 | tf_op jit(solution)/shard_map/sum_x/pallas_call | solution.py:251
  58.5 1.2 %collective-permute-start.7 = (f32[14,32,128]{2,1,0:T(8,128)S(1)}, f32[14,32,128]{2,1,0:T(8,128)S(1)}, u32[]{:S(2)}, u32[]{:S(2)}) collective-permute-start(f32[14,32,128]{2,1,0:T(8,128)S(1)} %get-tuple-element.68), channel_id=1, source_target_pairs={{0,1},{1,2},{2,3},{3,0},{4,5},{5,6},{6,7},{7,4},{8,9},{9,10},{10,1... | collective-permute-start | bytes 688136 | tf_op jit(solution)/shard_map/ppermute | solution.py:476
  59.7 2.1 %collective-permute-start.9 = (f32[14,32,128]{2,1,0:T(8,128)S(1)}, f32[14,32,128]{2,1,0:T(8,128)S(1)}, u32[]{:S(2)}, u32[]{:S(2)}) collective-permute-start(f32[14,32,128]{2,1,0:T(8,128)S(1)} %get-tuple-element.70), channel_id=1, source_target_pairs={{0,3},{1,0},{2,1},{3,2},{4,7},{5,4},{6,5},{7,6},{8,11},{9,8},{10,9... | collective-permute-start | bytes 688136 | tf_op jit(solution)/shard_map/ppermute | solution.py:476
  61.8 0.0 collective-permute-done.13.refs_6_
  61.8 1.2 %collective-permute-start.8 = (bf16[14,32,128]{2,1,0:T(8,128)(2,1)S(1)}, bf16[14,32,128]{2,1,0:T(8,128)(2,1)S(1)}, u32[]{:S(2)}, u32[]{:S(2)}) collective-permute-start(bf16[14,32,128]{2,1,0:T(8,128)(2,1)S(1)} %get-tuple-element.69), channel_id=1, source_target_pairs={{0,2},{1,3},{2,0},{3,1},{4,6},{5,7},{6,4},{7,5},{8,10},{9,11},{10,... | collective-permute-start | bytes 344072 | tf_op jit(solution)/shard_map/ppermute | solution.py:476
  63.0 6.4 %collective-permute-done.8.refs_2_ = bf16[14,32,128]{2,1,0:T(8,128)(2,1)S(1)} collective-permute-done((bf16[14,32,128]{2,1,0:T(8,128)(2,1)S(1)}, bf16[14,32,128]{2,1,0:T(8,128)(2,1)S(1)}, u32[]{:S(2)}, u32[]{:S(2)}) %collective-permute-start.8) | collective-permute-done | bytes 114720 | tf_op jit(solution)/shard_map/ppermute | solution.py:476
  69.4 0.0 collective-permute-done.12.refs_5_
  69.4 0.0 collective-permute-done.14.refs_7_
  69.4 0.0 collective-permute-done.7.refs_1_
  69.4 0.0 collective-permute-done.9.refs_3_
  69.4 0.0 all-to-all-done.1.refs_9_
  69.5 0.0 copy-start.2
  69.5 0.0 copy-start.3
  69.5 1.4 %finish.1 = bf16[16,2,2,32,128]{4,3,2,1,0:T(8,128)(2,1)S(1)} custom-call(f32[14,32,128]{2,1,0:T(8,128)S(1)} %get-tuple-element.67.refs_0_, f32[14,32,128]{2,1,0:T(8,128)S(1)} %collective-permute-done.7.refs_1_, bf16[14,32,128]{2,1,0:T(8,128)(2,1)S(1)} %collective-permute-done.8.refs_2_, f32[14,32,128]{2,1,0:T(8,128)S(1)} %collective-permute-done.9.refs_3_, ...), custom_call_target="tpu_custom_call" | custom-call | flops 917504 | bytes 3440640 | tf_op jit(solution)/shard_map/finish/pallas_call | solution.py:394
  70.9 13.5 %all_to_all.15.arrived = bf16[16,2,2,32,128]{4,3,2,1,0:T(8,128)(2,1)S(1)} all-to-all(bf16[16,2,2,32,128]{4,3,2,1,0:T(8,128)(2,1)S(1)} %finish.1), channel_id=1, replica_groups=mesh['frow'=8,'fcol'=16] {'fcol'}, dimensions={0} | all-to-all | bytes 1048576 | tf_op jit(solution)/shard_map/all_to_all | solution.py:522
  84.4 0.0 copy-done.2
  84.4 0.0 copy-done.3
  84.4 1.2 %tail.1 = (bf16[224,512]{1,0:T(8,128)(2,1)}, f32[96,224]{1,0:T(8,128)}, f32[64,96]{1,0:T(8,128)}, bf16[32,512]{1,0:T(8,128)(2,1)}) custom-call(bf16[16,2,2,32,128]{4,3,2,1,0:T(8,128)(2,1)S(1)} %all_to_all.15.arrived, bf16[96,512]{1,0:T(8,128)(2,1)S(1)} %bitcast.11, bf16[64,256]{1,0:T(8,128)(2,1)S(1)} %bitcast.10, ...), custom_call_target="tpu_custom_call" | custom-call | flops 75497472 | bytes 786432 | tf_op jit(solution)/shard_map/tail/pallas_call | solution.py:460
Async XLA Ops:
  3.0 8.1 %copy-start = (bf16[16,272,128]{2,1,0:T(8,128)(2,1)S(1)}, bf16[16,272,128]{2,1,0:T(8,128)(2,1)}, u32[]{:S(2)}) copy-start(bf16[16,272,128]{2,1,0:T(8,128)(2,1)} %pack.1.token) | copy-start | bytes 3342340
  3.0 29.8 %all-to-all-start = ((bf16[16,272,128]{2,1,0:T(8,128)(2,1)}), bf16[16,272,128]{2,1,0:T(8,128)(2,1)S(1)}, u32[]{:S(2)}, u32[]{:S(2)}) async-start(bf16[16,272,128]{2,1,0:T(8,128)(2,1)} %pack.1.token), calls=%async_computation | async-start | bytes 2228224 | tf_op jit(solution)/shard_map/all_to_all | solution.py:494
  19.3 12.7 %collective-permute-start = (bf16[7,32,512]{2,1,0:T(8,128)(2,1)S(1)}, bf16[7,32,512]{2,1,0:T(8,128)(2,1)S(1)}, u32[]{:S(2)}, u32[]{:S(2)}) collective-permute-start(bf16[7,32,512]{2,1,0:T(8,128)(2,1)S(1)} %get-tuple-element.55), channel_id=1, source_target_pairs={{0,4},{1,5},{2,6},{3,7},{4,8},{5,9},{6,10},{7,11},{8,12},{9,13},{1... | collective-permute-start | bytes 688136 | tf_op jit(solution)/shard_map/ppermute | solution.py:476
  21.3 10.8 %collective-permute-start.1 = (bf16[7,32,512]{2,1,0:T(8,128)(2,1)S(1)}, bf16[7,32,512]{2,1,0:T(8,128)(2,1)S(1)}, u32[]{:S(2)}, u32[]{:S(2)}) collective-permute-start(bf16[7,32,512]{2,1,0:T(8,128)(2,1)S(1)} %get-tuple-element.56), channel_id=1, source_target_pairs={{0,12},{1,13},{2,14},{3,15},{4,0},{5,1},{6,2},{7,3},{8,4},{9,5},{1... | collective-permute-start | bytes 688136 | tf_op jit(solution)/shard_map/ppermute | solution.py:476
  22.6 10.2 %collective-permute-start.2 = (bf16[28,32,128]{2,1,0:T(8,128)(2,1)S(1)}, bf16[28,32,128]{2,1,0:T(8,128)(2,1)S(1)}, u32[]{:S(2)}, u32[]{:S(2)}) collective-permute-start(bf16[28,32,128]{2,1,0:T(8,128)(2,1)S(1)} %get-tuple-element.61), channel_id=1, source_target_pairs={{0,1},{1,2},{2,3},{3,0},{4,5},{5,6},{6,7},{7,4},{8,9},{9,10},{10,1... | collective-permute-start | bytes 688136 | tf_op jit(solution)/shard_map/ppermute | solution.py:476
  24.5 8.3 %collective-permute-start.3 = (bf16[28,32,128]{2,1,0:T(8,128)(2,1)S(1)}, bf16[28,32,128]{2,1,0:T(8,128)(2,1)S(1)}, u32[]{:S(2)}, u32[]{:S(2)}) collective-permute-start(bf16[28,32,128]{2,1,0:T(8,128)(2,1)S(1)} %get-tuple-element.62), channel_id=1, source_target_pairs={{0,3},{1,0},{2,1},{3,2},{4,7},{5,4},{6,5},{7,6},{8,11},{9,8},{10,9... | collective-permute-start | bytes 688136 | tf_op jit(solution)/shard_map/ppermute | solution.py:476
  25.9 7.0 %copy-start.1 = (bf16[256,64]{0,1:T(8,128)(2,1)S(1)}, bf16[256,64]{0,1:T(8,128)(2,1)}, u32[]{:S(2)}) copy-start(bf16[256,64]{0,1:T(8,128)(2,1)} %param.15) | copy-start | bytes 98308
  35.9 6.6 %collective-permute-start.6 = (bf16[16,272,128]{2,1,0:T(8,128)(2,1)S(1)}, bf16[16,272,128]{2,1,0:T(8,128)(2,1)S(1)}, u32[]{:S(2)}, u32[]{:S(2)}) collective-permute-start(bf16[16,272,128]{2,1,0:T(8,128)(2,1)S(1)} %get-tuple-element.65.mine), channel_id=1, source_target_pairs={{0,16},{16,0},{32,48},{48,32},{64,80},{80,64},{96,112},{112,96},{1... | collective-permute-start | bytes 3342344 | tf_op jit(solution)/shard_map/ppermute | solution.py:476
  36.0 15.1 %collective-permute-start.10 = (bf16[60,32,128]{2,1,0:T(8,128)(2,1)}, bf16[60,32,128]{2,1,0:T(8,128)(2,1)S(1)}, u32[]{:S(2)}, u32[]{:S(2)}) collective-permute-start(bf16[60,32,128]{2,1,0:T(8,128)(2,1)} %get-tuple-element.73), channel_id=1, source_target_pairs={{0,1},{1,2},{2,3},{3,0},{4,5},{5,6},{6,7},{7,4},{8,9},{9,10},{10,1... | collective-permute-start | bytes 1474568 | tf_op jit(solution)/shard_map/ppermute | solution.py:476
  36.7 14.4 %collective-permute-start.11 = (bf16[60,32,128]{2,1,0:T(8,128)(2,1)}, bf16[60,32,128]{2,1,0:T(8,128)(2,1)S(1)}, u32[]{:S(2)}, u32[]{:S(2)}) collective-permute-start(bf16[60,32,128]{2,1,0:T(8,128)(2,1)} %get-tuple-element.74), channel_id=1, source_target_pairs={{0,3},{1,0},{2,1},{3,2},{4,7},{5,4},{6,5},{7,6},{8,11},{9,8},{10,9... | collective-permute-start | bytes 1474568 | tf_op jit(solution)/shard_map/ppermute | solution.py:476
  39.3 18.0 %collective-permute-start.4 = (bf16[14,32,512]{2,1,0:T(8,128)(2,1)}, bf16[14,32,512]{2,1,0:T(8,128)(2,1)S(1)}, u32[]{:S(2)}, u32[]{:S(2)}) collective-permute-start(bf16[14,32,512]{2,1,0:T(8,128)(2,1)} %get-tuple-element.63), channel_id=1, source_target_pairs={{0,4},{1,5},{2,6},{3,7},{4,8},{5,9},{6,10},{7,11},{8,12},{9,13},{1... | collective-permute-start | bytes 1376264 | tf_op jit(solution)/shard_map/ppermute | solution.py:476
  39.5 17.7 %collective-permute-start.5 = (bf16[14,32,512]{2,1,0:T(8,128)(2,1)}, bf16[14,32,512]{2,1,0:T(8,128)(2,1)S(1)}, u32[]{:S(2)}, u32[]{:S(2)}) collective-permute-start(bf16[14,32,512]{2,1,0:T(8,128)(2,1)} %get-tuple-element.64), channel_id=1, source_target_pairs={{0,12},{1,13},{2,14},{3,15},{4,0},{5,1},{6,2},{7,3},{8,4},{9,5},{1... | collective-permute-start | bytes 1376264 | tf_op jit(solution)/shard_map/ppermute | solution.py:476
  46.6 22.9 %all-to-all-start.1 = ((bf16[4,28,32,128]{3,2,1,0:T(8,128)(2,1)}), bf16[4,28,32,128]{3,2,1,0:T(8,128)(2,1)S(1)}, u32[]{:S(2)}, u32[]{:S(2)}) async-start(bf16[4,28,32,128]{3,2,1,0:T(8,128)(2,1)} %get-tuple-element.80), calls=%async_computation.1 | async-start | bytes 1835008 | tf_op jit(solution)/shard_map/all_to_all | solution.py:509
  52.4 9.4 %collective-permute-start.13 = (bf16[14,32,128]{2,1,0:T(8,128)(2,1)S(1)}, bf16[14,32,128]{2,1,0:T(8,128)(2,1)S(1)}, u32[]{:S(2)}, u32[]{:S(2)}) collective-permute-start(bf16[14,32,128]{2,1,0:T(8,128)(2,1)S(1)} %get-tuple-element.77), channel_id=1, source_target_pairs={{0,8},{1,9},{2,10},{3,11},{4,12},{5,13},{6,14},{7,15},{8,0},{9,1},... | collective-permute-start | bytes 344072 | tf_op jit(solution)/shard_map/ppermute | solution.py:476
  54.0 15.4 %collective-permute-start.12 = (f32[14,32,128]{2,1,0:T(8,128)S(1)}, f32[14,32,128]{2,1,0:T(8,128)S(1)}, u32[]{:S(2)}, u32[]{:S(2)}) collective-permute-start(f32[14,32,128]{2,1,0:T(8,128)S(1)} %get-tuple-element.76), channel_id=1, source_target_pairs={{0,4},{1,5},{2,6},{3,7},{4,8},{5,9},{6,10},{7,11},{8,12},{9,13},{1... | collective-permute-start | bytes 688136 | tf_op jit(solution)/shard_map/ppermute | solution.py:476
  54.6 14.9 %collective-permute-start.14 = (f32[14,32,128]{2,1,0:T(8,128)S(1)}, f32[14,32,128]{2,1,0:T(8,128)S(1)}, u32[]{:S(2)}, u32[]{:S(2)}) collective-permute-start(f32[14,32,128]{2,1,0:T(8,128)S(1)} %get-tuple-element.78), channel_id=1, source_target_pairs={{0,12},{1,13},{2,14},{3,15},{4,0},{5,1},{6,2},{7,3},{8,4},{9,5},{1... | collective-permute-start | bytes 688136 | tf_op jit(solution)/shard_map/ppermute | solution.py:476
  58.5 10.9 %collective-permute-start.7 = (f32[14,32,128]{2,1,0:T(8,128)S(1)}, f32[14,32,128]{2,1,0:T(8,128)S(1)}, u32[]{:S(2)}, u32[]{:S(2)}) collective-permute-start(f32[14,32,128]{2,1,0:T(8,128)S(1)} %get-tuple-element.68), channel_id=1, source_target_pairs={{0,1},{1,2},{2,3},{3,0},{4,5},{5,6},{6,7},{7,4},{8,9},{9,10},{10,1... | collective-permute-start | bytes 688136 | tf_op jit(solution)/shard_map/ppermute | solution.py:476
  59.7 9.8 %collective-permute-start.9 = (f32[14,32,128]{2,1,0:T(8,128)S(1)}, f32[14,32,128]{2,1,0:T(8,128)S(1)}, u32[]{:S(2)}, u32[]{:S(2)}) collective-permute-start(f32[14,32,128]{2,1,0:T(8,128)S(1)} %get-tuple-element.70), channel_id=1, source_target_pairs={{0,3},{1,0},{2,1},{3,2},{4,7},{5,4},{6,5},{7,6},{8,11},{9,8},{10,9... | collective-permute-start | bytes 688136 | tf_op jit(solution)/shard_map/ppermute | solution.py:476
  61.8 7.6 %collective-permute-start.8 = (bf16[14,32,128]{2,1,0:T(8,128)(2,1)S(1)}, bf16[14,32,128]{2,1,0:T(8,128)(2,1)S(1)}, u32[]{:S(2)}, u32[]{:S(2)}) collective-permute-start(bf16[14,32,128]{2,1,0:T(8,128)(2,1)S(1)} %get-tuple-element.69), channel_id=1, source_target_pairs={{0,2},{1,3},{2,0},{3,1},{4,6},{5,7},{6,4},{7,5},{8,10},{9,11},{10,... | collective-permute-start | bytes 344072 | tf_op jit(solution)/shard_map/ppermute | solution.py:476
  69.5 14.9 %copy-start.2 = (bf16[512,96]{0,1:T(8,128)(2,1)S(1)}, bf16[512,96]{0,1:T(8,128)(2,1)}, u32[]{:S(2)}) copy-start(bf16[512,96]{0,1:T(8,128)(2,1)} %param.14) | copy-start | bytes 294916
  69.5 14.9 %copy-start.3 = (s32[1,32]{1,0:T(1,128)S(1)}, s32[1,32]{1,0:T(1,128)}, u32[]{:S(2)}) copy-start(s32[1,32]{1,0:T(1,128)} %piv_parent.1) | copy-start | bytes 388
